TPU v7x, 512 devices: a whole 4x8x8 slice. The times are simulated.
512 devices in a mesh: dom: 128 (over y, z, core), sub: 4 (over x).
Axes of the slice: x: 4, y: 8, z: 8, core: 2. Of those that a mesh axis runs over, the one named last changes fastest.
Arguments:
- firm_act: bfloat16 [131072, 512], P('dom', 'sub'), may hold values from -6 to 6
- w_self: bfloat16 [512, 512], replicated, may hold values from -0.25 to 0.25
- w_nbr: bfloat16 [512, 512], replicated, may hold values from -0.25 to 0.25
- halo_rows: int32 [128, 128, 8], P('dom'), may hold values from 0 to 1023
- nbr_index: int32 [131072, 16], P('dom'), may hold values from 0 to 2047
- nbr_count: int32 [131072], P('dom'), may hold values from 1 to 16
- w_pair: bfloat16 [1536, 1024], replicated, may hold values from -0.15625 to 0.15625
- w_out: float32 [1024], replicated, may hold values from -0.9 to 0.9
- push_rows: int32 [128, 128, 4, 2], P('dom'), may hold values from 0 to 1023
- pair_slots: int32 [65536, 2], P(('dom', 'sub')), may hold values from 0 to 255, as said below
- labels: int32 [65536], P(('dom', 'sub')), may hold values 0 or 1
Outputs:
- pair_loss: float32 [65536], P(('dom', 'sub'))
- embed_grad: float32 [131072, 512], P('dom', 'sub')
Inputs may be any that keep to these rules, and one draw needn't show every extreme that they name: `halo_rows`: rows of the sending partition's own firms. `nbr_index`: slots of the firm's partition table: its own 1024 rows, then its 1024 halo rows; slots from nbr_count on are unused. `push_rows`: rows of the sending partition's own firms; a firm may be sent several times. `pair_slots`: each pair device's 128 pairs name each of its 256 received slots exactly once.
All inputs are finite; a program needn't handle non-finite values. No bound on the sum of `labels` on one device may be relied on, other than what follows from the above.
Results may differ from a plain program's by a relative error of at most 0.0058.
Values may be sent and summed in bfloat16 or wider, within the bound.
No kernel may reach another device: no remote copies, remote signals or barrier semaphores. Data moves between devices by JAX's collectives and lax.ppermute only.
A program may use at most 64 MiB of HBM per device.

v0:
```python
import jax
import jax.numpy as jnp
from jax import lax
from jax.sharding import PartitionSpec as P


def per_device(
    firm_act,
    w_self,
    w_nbr,
    halo_rows,
    nbr_index,
    nbr_count,
    w_pair,
    w_out,
    push_rows,
    pair_slots,
    labels,
):
    row_count, narrow = firm_act.shape
    full_width = w_self.shape[1]
    dom_count = lax.axis_size("dom")
    sub_count = lax.axis_size("sub")
    slot_count = halo_rows.shape[2]
    outgoing = firm_act[halo_rows[0].reshape(-1)].reshape(dom_count, slot_count, narrow)
    incoming = lax.all_to_all(outgoing, "dom", split_axis=0, concat_axis=0, tiled=True)
    row_table = jnp.concatenate([firm_act, incoming.reshape(dom_count * slot_count, narrow)], 0)
    picked = row_table[nbr_index]
    degree = nbr_index.shape[1]
    live_mask = (jnp.arange(degree, dtype=jnp.int32)[None, :] < nbr_count[:, None]).astype(
        jnp.bfloat16
    )
    summed = jnp.einsum("fk,fkc->fc", live_mask, picked, preferred_element_type=jnp.float32)
    neighbour = (summed / nbr_count[:, None].astype(jnp.float32)).astype(jnp.bfloat16)
    column = lax.axis_index("sub") * narrow
    self_cols = lax.dynamic_slice_in_dim(w_self, column, narrow, 1)
    near_cols = lax.dynamic_slice_in_dim(w_nbr, column, narrow, 1)
    own_piece = lax.all_gather(firm_act, "sub", axis=1, tiled=True)
    near_piece = lax.all_gather(neighbour, "sub", axis=1, tiled=True)
    total = jnp.dot(own_piece, self_cols, preferred_element_type=jnp.float32)
    embed = (total + jnp.dot(near_piece, near_cols, preferred_element_type=jnp.float32)).astype(
        jnp.bfloat16
    )
    capacity = push_rows.shape[3]
    outgoing_rows = embed[push_rows[0].reshape(-1)].reshape(dom_count, sub_count, capacity, narrow)
    arrived = lax.all_to_all(
        lax.all_to_all(outgoing_rows, "dom", split_axis=0, concat_axis=0, tiled=True),
        "sub",
        split_axis=1,
        concat_axis=3,
        tiled=True,
    )
    slot_rows = arrived.reshape(dom_count * capacity, full_width)
    end_rows = slot_rows[pair_slots.reshape(-1)].reshape(-1, 2, full_width)
    left_end = end_rows[:, 0]
    right_end = end_rows[:, 1]
    product = (left_end.astype(jnp.float32) * right_end.astype(jnp.float32)).astype(jnp.bfloat16)
    features = jnp.concatenate([left_end, right_end, product], 1)
    pre_act = jnp.dot(features, w_pair, preferred_element_type=jnp.float32)
    gate_value = jax.nn.sigmoid(pre_act)
    logit = jnp.sum(pre_act * gate_value * w_out[None, :], axis=1)
    target = labels.astype(jnp.float32)
    pair_loss = jax.nn.softplus(logit) - target * logit
    outer_grad = jax.nn.sigmoid(logit) - target
    pre_grad = (
        outer_grad[:, None] * w_out[None, :] * gate_value * (1.0 + pre_act * (1.0 - gate_value))
    ).astype(jnp.bfloat16)
    feat_grad = lax.dot_general(
        pre_grad, w_pair, (((1,), (1,)), ((), ())), preferred_element_type=jnp.float32
    )
    left_grad = feat_grad[:, :full_width] + feat_grad[:, 2 * full_width :] * right_end.astype(
        jnp.float32
    )
    right_grad = feat_grad[:, full_width : 2 * full_width] + feat_grad[
        :, 2 * full_width :
    ] * left_end.astype(jnp.float32)
    end_grads = jnp.stack([left_grad, right_grad], 1).reshape(-1, full_width).astype(jnp.bfloat16)
    ordered = jnp.zeros_like(slot_rows).at[pair_slots.reshape(-1)].set(end_grads)
    returned = lax.all_to_all(
        lax.all_to_all(
            ordered.reshape(dom_count, 1, capacity, full_width),
            "dom",
            split_axis=0,
            concat_axis=1,
            tiled=True,
        ),
        "sub",
        split_axis=3,
        concat_axis=0,
        tiled=True,
    )
    targets = jnp.transpose(push_rows[0], (1, 0, 2)).reshape(-1)
    embed_grad = (
        jnp.zeros((row_count, narrow), jnp.float32)
        .at[targets]
        .add(returned.reshape(-1, narrow).astype(jnp.float32))
    )
    return (pair_loss, embed_grad)


def solution(mesh):
    in_specs = (
        P("dom", "sub"),
        P(),
        P(),
        P("dom", None, None),
        P("dom", None),
        P("dom"),
        P(),
        P(),
        P("dom", None, None, None),
        P(("dom", "sub"), None),
        P(("dom", "sub")),
    )
    out_specs = (P(("dom", "sub")), P("dom", "sub"))
    return jax.shard_map(
        per_device, mesh=mesh, in_specs=in_specs, out_specs=out_specs, check_vma=False
    )
```

profile of v0, /device:TPU:1, one launch (start us, length us, event | category | flops | bytes accessed | tf_op | source)
XLA Modules:
  0.0 240.8 jit_solution(3594365358888685827)
XLA Ops:
  7.2 0.7 all-gather.3.cloned.1.call-update
  7.9 0.9 copy.56
  9.0 5.1 %gather_fusion = bf16[1024,128]{1,0:T(8,128)(2,1)} fusion(bf16[1024,128]{1,0:T(8,128)(2,1)} %param.11, s32[1024]{0:T(1024)S(1)} %broadcast_clamp_fusion.2), kind=kCustom, calls=%fused_computation | custom fusion | bytes 528384 | tf_op jit(solution)/shard_map/gather | solution.py:25
  14.0 18.9 %all-to-all-start = ((bf16[128,8,128]{2,1,0:T(8,128)(2,1)}), bf16[128,8,128]{2,1,0:T(8,128)(2,1)}, u32[]{:S(2)}, u32[]{:S(2)}) async-start(bf16[128,8,128]{2,1,0:T(8,128)(2,1)} %bitcast.50), calls=%async_computation | async-start | bytes 524288 | tf_op jit(solution)/shard_map/all_to_all | solution.py:26
  32.9 1.5 fusion.3
  34.5 0.8 compare_select_fusion
  35.3 0.7 convert_element_type.44
  36.0 1.0 copy.57
  37.0 1.2 reshape.178
  38.3 8.6 %all-to-all-done = bf16[128,8,128]{2,1,0:T(8,128)(2,1)} async-done(((bf16[128,8,128]{2,1,0:T(8,128)(2,1)}), bf16[128,8,128]{2,1,0:T(8,128)(2,1)}, u32[]{:S(2)}, u32[]{:S(2)}) %all-to-all-start) | async-done | bytes 262176 | tf_op jit(solution)/shard_map/all_to_all | solution.py:26
  46.9 1.8 pad_maximum_fusion
  48.7 56.5 %gather_fusion.1 = bf16[16384,128]{1,0:T(8,128)(2,1)} fusion(bf16[2048,128]{1,0:T(8,128)(2,1)} %pad_maximum_fusion, s32[16384]{0:T(1024)S(1)} %broadcast_clamp_fusion), kind=kCustom, calls=%fused_computation.1 | custom fusion | bytes 8454144 | tf_op jit(solution)/shard_map/gather | solution.py:28
  105.2 3.4 %fusion = f32[1024,1,128]{2,1,0:T(1,128)S(1)} fusion(bf16[1024,16,128]{2,1,0:T(8,128)(2,1)} %bitcast.49, pred[1024,16,1]{1,0,2:T(32,128)(4,1)S(1)} %copy-done.2), kind=kOutput, calls=%fused_computation.6 | convolution fusion | flops 4194304 | bytes 4734976 | tf_op jit(solution)/shard_map/fk,fkc->fc/dot_general | solution.py:33
  108.7 0.9 divide_convert_fusion
  109.6 0.2 copy.59
  109.8 0.3 reshape_squeeze.7
  110.1 2.6 %convolution_bitcast_fusion = f32[1024,128]{0,1:T(8,128)} fusion(bf16[1024,512]{1,0:T(8,128)(2,1)} %all-gather.3.cloned.1.call-done, bf16[512,512]{1,0:T(8,128)(2,1)} %param.12, s32[]{:T(128)S(6)} %select_n.52), kind=kOutput, calls=%fused_computation.9 | convolution fusion | flops 134217728 | bytes 1703940 | tf_op jit(solution)/shard_map/dot_general | solution.py:40
  112.7 20.4 %all-gather.5.cloned.1.call-done = bf16[1024,512]{1,0:T(8,128)(2,1)} async-done(((bf16[1024,128]{1,0:T(8,128)(2,1)}), bf16[1024,512]{1,0:T(8,128)(2,1)}) %all-gather.5.cloned.1.call-update) | async-done | bytes 1048592 | tf_op jit(solution)/shard_map/all_gather | solution.py:39
  133.1 2.6 %fusion.2 = bf16[1024,128]{0,1:T(8,128)(2,1)} fusion(f32[1024,128]{0,1:T(8,128)} %convolution_bitcast_fusion, bf16[1024,512]{1,0:T(8,128)(2,1)} %all-gather.5.cloned.1.call-done, bf16[512,512]{1,0:T(8,128)(2,1)} %param.13, s32[]{:T(128)S(6)} %select_n.52), kind=kOutput, calls=%fused_computation.10 | convolution fusion | flops 134479872 | bytes 1966084 | tf_op jit(solution)/shard_map/dot_general | solution.py:41
  135.8 1.1 copy.60
  136.9 4.3 %gather_fusion.2 = bf16[1024,128]{1,0:T(8,128)(2,1)} fusion(bf16[1024,128]{1,0:T(8,128)(2,1)S(1)} %copy.60, s32[1024]{0:T(1024)S(1)} %broadcast_clamp_fusion.1), kind=kCustom, calls=%fused_computation.2 | custom fusion | bytes 528384 | tf_op jit(solution)/shard_map/gather | solution.py:45
  141.2 15.3 %all-to-all-start.1 = ((bf16[128,4,2,128]{3,2,1,0:T(2,128)(2,1)}), bf16[128,4,2,128]{3,2,1,0:T(2,128)(2,1)S(1)}, u32[]{:S(2)}, u32[]{:S(2)}) async-start(bf16[128,4,2,128]{3,2,1,0:T(2,128)(2,1)} %bitcast.51), calls=%async_computation.1 | async-start | bytes 524288 | tf_op jit(solution)/shard_map/all_to_all | solution.py:47
  156.6 0.1 reshape.162
  156.8 14.0 %all-to-all-done.1 = bf16[128,4,2,128]{3,2,1,0:T(2,128)(2,1)S(1)} async-done(((bf16[128,4,2,128]{3,2,1,0:T(2,128)(2,1)}), bf16[128,4,2,128]{3,2,1,0:T(2,128)(2,1)S(1)}, u32[]{:S(2)}, u32[]{:S(2)}) %all-to-all-start.1) | async-done | bytes 262176 | tf_op jit(solution)/shard_map/all_to_all | solution.py:47
  170.7 0.9 copy.61
  171.6 3.7 %all-to-all-start.2 = ((bf16[128,4,2,128]{3,2,0,1:T(2,128)(2,1)}), bf16[128,4,2,128]{3,2,0,1:T(2,128)(2,1)S(1)}, u32[]{:S(2)}, u32[]{:S(2)}) async-start(bf16[128,4,2,128]{3,2,0,1:T(2,128)(2,1)} %copy.61), calls=%async_computation.2 | async-start | bytes 524288 | tf_op jit(solution)/shard_map/all_to_all | solution.py:46
  175.3 5.5 %all-to-all-done.2 = bf16[128,4,2,128]{3,2,0,1:T(2,128)(2,1)S(1)} async-done(((bf16[128,4,2,128]{3,2,0,1:T(2,128)(2,1)}), bf16[128,4,2,128]{3,2,0,1:T(2,128)(2,1)S(1)}, u32[]{:S(2)}, u32[]{:S(2)}) %all-to-all-start.2) | async-done | bytes 262176 | tf_op jit(solution)/shard_map/all_to_all | solution.py:46
  180.9 0.3 copy.62
  181.2 1.9 gather_fusion.3
  183.1 1.1 reshape.163
  184.2 0.4 fusion.32
  184.6 0.8 multiply_reduce_fusion
  185.4 0.5 divide_subtract_fusion
  185.9 1.2 fusion.10
  187.3 0.3 copy.67
  187.6 0.8 reshape.204
  188.4 2.0 scatter_custom_fusion
  190.3 0.8 reshape.165
  191.1 8.4 %all-to-all-start.3 = ((bf16[128,1,2,512]{3,2,1,0:T(2,128)(2,1)}), bf16[128,1,2,512]{3,2,1,0:T(2,128)(2,1)S(1)}, u32[]{:S(2)}, u32[]{:S(2)}) async-start(bf16[128,1,2,512]{3,2,1,0:T(2,128)(2,1)} %bitcast.55), calls=%async_computation.3 | async-start | bytes 524288 | tf_op jit(solution)/shard_map/all_to_all | solution.py:80
  199.5 0.9 copy.66
  200.4 1.1 reshape.164
  201.5 12.4 %all-to-all-done.3 = bf16[128,1,2,512]{3,2,1,0:T(2,128)(2,1)S(1)} async-done(((bf16[128,1,2,512]{3,2,1,0:T(2,128)(2,1)}), bf16[128,1,2,512]{3,2,1,0:T(2,128)(2,1)S(1)}, u32[]{:S(2)}, u32[]{:S(2)}) %all-to-all-start.3) | async-done | bytes 262176 | tf_op jit(solution)/shard_map/all_to_all | solution.py:80
  213.9 1.0 copy.69
  214.9 3.4 %all-to-all-start.4 = ((bf16[1,128,2,512]{1,2,0,3:T(2,128)(2,1)}), bf16[1,128,2,512]{1,2,0,3:T(2,128)(2,1)S(1)}, u32[]{:S(2)}, u32[]{:S(2)}) async-start(bf16[1,128,2,512]{1,2,0,3:T(2,128)(2,1)} %copy.69), calls=%async_computation.4 | async-start | bytes 524288 | tf_op jit(solution)/shard_map/all_to_all | solution.py:79
  218.4 5.5 %all-to-all-done.4 = bf16[1,128,2,512]{1,2,0,3:T(2,128)(2,1)S(1)} async-done(((bf16[1,128,2,512]{1,2,0,3:T(2,128)(2,1)}), bf16[1,128,2,512]{1,2,0,3:T(2,128)(2,1)S(1)}, u32[]{:S(2)}, u32[]{:S(2)}) %all-to-all-start.4) | async-done | bytes 262176 | tf_op jit(solution)/shard_map/all_to_all | solution.py:79
  223.9 0.8 convert_bitcast_fusion
  224.7 2.0 copy.71
  226.7 7.2 %scatter_custom_fusion.1 = f32[1024,128]{1,0:T(8,128)} fusion(s32[1024]{0:T(1024)S(1)} %bitcast.64, f32[1024,128]{1,0:T(8,128)} %bitcast.58, f32[]{:T(128)} %constant.3.clone.1), kind=kCustom, calls=%fused_computation.37 | custom fusion | flops 131072 | bytes 524800 | tf_op jit(solution)/shard_map/scatter-add | solution.py:96
  (33 shorter events, 0.7 us)
Async XLA Ops:
  7.2 177.4 %copy-start = (bf16[1536,1024]{1,0:T(8,128)(2,1)S(1)}, bf16[1536,1024]{1,0:T(8,128)(2,1)}, u32[]{:S(2)}) copy-start(bf16[1536,1024]{1,0:T(8,128)(2,1)} %param.17) | copy-start | bytes 9437188
  7.2 39.8 %copy-start.1 = (bf16[1024,128]{1,0:T(8,128)(2,1)S(1)}, bf16[1024,128]{1,0:T(8,128)(2,1)}, u32[]{:S(2)}) copy-start(bf16[1024,128]{1,0:T(8,128)(2,1)} %param.11) | copy-start | bytes 786436
  7.2 102.9 %all-gather.3.cloned.1.call-start = ((), (), s32[]{:S(2)}) async-start(), calls=%async_computation.5 | async-start | bytes 1310720 | tf_op jit(solution)/shard_map/all_gather | solution.py:38
  14.0 32.9 %all-to-all-start = ((bf16[128,8,128]{2,1,0:T(8,128)(2,1)}), bf16[128,8,128]{2,1,0:T(8,128)(2,1)}, u32[]{:S(2)}, u32[]{:S(2)}) async-start(bf16[128,8,128]{2,1,0:T(8,128)(2,1)} %bitcast.50), calls=%async_computation | async-start | bytes 524288 | tf_op jit(solution)/shard_map/all_to_all | solution.py:26
  32.9 100.2 %all-gather.5.cloned.1.call-start = ((), (), s32[]{:S(2)}) async-start(), calls=%async_computation.6 | async-start | bytes 1310720 | tf_op jit(solution)/shard_map/all_gather | solution.py:39
  48.7 56.5 %copy-start.2 = (pred[1024,16,1]{1,0,2:T(32,128)(4,1)S(1)}, pred[1024,16,1]{1,0,2:T(32,128)(4,1)}, u32[]{:S(2)}) copy-start(pred[1024,16,1]{1,0,2:T(32,128)(4,1)} %fusion.3) | copy-start | bytes 49156
  105.2 4.4 %copy-start.3 = (s32[1,128,4,2]{1,3,2,0:T(2,128)S(1)}, s32[1,128,4,2]{1,3,2,0:T(2,128)}, u32[]{:S(2)}) copy-start(s32[1,128,4,2]{1,3,2,0:T(2,128)} %param.19) | copy-start | bytes 12292
  108.7 47.9 %copy-start.4 = (s32[128,2]{0,1:T(2,128)S(1)}, s32[128,2]{0,1:T(2,128)}, u32[]{:S(2)}) copy-start(s32[128,2]{0,1:T(2,128)} %param.20) | copy-start | bytes 3076
  141.2 43.4 %copy-start.6 = (f32[1024]{0:T(1024)S(1)}, f32[1024]{0:T(1024)}, u32[]{:S(2)}) copy-start(f32[1024]{0:T(1024)} %param.18) | copy-start | bytes 12292
  141.2 29.5 %all-to-all-start.1 = ((bf16[128,4,2,128]{3,2,1,0:T(2,128)(2,1)}), bf16[128,4,2,128]{3,2,1,0:T(2,128)(2,1)S(1)}, u32[]{:S(2)}, u32[]{:S(2)}) async-start(bf16[128,4,2,128]{3,2,1,0:T(2,128)(2,1)} %bitcast.51), calls=%async_computation.1 | async-start | bytes 524288 | tf_op jit(solution)/shard_map/all_to_all | solution.py:47
  171.6 9.2 %all-to-all-start.2 = ((bf16[128,4,2,128]{3,2,0,1:T(2,128)(2,1)}), bf16[128,4,2,128]{3,2,0,1:T(2,128)(2,1)S(1)}, u32[]{:S(2)}, u32[]{:S(2)}) async-start(bf16[128,4,2,128]{3,2,0,1:T(2,128)(2,1)} %copy.61), calls=%async_computation.2 | async-start | bytes 524288 | tf_op jit(solution)/shard_map/all_to_all | solution.py:46
  184.2 1.2 copy-start.5
  191.1 22.7 %all-to-all-start.3 = ((bf16[128,1,2,512]{3,2,1,0:T(2,128)(2,1)}), bf16[128,1,2,512]{3,2,1,0:T(2,128)(2,1)S(1)}, u32[]{:S(2)}, u32[]{:S(2)}) async-start(bf16[128,1,2,512]{3,2,1,0:T(2,128)(2,1)} %bitcast.55), calls=%async_computation.3 | async-start | bytes 524288 | tf_op jit(solution)/shard_map/all_to_all | solution.py:80
  214.9 8.9 %all-to-all-start.4 = ((bf16[1,128,2,512]{1,2,0,3:T(2,128)(2,1)}), bf16[1,128,2,512]{1,2,0,3:T(2,128)(2,1)S(1)}, u32[]{:S(2)}, u32[]{:S(2)}) async-start(bf16[1,128,2,512]{1,2,0,3:T(2,128)(2,1)} %copy.69), calls=%async_computation.4 | async-start | bytes 524288 | tf_op jit(solution)/shard_map/all_to_all | solution.py:79
Sparse Core Ops, SparseCore 0:
  10.1 35.7 all-gather.2
  109.7 23.3 all-gather.4
where the time goes:
time: 242 us; the launch traced here: 241 us
  local copies, waits for them, and re-layouts  84.4 us (35%)
  waiting for transfers between devices  67.1 us (28%)
  starting transfers between devices  49.7 us (21%)
  other arithmetic  14.6 us (6%)
  between operations  14.3 us (6%)
  matrix products  10.6 us (4%)
    gather x1, local copies, waits for them, and re-layouts, per_device(): picked = row_table[nbr_index]  56.5 us
    all_gather x1, waiting for transfers between devices, per_device(): near_piece = lax.all_gather(neighbour, 'sub', axis=1, tiled=True)  20.4 us
    all_to_all x1, starting transfers between devices, per_device(): lax.all_to_all(outgoing, 'dom', split_axis=0, concat_axis=0, tiled=True)  18.9 us
    all_to_all x1, starting transfers between devices, per_device(): lax.all_to_all(outgoing_rows, 'dom', split_axis=0, concat_axis=0, tiled=T...  15.3 us
    all_to_all x1, waiting for transfers between devices, per_device(): lax.all_to_all(outgoing_rows, 'dom', split_axis=0, concat_axis=0, tiled=T...  14 us
    all_to_all x1, waiting for transfers between devices, per_device(): lax.all_to_all(ordered.reshape(dom_count, 1, capacity, full_width), 'dom'...  12.4 us
    all_to_all x1, waiting for transfers between devices, per_device(): lax.all_to_all(outgoing, 'dom', split_axis=0, concat_axis=0, tiled=True)  8.65 us
    all_to_all x1, starting transfers between devices, per_device(): lax.all_to_all(ordered.reshape(dom_count, 1, capacity, full_width), 'dom'...  8.38 us
  transfers between devices with their start and end apart: 7, of which 6 were waited for; matrix products, arithmetic and copies ran while one was open for 33% of the time, Pallas kernels for 0%

commit v1 on v0

v1 whole, which is shorter than its diff:
```python
import jax
import jax.numpy as jnp
from jax import lax
from jax.experimental import pallas as pl
from jax.experimental.pallas import tpu as pltpu
from jax.sharding import PartitionSpec as P

BF = jnp.bfloat16
F32 = jnp.float32
DEAD = 4095
MIB = 1024 * 1024


def contract_first(a, b):
    return lax.dot_general(a, b, (((0,), (0,)), ((), ())), preferred_element_type=F32)


def call(kernel, out_shape, scratch, flops, nbytes, *args):
    return pl.pallas_call(
        kernel,
        out_shape=out_shape,
        scratch_shapes=scratch,
        compiler_params=pltpu.CompilerParams(vmem_limit_bytes=24 * MIB),
        cost_estimate=pl.CostEstimate(flops=flops, bytes_accessed=nbytes, transcendentals=0),
    )(*args)


def halo_kernel(act_ref, rows_ref, out_ref, tmp_ref):
    slots, parts = rows_ref.shape
    rows = rows_ref[...].T
    act = act_ref[...]
    row = lax.broadcasted_iota(jnp.int32, (parts, act.shape[0]), 1)
    for j in range(slots):
        pick = jnp.where(rows[:, j : j + 1] == row, 1.0, 0.0).astype(BF)
        tmp_ref[pl.ds(j, parts, stride=slots), :] = jnp.dot(
            pick, act, preferred_element_type=F32
        )
    out_ref[...] = tmp_ref[...].astype(BF)


def count_kernel(
    act_ref, push_ref, nbr_ref, cnt_ref, near_ref, own_ref, cntp_ref, actp_ref, pick_ref, mine_ref
):
    groups, parts = push_ref.shape
    firms = act_ref.shape[0]
    degree = nbr_ref.shape[0]
    firm = lax.broadcasted_iota(jnp.int32, (firms, parts), 0)
    for b in range(groups):
        pick_ref[:, b * parts : (b + 1) * parts] = jnp.where(
            firm == push_ref[b : b + 1, :], 1.0, 0.0
        ).astype(BF)
    count = cnt_ref[...]
    live = lax.broadcasted_iota(jnp.int32, (degree, firms), 0) < count
    slot = jnp.where(live, nbr_ref[...], DEAD)
    stack = jnp.concatenate(
        [slot >> 4, slot & 15, jnp.broadcast_to(count, (degree, firms))], 0
    ).astype(F32)
    chosen = jnp.dot(stack.astype(BF), pick_ref[...], preferred_element_type=F32)
    wanted = (chosen[:degree] * 16.0 + chosen[degree : 2 * degree]).astype(jnp.int32)
    cntp_ref[...] = chosen[2 * degree : 2 * degree + 8]
    actp_ref[...] = contract_first(act_ref[...], pick_ref[...])
    chunk = 128
    one = jnp.ones((chunk, parts), BF)
    zero = jnp.zeros((chunk, parts), BF)
    base = lax.broadcasted_iota(jnp.int32, (chunk, parts), 0).astype(jnp.int16)
    for b in range(groups):
        lanes = slice(b * parts, (b + 1) * parts)
        want = wanted[:, lanes].astype(jnp.int16)
        spread = [jnp.broadcast_to(want[k : k + 1, :], (chunk, parts)) for k in range(degree)]

        def fill(r, carry, out, first):
            number = base + (first + r * chunk).astype(jnp.int16)
            total = zero
            for k in range(degree):
                total = total + jnp.where(spread[k] == number, one, zero)
            out[pl.ds(pl.multiple_of(r * chunk, chunk), chunk), lanes] = total
            return carry

        lax.fori_loop(0, firms // chunk, lambda r, c: fill(r, c, mine_ref, 0), 0)
        lax.fori_loop(
            0, near_ref.shape[0] // chunk, lambda r, c: fill(r, c, near_ref, firms), 0
        )
    own_ref[...] = contract_first(act_ref[...], mine_ref[...])


def mean_kernel(halo_ref, near_ref, own_ref, cntp_ref, actp_ref, out_ref, tmp_ref):
    groups = 8
    parts = own_ref.shape[1] // groups
    summed = own_ref[...] + contract_first(halo_ref[...], near_ref[...])
    mean = (summed / cntp_ref[0:1, :]).astype(BF).astype(F32)
    for b in range(groups):
        lanes = slice(b * parts, (b + 1) * parts)
        at = (b // 2) * 4 + b % 2
        tmp_ref[pl.ds(at, parts, stride=2 * groups), :] = actp_ref[:, lanes].T
        tmp_ref[pl.ds(at + 2, parts, stride=2 * groups), :] = mean[:, lanes].T
    out_ref[...] = tmp_ref[...].astype(BF)


def decode_kernel(
    recv_ref, self_ref, near_ref, pair_ref, wout_ref, slots_ref, label_ref,
    loss_ref, out_ref, tmp_ref, back_ref,
):
    parts = recv_ref.shape[0] // 16
    pairs = slots_ref.shape[1]
    width = self_ref.shape[0]
    tmp_ref[...] = recv_ref[...].astype(F32)

    def rows_of(kind):
        halves = [
            jnp.concatenate(
                [
                    tmp_ref[pl.ds(s * 4 + kind * 2 + c, parts, stride=16), :]
                    for s in range(4)
                ],
                1,
            )
            for c in range(2)
        ]
        return jnp.concatenate(halves, 0).astype(BF)

    embed = (
        jnp.dot(rows_of(0), self_ref[...], preferred_element_type=F32)
        + jnp.dot(rows_of(1), near_ref[...], preferred_element_type=F32)
    ).astype(BF)
    place = lax.broadcasted_iota(jnp.int32, (2 * parts, pairs), 0)
    slot = jnp.where(place < parts, 2 * place, 2 * (place - parts) + 1)
    left_pick = jnp.where(slot == slots_ref[0:1, :], 1.0, 0.0).astype(BF)
    right_pick = jnp.where(slot == slots_ref[1:2, :], 1.0, 0.0).astype(BF)
    left = contract_first(left_pick, embed)
    right = contract_first(right_pick, embed)
    product = (left * right).astype(BF)
    pre_act = (
        jnp.dot(left.astype(BF), pair_ref[0:width, :], preferred_element_type=F32)
        + jnp.dot(right.astype(BF), pair_ref[width : 2 * width, :], preferred_element_type=F32)
        + jnp.dot(product, pair_ref[2 * width : 3 * width, :], preferred_element_type=F32)
    )
    gate = jax.nn.sigmoid(pre_act)
    wout = wout_ref[...]
    logit = jnp.sum(pre_act * gate * wout, axis=1, keepdims=True)
    target = jnp.broadcast_to(label_ref[...].astype(F32), (pairs, pairs)).T[:, 0:1]
    loss = jnp.maximum(logit, 0.0) + jnp.log1p(jnp.exp(-jnp.abs(logit))) - target * logit
    loss_ref[...] = jnp.broadcast_to(loss, (pairs, pairs)).T[0:1, :]
    outer = jax.nn.sigmoid(logit) - target
    pre_grad = (outer * wout * gate * (1.0 + pre_act * (1.0 - gate))).astype(BF)
    feat = lax.dot_general(
        pre_grad, pair_ref[...], (((1,), (1,)), ((), ())), preferred_element_type=F32
    )
    third = feat[:, 2 * width :]
    left_grad = (feat[:, :width] + third * right).astype(BF)
    right_grad = (feat[:, width : 2 * width] + third * left).astype(BF)
    back = jnp.dot(left_pick, left_grad, preferred_element_type=F32) + jnp.dot(
        right_pick, right_grad, preferred_element_type=F32
    )
    for s in range(4):
        for c in range(2):
            back_ref[pl.ds(s * 2 + c, parts, stride=8), :] = back[
                c * parts : (c + 1) * parts, s * 128 : (s + 1) * 128
            ]
    out_ref[...] = back_ref[...].astype(BF)


def owner_kernel(recv_ref, push_ref, out_ref, tmp_ref):
    groups, parts = push_ref.shape
    tmp_ref[...] = recv_ref[...].astype(F32)
    grads = jnp.concatenate(
        [tmp_ref[pl.ds(b, parts, stride=groups), :] for b in range(groups)], 0
    ).astype(BF)
    firm = lax.broadcasted_iota(jnp.int32, (out_ref.shape[0], parts), 0)
    pick = jnp.concatenate(
        [
            jnp.where(firm == push_ref[b : b + 1, :], 1.0, 0.0).astype(BF)
            for b in range(groups)
        ],
        1,
    )
    out_ref[...] = jnp.dot(pick, grads, preferred_element_type=F32)


def per_device(
    firm_act, w_self, w_nbr, halo_rows, nbr_index, nbr_count, w_pair, w_out, push_rows,
    pair_slots, labels,
):
    firms, narrow = firm_act.shape
    doms, subs, cap = push_rows.shape[1:]
    slots = halo_rows.shape[2]
    both = ("dom", "sub")
    shape = jax.ShapeDtypeStruct
    vmem = pltpu.VMEM
    halo_t = jnp.transpose(halo_rows[0])
    push_t = jnp.transpose(push_rows[0], (1, 2, 0)).reshape(subs * cap, doms)
    pushed = doms * subs * cap
    halos = doms * slots

    outgoing = call(
        halo_kernel, shape((halos, narrow), BF), [vmem((halos, narrow), F32)],
        2 * halos * firms * narrow, 600_000, firm_act, halo_t,
    )
    incoming = lax.all_to_all(
        outgoing.reshape(doms, slots, narrow), "dom", 0, 0, tiled=True
    ).reshape(halos, narrow)
    near_counts, own_sum, push_count, push_act = call(
        count_kernel,
        (
            shape((halos, pushed), BF), shape((narrow, pushed), F32),
            shape((8, pushed), F32), shape((narrow, pushed), F32),
        ),
        [vmem((firms, pushed), BF), vmem((firms, pushed), BF)],
        10_000_000_000, 4_000_000,
        firm_act, push_t, jnp.transpose(nbr_index), nbr_count.reshape(1, firms),
    )
    message = call(
        mean_kernel, shape((2 * pushed, narrow), BF), [vmem((2 * pushed, narrow), F32)],
        2 * halos * pushed * narrow, 4_000_000,
        incoming, near_counts, own_sum, push_count, push_act,
    )
    arrived = lax.all_to_all(
        message.reshape(doms * subs, 2 * cap, narrow), both, 0, 0, tiled=True
    ).reshape(2 * pushed, narrow)
    pairs = labels.shape[0]
    pair_loss, back = call(
        decode_kernel,
        (shape((1, pairs), F32), shape((pushed, narrow), BF)),
        [vmem((2 * pushed, narrow), F32), vmem((pushed, narrow), F32)],
        1_200_000_000, 5_000_000,
        arrived, w_self, w_nbr, w_pair, w_out.reshape(1, -1), jnp.transpose(pair_slots),
        labels.reshape(1, pairs),
    )
    returned = lax.all_to_all(
        back.reshape(doms * subs, cap, narrow), both, 0, 0, tiled=True
    ).reshape(pushed, narrow)
    embed_grad = call(
        owner_kernel, shape((firms, narrow), F32), [vmem((pushed, narrow), F32)],
        2 * pushed * firms * narrow, 1_000_000, returned, push_t,
    )
    return (pair_loss.reshape(pairs), embed_grad)


def solution(mesh):
    in_specs = (
        P("dom", "sub"), P(), P(), P("dom", None, None), P("dom", None), P("dom"), P(), P(),
        P("dom", None, None, None), P(("dom", "sub"), None), P(("dom", "sub")),
    )
    out_specs = (P(("dom", "sub")), P("dom", "sub"))
    return jax.shard_map(
        per_device, mesh=mesh, in_specs=in_specs, out_specs=out_specs, check_vma=False
    )
```

time: 242 us -> 113 us (0.47)
  local copies, waits for them, and re-layouts: 84.4 us -> 11.5 us
  waiting for transfers between devices: 67.1 us -> 0.01 us
  blocking collectives: 0 us -> 65.2 us
  starting transfers between devices: 49.7 us -> 18.4 us
  Pallas kernels: 0 us -> 17.1 us
  other arithmetic: 14.6 us -> 0 us
  between operations: 14.3 us -> 0.73 us
  matrix products: 10.6 us -> 0 us
    gather x4 -> x0, local copies, waits for them, and re-layouts: 67.7 us -> none  [the longest x1 56.5 us: per_device(): picked = row_table[nbr_index]]
    all_to_all x0 -> x2, blocking collectives: none -> 65.2 us  [the longest x1 39.2 us: per_device(): lax.all_to_all(message.reshape(doms * subs, 2 * cap, narrow), both, 0, 0,...]
    all_to_all x5 -> x1, waiting for transfers between devices: 46 us -> 0.01 us  [per_device(): lax.all_to_all(outgoing.reshape(doms, slots, narrow), 'dom', 0, 0, tiled=...]
    all_to_all x5 -> x1, starting transfers between devices: 49.7 us -> 18.4 us  [per_device(): lax.all_to_all(outgoing.reshape(doms, slots, narrow), 'dom', 0, 0, tiled=...]
    all_gather x2 -> x0, waiting for transfers between devices: 20.4 us -> none  [the longest x1 20.4 us: per_device(): near_piece = lax.all_gather(neighbour, 'sub', axis=1, tiled=True)]
    pallas_call x0 -> x5, Pallas kernels: none -> 17.1 us  [call(): pl.pallas_call(kernel, out_shape=out_shape, scratch_shapes=scratch, compi...]
    dot_general x5 -> x0, matrix products: 10.6 us -> none  [the longest x1 3.42 us: per_device(): jnp.einsum('fk,fkc->fc', live_mask, picked, preferred_element_type=jnp.fl...]
    unnamed x18 -> x38, local copies, waits for them, and re-layouts: 1.27 us -> 11.5 us
  transfers between devices with their start and end apart: 7 -> 1, of which waited for: 6 -> 0; matrix products, arithmetic and copies ran while one was open for 33% -> 0% of each run, Pallas kernels for 0% -> 9%
where the time goes in v1:
time: 113 us
  blocking collectives  65.2 us (58%)
  starting transfers between devices  18.4 us (16%)
  Pallas kernels  17.1 us (15%)
  local copies, waits for them, and re-layouts  11.5 us (10%)
    all_to_all x1, blocking collectives, per_device(): lax.all_to_all(message.reshape(doms * subs, 2 * cap, narrow), both, 0, 0,...  39.2 us
    all_to_all x1, blocking collectives, per_device(): lax.all_to_all(back.reshape(doms * subs, cap, narrow), both, 0, 0, tiled=...  26 us
    all_to_all x1, starting transfers between devices, per_device(): lax.all_to_all(outgoing.reshape(doms, slots, narrow), 'dom', 0, 0, tiled=...  18.4 us
    pallas_call x5, Pallas kernels, call(): pl.pallas_call(kernel, out_shape=out_shape, scratch_shapes=scratch, compi...  17.1 us
    unnamed x38, local copies, waits for them, and re-layouts  11.5 us
  transfers between devices with their start and end apart: 1, of which 0 were waited for; matrix products, arithmetic and copies ran while one was open for 0% of the time, Pallas kernels for 9%

profile of v1, /device:TPU:1, one launch (start us, length us, event | category | flops | bytes accessed | tf_op | source)
XLA Modules:
  0.0 113.0 jit_solution(15399218031079725643)
XLA Ops:
  0.6 0.0 copy-start.12
  0.6 0.9 copy-done.12
  1.6 0.0 copy-start.15
  1.6 0.7 copy-done.15
  2.3 1.7 %shard_map.122 = bf16[1024,128]{1,0:T(8,128)(2,1)} custom-call(bf16[1024,128]{1,0:T(8,128)(2,1)S(1)} %copy-done.12, s32[8,128]{1,0:T(8,128)S(1)} %bitcast.29), custom_call_target="tpu_custom_call" | custom-call | flops 268435456 | bytes 600000 | tf_op jit(solution)/shard_map/pallas_call | solution.py:19
  4.0 18.4 %all-to-all-start = ((bf16[128,8,128]{2,1,0:T(8,128)(2,1)}), bf16[128,8,128]{2,1,0:T(8,128)(2,1)S(1)}, u32[]{:S(2)}, u32[]{:S(2)}) async-start(bf16[128,8,128]{2,1,0:T(8,128)(2,1)} %bitcast.2), calls=%async_computation | async-start | bytes 524288 | tf_op jit(solution)/shard_map/all_to_all | solution.py:198
  22.4 0.0 copy-start.13
  22.4 0.9 copy-done.13
  23.4 0.0 copy-start.14
  23.4 0.8 copy-done.14
  24.2 0.0 copy-start.16
  24.2 0.7 copy-done.16
  24.9 0.0 copy-start.17
  24.9 0.7 copy-done.17
  25.6 0.0 copy-start.9
  25.6 0.0 copy-start.10
  25.6 0.0 copy-start.11
  25.6 10.0 %shard_map.123 = (bf16[1024,1024]{1,0:T(8,128)(2,1)S(1)}, f32[128,1024]{1,0:T(8,128)S(1)}, f32[8,1024]{1,0:T(8,128)S(1)}, f32[128,1024]{1,0:T(8,128)S(1)}) custom-call(bf16[1024,128]{1,0:T(8,128)(2,1)S(1)} %copy-done.13, s32[8,128]{1,0:T(8,128)S(1)} %bitcast.31, s32[16,1024]{1,0:T(8,128)S(1)} %bitcast.28, s32[1,1024]{1,0:T(1,128)S(1)} %bitcast.30), custom_call_target="tpu_custom_call" | custom-call | flops 10000000000 | bytes 4000000 | tf_op jit(solution)/shard_map/pallas_call | solution.py:19
  35.6 0.0 copy-start.1
  35.6 1.3 %copy-done.1 = bf16[1024,1024]{1,0:T(8,128)(2,1)} copy-done((bf16[1024,1024]{1,0:T(8,128)(2,1)}, bf16[1024,1024]{1,0:T(8,128)(2,1)S(1)}, u32[]{:S(2)}) %copy-start.1) | copy-done | bytes 2097176
  36.9 0.0 copy-start.5
  36.9 0.8 copy-done.5
  37.7 0.0 copy-start.7
  37.7 0.8 copy-done.7
  38.5 0.0 copy-start
  38.5 0.0 all-to-all-done
  38.5 0.0 copy-start.2
  38.5 1.7 %copy-done.2 = bf16[1024,1024]{1,0:T(8,128)(2,1)S(1)} copy-done((bf16[1024,1024]{1,0:T(8,128)(2,1)S(1)}, bf16[1024,1024]{1,0:T(8,128)(2,1)}, u32[]{:S(2)}) %copy-start.2) | copy-done | bytes 2097176
  40.3 0.0 copy-start.6
  40.3 1.0 copy-done.6
  41.3 0.0 copy-start.8
  41.3 1.0 copy-done.8
  42.3 0.0 copy-start.3
  42.4 0.0 copy-start.4
  42.4 0.7 shard_map.124
  43.1 0.0 copy-start.18
  43.1 39.2 %all_to_all.15 = bf16[512,4,128]{2,1,0:T(4,128)(2,1)S(1)} all-to-all(bf16[512,4,128]{2,1,0:T(4,128)(2,1)S(1)} %bitcast.20), channel_id=1, replica_groups=mesh['dom'=128,'sub'=4] {'dom','sub'}, dimensions={0} | all-to-all | bytes 1048576 | tf_op jit(solution)/shard_map/all_to_all | solution.py:216
  82.3 0.0 copy-done.9
  82.3 0.0 copy-done.10
  82.3 0.0 copy-done.11
  82.3 0.0 copy-done
  82.3 0.0 copy-done.3
  82.3 0.0 copy-done.4
  82.3 3.1 %shard_map.125 = (f32[1,128]{1,0:T(1,128)}, bf16[1024,128]{1,0:T(8,128)(2,1)S(1)}) custom-call(bf16[2048,128]{1,0:T(8,128)(2,1)S(1)} %bitcast.21, bf16[512,512]{1,0:T(8,128)(2,1)S(1)} %copy-done.3, bf16[512,512]{1,0:T(8,128)(2,1)S(1)} %copy-done.4, bf16[1536,1024]{1,0:T(8,128)(2,1)S(1)} %copy-done, f32[1,1024]{1,0:T(1,128)S(1)} %bitcast.25, ...), custom_call_target="tpu_custom_call" | custom-call | flops 1200000000 | bytes 5000000 | tf_op jit(solution)/shard_map/pallas_call | solution.py:19
  85.5 26.0 %all_to_all.16 = bf16[512,2,128]{2,1,0:T(2,128)(2,1)S(1)} all-to-all(bf16[512,2,128]{2,1,0:T(2,128)(2,1)S(1)} %bitcast.23), channel_id=1, replica_groups=mesh['dom'=128,'sub'=4] {'dom','sub'}, dimensions={0} | all-to-all | bytes 524288 | tf_op jit(solution)/shard_map/all_to_all | solution.py:228
  111.4 0.0 copy-done.18
  111.4 1.5 %shard_map.126 = f32[1024,128]{1,0:T(8,128)} custom-call(bf16[1024,128]{1,0:T(8,128)(2,1)S(1)} %bitcast.24, s32[8,128]{1,0:T(8,128)S(1)} %bitcast.32), custom_call_target="tpu_custom_call" | custom-call | flops 268435456 | bytes 1000000 | tf_op jit(solution)/shard_map/pallas_call | solution.py:19
Async XLA Ops:
  0.6 1.0 copy-start.12
  1.6 0.7 copy-start.15
  4.0 34.5 %all-to-all-start = ((bf16[128,8,128]{2,1,0:T(8,128)(2,1)}), bf16[128,8,128]{2,1,0:T(8,128)(2,1)S(1)}, u32[]{:S(2)}, u32[]{:S(2)}) async-start(bf16[128,8,128]{2,1,0:T(8,128)(2,1)} %bitcast.2), calls=%async_computation | async-start | bytes 524288 | tf_op jit(solution)/shard_map/all_to_all | solution.py:198
  22.4 1.0 copy-start.13
  23.4 0.8 copy-start.14
  24.2 0.7 copy-start.16
  24.9 0.7 copy-start.17
  25.6 56.7 %copy-start.9 = (f32[1024]{0:T(1024)S(1)}, f32[1024]{0:T(1024)}, u32[]{:S(2)}) copy-start(f32[1024]{0:T(1024)} %param.18) | copy-start | bytes 12292
  25.6 56.7 %copy-start.10 = (s32[128,2]{0,1:T(2,128)S(1)}, s32[128,2]{0,1:T(2,128)}, u32[]{:S(2)}) copy-start(s32[128,2]{0,1:T(2,128)} %param.20) | copy-start | bytes 3076
  25.6 56.7 %copy-start.11 = (s32[128]{0:T(128)S(1)}, s32[128]{0:T(128)}, u32[]{:S(2)}) copy-start(s32[128]{0:T(128)} %param.21) | copy-start | bytes 1540
  35.6 1.3 %copy-start.1 = (bf16[1024,1024]{1,0:T(8,128)(2,1)}, bf16[1024,1024]{1,0:T(8,128)(2,1)S(1)}, u32[]{:S(2)}) copy-start(bf16[1024,1024]{1,0:T(8,128)(2,1)S(1)} %get-tuple-element.8.near_ref) | copy-start | bytes 6291460
  36.9 0.8 copy-start.5
  37.7 0.8 copy-start.7
  38.5 43.8 %copy-start = (bf16[1536,1024]{1,0:T(8,128)(2,1)S(1)}, bf16[1536,1024]{1,0:T(8,128)(2,1)}, u32[]{:S(2)}) copy-start(bf16[1536,1024]{1,0:T(8,128)(2,1)} %pair_ref.1) | copy-start | bytes 9437188
  38.5 1.7 %copy-start.2 = (bf16[1024,1024]{1,0:T(8,128)(2,1)S(1)}, bf16[1024,1024]{1,0:T(8,128)(2,1)}, u32[]{:S(2)}) copy-start(bf16[1024,1024]{1,0:T(8,128)(2,1)} %copy-done.1) | copy-start | bytes 6291460
  40.3 1.0 copy-start.6
  41.3 1.0 copy-start.8
  42.3 40.0 %copy-start.3 = (bf16[512,512]{1,0:T(8,128)(2,1)S(1)}, bf16[512,512]{1,0:T(8,128)(2,1)}, u32[]{:S(2)}) copy-start(bf16[512,512]{1,0:T(8,128)(2,1)} %self_ref.1) | copy-start | bytes 1572868
  42.4 40.0 %copy-start.4 = (bf16[512,512]{1,0:T(8,128)(2,1)S(1)}, bf16[512,512]{1,0:T(8,128)(2,1)}, u32[]{:S(2)}) copy-start(bf16[512,512]{1,0:T(8,128)(2,1)} %near_ref.1) | copy-start | bytes 1572868
  43.1 68.4 %copy-start.18 = (s32[1,128,4,2]{1,3,2,0:T(2,128)S(1)}, s32[1,128,4,2]{1,3,2,0:T(2,128)}, u32[]{:S(2)}) copy-start(s32[1,128,4,2]{1,3,2,0:T(2,128)} %param.19) | copy-start | bytes 12292

commit v2 on v1

--- a/solution.py
+++ b/solution.py
@@ -15,11 +15,22 @@
     return lax.dot_general(a, b, (((0,), (0,)), ((), ())), preferred_element_type=F32)
 
 
-def call(kernel, out_shape, scratch, flops, nbytes, *args):
+def call(kernel, out_shape, scratch, flops, nbytes, *args, in_specs=None, out_specs=None):
+    where = {"hbm": pl.ANY, "vmem": pltpu.VMEM}
+    specs = {}
+    if in_specs is not None:
+        args = [
+            pltpu.with_memory_space_constraint(a, pltpu.HBM) if w[0] == "hbm" else a
+            for a, w in zip(args, in_specs)
+        ]
+        specs["in_specs"] = [pl.BlockSpec(memory_space=where[w[-1]]) for w in in_specs]
+    if out_specs is not None:
+        specs["out_specs"] = [pl.BlockSpec(memory_space=where[w]) for w in out_specs]
     return pl.pallas_call(
         kernel,
         out_shape=out_shape,
         scratch_shapes=scratch,
+        **specs,
         compiler_params=pltpu.CompilerParams(vmem_limit_bytes=24 * MIB),
         cost_estimate=pl.CostEstimate(flops=flops, bytes_accessed=nbytes, transcendentals=0),
     )(*args)
@@ -39,7 +50,8 @@
 
 
 def count_kernel(
-    act_ref, push_ref, nbr_ref, cnt_ref, near_ref, own_ref, cntp_ref, actp_ref, pick_ref, mine_ref
+    act_ref, push_ref, nbr_ref, cnt_ref, near_out, own_out, actp_out, cntp_ref,
+    near_ref, own_ref, actp_ref, pick_ref, mine_ref, sems,
 ):
     groups, parts = push_ref.shape
     firms = act_ref.shape[0]
@@ -59,6 +71,8 @@
     wanted = (chosen[:degree] * 16.0 + chosen[degree : 2 * degree]).astype(jnp.int32)
     cntp_ref[...] = chosen[2 * degree : 2 * degree + 8]
     actp_ref[...] = contract_first(act_ref[...], pick_ref[...])
+    copies = [pltpu.make_async_copy(actp_ref, actp_out, sems.at[groups])]
+    copies[0].start()
     chunk = 128
     one = jnp.ones((chunk, parts), BF)
     zero = jnp.zeros((chunk, parts), BF)
@@ -80,19 +94,52 @@
         lax.fori_loop(
             0, near_ref.shape[0] // chunk, lambda r, c: fill(r, c, near_ref, firms), 0
         )
+        copies.append(
+            pltpu.make_async_copy(near_ref.at[:, lanes], near_out.at[:, lanes], sems.at[b])
+        )
+        copies[-1].start()
     own_ref[...] = contract_first(act_ref[...], mine_ref[...])
-
-
-def mean_kernel(halo_ref, near_ref, own_ref, cntp_ref, actp_ref, out_ref, tmp_ref):
+    copies.append(pltpu.make_async_copy(own_ref, own_out, sems.at[groups + 1]))
+    copies[-1].start()
+    for copy in copies:
+        copy.wait()
+
+
+def mean_kernel(
+    halo_ref, near_in, own_in, actp_in, cntp_ref, out_ref, tmp_ref, near_ref, own_ref, actp_ref, sems
+):
     groups = 8
     parts = own_ref.shape[1] // groups
-    summed = own_ref[...] + contract_first(halo_ref[...], near_ref[...])
-    mean = (summed / cntp_ref[0:1, :]).astype(BF).astype(F32)
+    parcels = 4
+    step = near_ref.shape[0] // parcels
+    act_copy = pltpu.make_async_copy(actp_in, actp_ref, sems.at[parcels])
+    own_copy = pltpu.make_async_copy(own_in, own_ref, sems.at[parcels + 1])
+    copies = [
+        pltpu.make_async_copy(
+            near_in.at[pl.ds(i * step, step), :], near_ref.at[pl.ds(i * step, step), :], sems.at[i]
+        )
+        for i in range(parcels)
+    ]
+    act_copy.start()
+    own_copy.start()
+    for copy in copies:
+        copy.start()
+    act_copy.wait()
     for b in range(groups):
         lanes = slice(b * parts, (b + 1) * parts)
         at = (b // 2) * 4 + b % 2
         tmp_ref[pl.ds(at, parts, stride=2 * groups), :] = actp_ref[:, lanes].T
-        tmp_ref[pl.ds(at + 2, parts, stride=2 * groups), :] = mean[:, lanes].T
+    own_copy.wait()
+    summed = own_ref[...]
+    for i, copy in enumerate(copies):
+        copy.wait()
+        rows = slice(i * step, (i + 1) * step)
+        summed = summed + contract_first(halo_ref[rows, :], near_ref[rows, :])
+    mean = (summed / cntp_ref[0:1, :]).astype(BF).astype(F32)
+    for b in range(groups):
+        lanes = slice(b * parts, (b + 1) * parts)
+        at = (b // 2) * 4 + b % 2 + 2
+        tmp_ref[pl.ds(at, parts, stride=2 * groups), :] = mean[:, lanes].T
     out_ref[...] = tmp_ref[...].astype(BF)
 
 
@@ -191,27 +238,39 @@
     pushed = doms * subs * cap
     halos = doms * slots
 
+    hbm = pltpu.HBM
+    sems = pltpu.SemaphoreType.DMA
+    fetch = ("hbm", "vmem")
     outgoing = call(
         halo_kernel, shape((halos, narrow), BF), [vmem((halos, narrow), F32)],
-        2 * halos * firms * narrow, 600_000, firm_act, halo_t,
+        2 * halos * firms * narrow, 600_000, firm_act, halo_t, in_specs=[fetch, fetch],
     )
     incoming = lax.all_to_all(
         outgoing.reshape(doms, slots, narrow), "dom", 0, 0, tiled=True
     ).reshape(halos, narrow)
-    near_counts, own_sum, push_count, push_act = call(
+    near_counts, own_sum, push_act, push_count = call(
         count_kernel,
         (
-            shape((halos, pushed), BF), shape((narrow, pushed), F32),
-            shape((8, pushed), F32), shape((narrow, pushed), F32),
+            hbm((halos, pushed), BF), hbm((narrow, pushed), F32), hbm((narrow, pushed), F32),
+            shape((8, pushed), F32),
         ),
-        [vmem((firms, pushed), BF), vmem((firms, pushed), BF)],
+        [
+            vmem((halos, pushed), BF), vmem((narrow, pushed), F32), vmem((narrow, pushed), F32),
+            vmem((firms, pushed), BF), vmem((firms, pushed), BF), sems((subs * cap + 2,)),
+        ],
         10_000_000_000, 4_000_000,
         firm_act, push_t, jnp.transpose(nbr_index), nbr_count.reshape(1, firms),
+        in_specs=[fetch] * 4, out_specs=["hbm"] * 3 + ["vmem"],
     )
     message = call(
-        mean_kernel, shape((2 * pushed, narrow), BF), [vmem((2 * pushed, narrow), F32)],
+        mean_kernel, shape((2 * pushed, narrow), BF),
+        [
+            vmem((2 * pushed, narrow), F32), vmem((halos, pushed), BF), vmem((narrow, pushed), F32),
+            vmem((narrow, pushed), F32), sems((6,)),
+        ],
         2 * halos * pushed * narrow, 4_000_000,
-        incoming, near_counts, own_sum, push_count, push_act,
+        incoming, near_counts, own_sum, push_act, push_count,
+        in_specs=[("vmem",)] + [("hbm",)] * 3 + [("vmem",)],
     )
     arrived = lax.all_to_all(
         message.reshape(doms * subs, 2 * cap, narrow), both, 0, 0, tiled=True

time: 113 us -> 106 us (0.938)
  local copies, waits for them, and re-layouts: 11.5 us -> 0.04 us
  Pallas kernels: 17.1 us -> 21.5 us
  waiting for transfers between devices: 0.01 us -> 2.35 us
  blocking collectives: 65.2 us -> 62.9 us
    unnamed x38 -> x14, local copies, waits for them, and re-layouts: 11.5 us -> 0.04 us
    pallas_call x5, Pallas kernels: 17.1 us -> 21.5 us  [call(): pl.pallas_call(kernel, out_shape=out_shape, scratch_shapes=scratch, **spe...]
    all_to_all x1, waiting for transfers between devices: 0.01 us -> 2.35 us  [per_device(): lax.all_to_all(outgoing.reshape(doms, slots, narrow), 'dom', 0, 0, tiled=...]
    all_to_all x1, blocking collectives: 39.2 us -> 36.9 us  [per_device(): lax.all_to_all(message.reshape(doms * subs, 2 * cap, narrow), both, 0, 0,...]
  transfers between devices with their start and end apart: 1 -> 1, of which waited for: 0 -> 1; matrix products, arithmetic and copies ran while one was open for 0% -> 0% of each run, Pallas kernels for 9% -> 11%
where the time goes in v2:
time: 106 us
  blocking collectives  62.9 us (59%)
  Pallas kernels  21.5 us (20%)
  starting transfers between devices  18.4 us (17%)
  waiting for transfers between devices  2.35 us (2%)
    all_to_all x1, blocking collectives, per_device(): lax.all_to_all(message.reshape(doms * subs, 2 * cap, narrow), both, 0, 0,...  36.9 us
    all_to_all x1, blocking collectives, per_device(): lax.all_to_all(back.reshape(doms * subs, cap, narrow), both, 0, 0, tiled=...  26 us
    pallas_call x5, Pallas kernels, call(): pl.pallas_call(kernel, out_shape=out_shape, scratch_shapes=scratch, **spe...  21.5 us
    all_to_all x1, starting transfers between devices, per_device(): lax.all_to_all(outgoing.reshape(doms, slots, narrow), 'dom', 0, 0, tiled=...  18.4 us
    all_to_all x1, waiting for transfers between devices, per_device(): lax.all_to_all(outgoing.reshape(doms, slots, narrow), 'dom', 0, 0, tiled=...  2.35 us
  transfers between devices with their start and end apart: 1, of which 1 were waited for; matrix products, arithmetic and copies ran while one was open for 0% of the time, Pallas kernels for 11%

profile of v2, /device:TPU:1, one launch (start us, length us, event | category | flops | bytes accessed | tf_op | source)
XLA Modules:
  0.0 106.0 jit_solution(6771101949753092537)
XLA Ops:
  0.6 2.7 %shard_map.122 = bf16[1024,128]{1,0:T(8,128)(2,1)} custom-call(bf16[1024,128]{1,0:T(8,128)(2,1)} %act_ref.3, s32[8,128]{1,0:T(8,128)} %bitcast.31), custom_call_target="tpu_custom_call" | custom-call | flops 268435456 | bytes 600000 | tf_op jit(solution)/shard_map/pallas_call | solution.py:29
  3.3 18.4 %all-to-all-start = ((bf16[128,8,128]{2,1,0:T(8,128)(2,1)}), bf16[128,8,128]{2,1,0:T(8,128)(2,1)S(1)}, u32[]{:S(2)}, u32[]{:S(2)}) async-start(bf16[128,8,128]{2,1,0:T(8,128)(2,1)} %bitcast.2), calls=%async_computation | async-start | bytes 524288 | tf_op jit(solution)/shard_map/all_to_all | solution.py:248
  21.7 11.8 %shard_map.123 = (bf16[1024,1024]{1,0:T(8,128)(2,1)}, f32[128,1024]{1,0:T(8,128)}, f32[128,1024]{1,0:T(8,128)}, f32[8,1024]{1,0:T(8,128)S(1)}) custom-call(bf16[1024,128]{1,0:T(8,128)(2,1)} %act_ref.3, s32[8,128]{1,0:T(8,128)} %bitcast.28, s32[16,1024]{1,0:T(8,128)} %bitcast.30, s32[1,1024]{1,0:T(1,128)} %bitcast.32), custom_call_target="tpu_custom_call" | custom-call | flops 10000000000 | bytes 4000000 | tf_op jit(solution)/shard_map/pallas_call | solution.py:29
  33.5 0.0 copy-start
  33.5 0.0 copy-start.3
  33.6 0.0 copy-start.4
  33.6 0.0 copy-start.5
  33.6 2.4 %all-to-all-done = bf16[128,8,128]{2,1,0:T(8,128)(2,1)S(1)} async-done(((bf16[128,8,128]{2,1,0:T(8,128)(2,1)}), bf16[128,8,128]{2,1,0:T(8,128)(2,1)S(1)}, u32[]{:S(2)}, u32[]{:S(2)}) %all-to-all-start) | async-done | bytes 262176 | tf_op jit(solution)/shard_map/all_to_all | solution.py:248
  35.9 0.0 copy-start.1
  35.9 0.0 copy-start.2
  35.9 2.4 %shard_map.124 = bf16[2048,128]{1,0:T(8,128)(2,1)S(1)} custom-call(bf16[1024,128]{1,0:T(8,128)(2,1)S(1)} %bitcast.22, bf16[1024,1024]{1,0:T(8,128)(2,1)} %get-tuple-element.8.near_in, f32[128,1024]{1,0:T(8,128)} %get-tuple-element.9.own_in, f32[128,1024]{1,0:T(8,128)} %get-tuple-element.10.actp_in, f32[8,1024]{1,0:T(8,128)S(1)} %get-tuple-element.11.cntp_ref), custom_call_target="tpu_custom_call" | custom-call | flops 268435456 | bytes 4000000 | tf_op jit(solution)/shard_map/pallas_call | solution.py:29
  38.4 0.0 copy-start.6
  38.4 36.9 %all_to_all.15 = bf16[512,4,128]{2,1,0:T(4,128)(2,1)S(1)} all-to-all(bf16[512,4,128]{2,1,0:T(4,128)(2,1)S(1)} %bitcast.20), channel_id=1, replica_groups=mesh['dom'=128,'sub'=4] {'dom','sub'}, dimensions={0} | all-to-all | bytes 1048576 | tf_op jit(solution)/shard_map/all_to_all | solution.py:275
  75.3 0.0 copy-done
  75.3 0.0 copy-done.3
  75.3 0.0 copy-done.4
  75.3 0.0 copy-done.5
  75.3 0.0 copy-done.1
  75.3 0.0 copy-done.2
  75.4 3.1 %shard_map.125 = (f32[1,128]{1,0:T(1,128)}, bf16[1024,128]{1,0:T(8,128)(2,1)S(1)}) custom-call(bf16[2048,128]{1,0:T(8,128)(2,1)S(1)} %bitcast.21, bf16[512,512]{1,0:T(8,128)(2,1)S(1)} %copy-done.1, bf16[512,512]{1,0:T(8,128)(2,1)S(1)} %copy-done.2, bf16[1536,1024]{1,0:T(8,128)(2,1)S(1)} %copy-done, f32[1,1024]{1,0:T(1,128)S(1)} %bitcast.25, ...), custom_call_target="tpu_custom_call" | custom-call | flops 1200000000 | bytes 5000000 | tf_op jit(solution)/shard_map/pallas_call | solution.py:29
  78.5 26.0 %all_to_all.16 = bf16[512,2,128]{2,1,0:T(2,128)(2,1)S(1)} all-to-all(bf16[512,2,128]{2,1,0:T(2,128)(2,1)S(1)} %bitcast.23), channel_id=1, replica_groups=mesh['dom'=128,'sub'=4] {'dom','sub'}, dimensions={0} | all-to-all | bytes 524288 | tf_op jit(solution)/shard_map/all_to_all | solution.py:287
  104.4 0.0 copy-done.6
  104.4 1.5 %shard_map.126 = f32[1024,128]{1,0:T(8,128)} custom-call(bf16[1024,128]{1,0:T(8,128)(2,1)S(1)} %bitcast.24, s32[8,128]{1,0:T(8,128)S(1)} %bitcast.29), custom_call_target="tpu_custom_call" | custom-call | flops 268435456 | bytes 1000000 | tf_op jit(solution)/shard_map/pallas_call | solution.py:29
Async XLA Ops:
  3.3 32.7 %all-to-all-start = ((bf16[128,8,128]{2,1,0:T(8,128)(2,1)}), bf16[128,8,128]{2,1,0:T(8,128)(2,1)S(1)}, u32[]{:S(2)}, u32[]{:S(2)}) async-start(bf16[128,8,128]{2,1,0:T(8,128)(2,1)} %bitcast.2), calls=%async_computation | async-start | bytes 524288 | tf_op jit(solution)/shard_map/all_to_all | solution.py:248
  33.5 41.8 %copy-start = (bf16[1536,1024]{1,0:T(8,128)(2,1)S(1)}, bf16[1536,1024]{1,0:T(8,128)(2,1)}, u32[]{:S(2)}) copy-start(bf16[1536,1024]{1,0:T(8,128)(2,1)} %pair_ref.1) | copy-start | bytes 9437188
  33.5 41.8 %copy-start.3 = (f32[1024]{0:T(1024)S(1)}, f32[1024]{0:T(1024)}, u32[]{:S(2)}) copy-start(f32[1024]{0:T(1024)} %param.18) | copy-start | bytes 12292
  33.6 41.8 %copy-start.4 = (s32[128,2]{0,1:T(2,128)S(1)}, s32[128,2]{0,1:T(2,128)}, u32[]{:S(2)}) copy-start(s32[128,2]{0,1:T(2,128)} %param.20) | copy-start | bytes 3076
  33.6 41.8 %copy-start.5 = (s32[128]{0:T(128)S(1)}, s32[128]{0:T(128)}, u32[]{:S(2)}) copy-start(s32[128]{0:T(128)} %param.21) | copy-start | bytes 1540
  35.9 39.4 %copy-start.1 = (bf16[512,512]{1,0:T(8,128)(2,1)S(1)}, bf16[512,512]{1,0:T(8,128)(2,1)}, u32[]{:S(2)}) copy-start(bf16[512,512]{1,0:T(8,128)(2,1)} %self_ref.1) | copy-start | bytes 1572868
  35.9 39.4 %copy-start.2 = (bf16[512,512]{1,0:T(8,128)(2,1)S(1)}, bf16[512,512]{1,0:T(8,128)(2,1)}, u32[]{:S(2)}) copy-start(bf16[512,512]{1,0:T(8,128)(2,1)} %near_ref.1) | copy-start | bytes 1572868
  38.4 66.1 %copy-start.6 = (s32[1,128,4,2]{1,3,2,0:T(2,128)S(1)}, s32[1,128,4,2]{1,3,2,0:T(2,128)}, u32[]{:S(2)}) copy-start(s32[1,128,4,2]{1,3,2,0:T(2,128)} %param.19) | copy-start | bytes 12292

commit v3 on v2

--- a/solution.py
+++ b/solution.py
@@ -36,70 +36,105 @@
     )(*args)
 
 
-def halo_kernel(act_ref, rows_ref, out_ref, tmp_ref):
+def one_hot_rows(columns, width):
+    number = lax.broadcasted_iota(jnp.int32, (columns.shape[0], width), 1)
+    return [
+        jnp.where(columns[:, j : j + 1] == number, 1.0, 0.0).astype(BF)
+        for j in range(columns.shape[1])
+    ]
+
+
+def halo_kernel(act_ref, rows_ref, out_ref, tmp_ref, pick_ref):
     slots, parts = rows_ref.shape
-    rows = rows_ref[...].T
-    act = act_ref[...]
-    row = lax.broadcasted_iota(jnp.int32, (parts, act.shape[0]), 1)
+    for j, rows in enumerate(one_hot_rows(rows_ref[...].T, act_ref.shape[0])):
+        pick_ref[j * parts : (j + 1) * parts, :] = rows
+    picked = jnp.dot(pick_ref[...], act_ref[...], preferred_element_type=F32)
     for j in range(slots):
-        pick = jnp.where(rows[:, j : j + 1] == row, 1.0, 0.0).astype(BF)
-        tmp_ref[pl.ds(j, parts, stride=slots), :] = jnp.dot(
-            pick, act, preferred_element_type=F32
-        )
+        tmp_ref[pl.ds(j, parts, stride=slots), :] = picked[j * parts : (j + 1) * parts]
     out_ref[...] = tmp_ref[...].astype(BF)
 
 
 def count_kernel(
     act_ref, push_ref, nbr_ref, cnt_ref, near_out, own_out, actp_out, cntp_ref,
-    near_ref, own_ref, actp_ref, pick_ref, mine_ref, sems,
+    near_ref, own_ref, actp_ref, pick_ref, mine_ref, where_ref, sems,
 ):
     groups, parts = push_ref.shape
     firms = act_ref.shape[0]
     degree = nbr_ref.shape[0]
-    firm = lax.broadcasted_iota(jnp.int32, (firms, parts), 0)
-    for b in range(groups):
-        pick_ref[:, b * parts : (b + 1) * parts] = jnp.where(
-            firm == push_ref[b : b + 1, :], 1.0, 0.0
+    pushed = groups * parts
+    i32, i16 = jnp.int32, jnp.int16
+    for j, rows in enumerate(one_hot_rows(push_ref[...].T, firms)):
+        pick_ref[j * parts : (j + 1) * parts, :] = rows
+    pick = pick_ref[...]
+    count = cnt_ref[...]
+    live = lax.broadcasted_iota(i32, (degree, firms), 0) < count
+    slot = jnp.where(live, nbr_ref[...], DEAD)
+    counts = jnp.broadcast_to(count, (degree, firms))
+    stack = jnp.concatenate([slot >> 7, slot & 127, counts], 0).astype(F32).astype(BF)
+    chosen = lax.dot_general(
+        pick, stack, (((1,), (1,)), ((), ())), preferred_element_type=F32
+    )
+    for j in range(groups):
+        block = chosen[j * parts : (j + 1) * parts, 2 * degree : 3 * degree]
+        cntp_ref[j : j + 1, :] = block.T[0:1, :]
+    actp_ref[...] = jnp.dot(pick, act_ref[...], preferred_element_type=F32).astype(BF)
+    copies = [pltpu.make_async_copy(actp_ref, actp_out, sems.at[0])]
+    copies[0].start()
+    batch = 16
+    span = batch * degree
+    shape = (2 * degree, 2 * span)
+    lane = lax.broadcasted_iota(i32, shape, 1)
+    spread = jnp.where(
+        lax.broadcasted_iota(i32, shape, 0) == (lane // span) * degree + lane % degree, 1.0, 0.0
+    ).astype(BF)
+    wide = jnp.dot(chosen[:, : 2 * degree].astype(BF), spread, preferred_element_type=F32)
+    row = lax.broadcasted_iota(i32, (pushed, 2 * span), 0) % batch
+    lane = (lax.broadcasted_iota(i32, (pushed, 2 * span), 1) % span) // degree
+    wide = jnp.where(row == lane, wide, 0.0).astype(BF)
+    shape = (pushed // batch, pushed)
+    gather = jnp.where(
+        lax.broadcasted_iota(i32, shape, 1) // batch == lax.broadcasted_iota(i32, shape, 0), 1.0, 0.0
+    ).astype(BF)
+    where_ref[...] = jnp.dot(gather, wide, preferred_element_type=F32)
+    own_row = (
+        lax.broadcasted_iota(i32, (batch, span), 1) // degree
+        == lax.broadcasted_iota(i32, (batch, span), 0)
+    )
+    low_number = lax.broadcasted_iota(i32, (128, span), 0).astype(i16)
+    one = jnp.ones((batch, span), BF)
+    zero = jnp.zeros((batch, span), BF)
+    mine_blocks = firms // 128
+    near_blocks = near_ref.shape[1] // 128
+
+    def fill(g, carry):
+        line = where_ref[pl.ds(g, 1), :]
+        high = jnp.where(own_row, jnp.broadcast_to(line[:, :span], (batch, span)), -1.0)
+        high = high.astype(i32).astype(i16)
+        lhs = jnp.concatenate(
+            [jnp.where(high == i16(h), one, zero) for h in range(mine_blocks + near_blocks)], 0
+        )
+        low = jnp.broadcast_to(line[:, span:], (128, span)).astype(i32).astype(i16)
+        rhs = jnp.where(low == low_number, jnp.ones((128, span), BF), jnp.zeros((128, span), BF))
+        counts = lax.dot_general(
+            lhs, rhs, (((1,), (1,)), ((), ())), preferred_element_type=F32
         ).astype(BF)
-    count = cnt_ref[...]
-    live = lax.broadcasted_iota(jnp.int32, (degree, firms), 0) < count
-    slot = jnp.where(live, nbr_ref[...], DEAD)
-    stack = jnp.concatenate(
-        [slot >> 4, slot & 15, jnp.broadcast_to(count, (degree, firms))], 0
-    ).astype(F32)
-    chosen = jnp.dot(stack.astype(BF), pick_ref[...], preferred_element_type=F32)
-    wanted = (chosen[:degree] * 16.0 + chosen[degree : 2 * degree]).astype(jnp.int32)
-    cntp_ref[...] = chosen[2 * degree : 2 * degree + 8]
-    actp_ref[...] = contract_first(act_ref[...], pick_ref[...])
-    copies = [pltpu.make_async_copy(actp_ref, actp_out, sems.at[groups])]
-    copies[0].start()
-    chunk = 128
-    one = jnp.ones((chunk, parts), BF)
-    zero = jnp.zeros((chunk, parts), BF)
-    base = lax.broadcasted_iota(jnp.int32, (chunk, parts), 0).astype(jnp.int16)
-    for b in range(groups):
-        lanes = slice(b * parts, (b + 1) * parts)
-        want = wanted[:, lanes].astype(jnp.int16)
-        spread = [jnp.broadcast_to(want[k : k + 1, :], (chunk, parts)) for k in range(degree)]
-
-        def fill(r, carry, out, first):
-            number = base + (first + r * chunk).astype(jnp.int16)
-            total = zero
-            for k in range(degree):
-                total = total + jnp.where(spread[k] == number, one, zero)
-            out[pl.ds(pl.multiple_of(r * chunk, chunk), chunk), lanes] = total
-            return carry
-
-        lax.fori_loop(0, firms // chunk, lambda r, c: fill(r, c, mine_ref, 0), 0)
-        lax.fori_loop(
-            0, near_ref.shape[0] // chunk, lambda r, c: fill(r, c, near_ref, firms), 0
-        )
-        copies.append(
-            pltpu.make_async_copy(near_ref.at[:, lanes], near_out.at[:, lanes], sems.at[b])
-        )
+        rows = pl.ds(pl.multiple_of(g * batch, batch), batch)
+        for h in range(mine_blocks):
+            mine_ref[rows, h * 128 : (h + 1) * 128] = counts[h * batch : (h + 1) * batch]
+        for h in range(near_blocks):
+            at = (mine_blocks + h) * batch
+            near_ref[rows, h * 128 : (h + 1) * 128] = counts[at : at + batch]
+        return carry
+
+    parcels = 4
+    each = pushed // batch // parcels
+    for p in range(parcels):
+        lax.fori_loop(p * each, (p + 1) * each, fill, 0, unroll=4)
+        rows = pl.ds(p * each * batch, each * batch)
+        copies.append(pltpu.make_async_copy(near_ref.at[rows, :], near_out.at[rows, :], sems.at[1 + p]))
         copies[-1].start()
-    own_ref[...] = contract_first(act_ref[...], mine_ref[...])
-    copies.append(pltpu.make_async_copy(own_ref, own_out, sems.at[groups + 1]))
+    own_ref[...] = jnp.dot(mine_ref[...], act_ref[...], preferred_element_type=F32)
+    copies.append(pltpu.make_async_copy(own_ref, own_out, sems.at[1 + parcels]))
     copies[-1].start()
     for copy in copies:
         copy.wait()
@@ -108,8 +143,7 @@
 def mean_kernel(
     halo_ref, near_in, own_in, actp_in, cntp_ref, out_ref, tmp_ref, near_ref, own_ref, actp_ref, sems
 ):
-    groups = 8
-    parts = own_ref.shape[1] // groups
+    groups, parts = cntp_ref.shape
     parcels = 4
     step = near_ref.shape[0] // parcels
     act_copy = pltpu.make_async_copy(actp_in, actp_ref, sems.at[parcels])
@@ -124,22 +158,24 @@
     own_copy.start()
     for copy in copies:
         copy.start()
+    divisor = cntp_ref[...].T
+    halo = halo_ref[...]
+
+    def place(b, rows, kind):
+        tmp_ref[pl.ds((b // 2) * 4 + kind * 2 + b % 2, parts, stride=2 * groups), :] = rows
+
     act_copy.wait()
     for b in range(groups):
-        lanes = slice(b * parts, (b + 1) * parts)
-        at = (b // 2) * 4 + b % 2
-        tmp_ref[pl.ds(at, parts, stride=2 * groups), :] = actp_ref[:, lanes].T
+        place(b, actp_ref[b * parts : (b + 1) * parts, :].astype(F32), 0)
     own_copy.wait()
-    summed = own_ref[...]
     for i, copy in enumerate(copies):
         copy.wait()
         rows = slice(i * step, (i + 1) * step)
-        summed = summed + contract_first(halo_ref[rows, :], near_ref[rows, :])
-    mean = (summed / cntp_ref[0:1, :]).astype(BF).astype(F32)
-    for b in range(groups):
-        lanes = slice(b * parts, (b + 1) * parts)
-        at = (b // 2) * 4 + b % 2 + 2
-        tmp_ref[pl.ds(at, parts, stride=2 * groups), :] = mean[:, lanes].T
+        summed = own_ref[rows, :] + jnp.dot(near_ref[rows, :], halo, preferred_element_type=F32)
+        for j in range(step // parts):
+            b = i * (step // parts) + j
+            mean = summed[j * parts : (j + 1) * parts] / divisor[:, b : b + 1]
+            place(b, mean.astype(BF).astype(F32), 1)
     out_ref[...] = tmp_ref[...].astype(BF)
 
 
@@ -242,7 +278,8 @@
     sems = pltpu.SemaphoreType.DMA
     fetch = ("hbm", "vmem")
     outgoing = call(
-        halo_kernel, shape((halos, narrow), BF), [vmem((halos, narrow), F32)],
+        halo_kernel, shape((halos, narrow), BF),
+        [vmem((halos, narrow), F32), vmem((halos, firms), BF)],
         2 * halos * firms * narrow, 600_000, firm_act, halo_t, in_specs=[fetch, fetch],
     )
     incoming = lax.all_to_all(
@@ -251,12 +288,13 @@
     near_counts, own_sum, push_act, push_count = call(
         count_kernel,
         (
-            hbm((halos, pushed), BF), hbm((narrow, pushed), F32), hbm((narrow, pushed), F32),
-            shape((8, pushed), F32),
+            hbm((pushed, halos), BF), hbm((pushed, narrow), F32), hbm((pushed, narrow), BF),
+            shape((subs * cap, doms), F32),
         ),
         [
-            vmem((halos, pushed), BF), vmem((narrow, pushed), F32), vmem((narrow, pushed), F32),
-            vmem((firms, pushed), BF), vmem((firms, pushed), BF), sems((subs * cap + 2,)),
+            vmem((pushed, halos), BF), vmem((pushed, narrow), F32), vmem((pushed, narrow), BF),
+            vmem((pushed, firms), BF), vmem((pushed, firms), BF), vmem((pushed // 16, 512), F32),
+            sems((6,)),
         ],
         10_000_000_000, 4_000_000,
         firm_act, push_t, jnp.transpose(nbr_index), nbr_count.reshape(1, firms),
@@ -265,8 +303,8 @@
     message = call(
         mean_kernel, shape((2 * pushed, narrow), BF),
         [
-            vmem((2 * pushed, narrow), F32), vmem((halos, pushed), BF), vmem((narrow, pushed), F32),
-            vmem((narrow, pushed), F32), sems((6,)),
+            vmem((2 * pushed, narrow), F32), vmem((pushed, halos), BF), vmem((pushed, narrow), F32),
+            vmem((pushed, narrow), BF), sems((6,)),
         ],
         2 * halos * pushed * narrow, 4_000_000,
         incoming, near_counts, own_sum, push_act, push_count,

time: 106 us -> 104 us (0.981)
  waiting for transfers between devices: 2.35 us -> 4.96 us
  blocking collectives: 62.9 us -> 60.3 us
  Pallas kernels: 21.5 us -> 19.1 us
    all_to_all x1, blocking collectives: 36.9 us -> 34.3 us  [per_device(): lax.all_to_all(message.reshape(doms * subs, 2 * cap, narrow), both, 0, 0,...]
    all_to_all x1, waiting for transfers between devices: 2.35 us -> 4.96 us  [per_device(): lax.all_to_all(outgoing.reshape(doms, slots, narrow), 'dom', 0, 0, tiled=...]
    pallas_call x5, Pallas kernels: 21.5 us -> 19.1 us  [call(): pl.pallas_call(kernel, out_shape=out_shape, scratch_shapes=scratch, **spe...]
  transfers between devices with their start and end apart: 1 -> 1, of which waited for: 1 -> 1; matrix products, arithmetic and copies ran while one was open for 0% -> 0% of each run, Pallas kernels for 11% -> 9%
where the time goes in v3:
time: 104 us
  blocking collectives  60.3 us (58%)
  Pallas kernels  19.1 us (18%)
  starting transfers between devices  18.4 us (18%)
  waiting for transfers between devices  4.96 us (5%)
    all_to_all x1, blocking collectives, per_device(): lax.all_to_all(message.reshape(doms * subs, 2 * cap, narrow), both, 0, 0,...  34.3 us
    all_to_all x1, blocking collectives, per_device(): lax.all_to_all(back.reshape(doms * subs, cap, narrow), both, 0, 0, tiled=...  25.9 us
    pallas_call x5, Pallas kernels, call(): pl.pallas_call(kernel, out_shape=out_shape, scratch_shapes=scratch, **spe...  19.1 us
    all_to_all x1, starting transfers between devices, per_device(): lax.all_to_all(outgoing.reshape(doms, slots, narrow), 'dom', 0, 0, tiled=...  18.4 us
    all_to_all x1, waiting for transfers between devices, per_device(): lax.all_to_all(outgoing.reshape(doms, slots, narrow), 'dom', 0, 0, tiled=...  4.96 us
  transfers between devices with their start and end apart: 1, of which 1 were waited for; matrix products, arithmetic and copies ran while one was open for 0% of the time, Pallas kernels for 9%

profile of v3, /device:TPU:1, one launch (start us, length us, event | category | flops | bytes accessed | tf_op | source)
XLA Modules:
  0.0 103.5 jit_solution(1618106206908427868)
XLA Ops:
  0.6 2.5 %shard_map.122 = bf16[1024,128]{1,0:T(8,128)(2,1)} custom-call(bf16[1024,128]{1,0:T(8,128)(2,1)} %act_ref.3, s32[8,128]{1,0:T(8,128)} %bitcast.31), custom_call_target="tpu_custom_call" | custom-call | flops 268435456 | bytes 600000 | tf_op jit(solution)/shard_map/pallas_call | solution.py:29
  3.1 18.4 %all-to-all-start = ((bf16[128,8,128]{2,1,0:T(8,128)(2,1)}), bf16[128,8,128]{2,1,0:T(8,128)(2,1)S(1)}, u32[]{:S(2)}, u32[]{:S(2)}) async-start(bf16[128,8,128]{2,1,0:T(8,128)(2,1)} %bitcast.2), calls=%async_computation | async-start | bytes 524288 | tf_op jit(solution)/shard_map/all_to_all | solution.py:285
  21.6 9.2 %shard_map.123 = (bf16[1024,1024]{1,0:T(8,128)(2,1)}, f32[1024,128]{1,0:T(8,128)}, bf16[1024,128]{1,0:T(8,128)(2,1)}, f32[8,128]{1,0:T(8,128)S(1)}) custom-call(bf16[1024,128]{1,0:T(8,128)(2,1)} %act_ref.3, s32[8,128]{1,0:T(8,128)} %bitcast.28, s32[16,1024]{1,0:T(8,128)} %bitcast.30, s32[1,1024]{1,0:T(1,128)} %bitcast.32), custom_call_target="tpu_custom_call" | custom-call | flops 10000000000 | bytes 4000000 | tf_op jit(solution)/shard_map/pallas_call | solution.py:29
  30.8 0.0 copy-start
  30.8 0.0 copy-start.3
  30.8 0.0 copy-start.4
  30.8 0.0 copy-start.5
  30.8 5.0 %all-to-all-done = bf16[128,8,128]{2,1,0:T(8,128)(2,1)S(1)} async-done(((bf16[128,8,128]{2,1,0:T(8,128)(2,1)}), bf16[128,8,128]{2,1,0:T(8,128)(2,1)S(1)}, u32[]{:S(2)}, u32[]{:S(2)}) %all-to-all-start) | async-done | bytes 262176 | tf_op jit(solution)/shard_map/all_to_all | solution.py:285
  35.8 0.0 copy-start.1
  35.8 0.0 copy-start.2
  35.8 2.7 %shard_map.124 = bf16[2048,128]{1,0:T(8,128)(2,1)S(1)} custom-call(bf16[1024,128]{1,0:T(8,128)(2,1)S(1)} %bitcast.22, bf16[1024,1024]{1,0:T(8,128)(2,1)} %get-tuple-element.8.near_in, f32[1024,128]{1,0:T(8,128)} %get-tuple-element.9.own_in, bf16[1024,128]{1,0:T(8,128)(2,1)} %get-tuple-element.10.actp_in, f32[8,128]{1,0:T(8,128)S(1)} %get-tuple-element.11.cntp_ref), custom_call_target="tpu_custom_call" | custom-call | flops 268435456 | bytes 4000000 | tf_op jit(solution)/shard_map/pallas_call | solution.py:29
  38.5 0.0 copy-start.6
  38.5 34.3 %all_to_all.15 = bf16[512,4,128]{2,1,0:T(4,128)(2,1)S(1)} all-to-all(bf16[512,4,128]{2,1,0:T(4,128)(2,1)S(1)} %bitcast.21), channel_id=1, replica_groups=mesh['dom'=128,'sub'=4] {'dom','sub'}, dimensions={0} | all-to-all | bytes 1048576 | tf_op jit(solution)/shard_map/all_to_all | solution.py:313
  72.8 0.0 copy-done
  72.8 0.0 copy-done.3
  72.8 0.0 copy-done.4
  72.9 0.0 copy-done.5
  72.9 0.0 copy-done.1
  72.9 0.0 copy-done.2
  72.9 3.1 %shard_map.125 = (f32[1,128]{1,0:T(1,128)}, bf16[1024,128]{1,0:T(8,128)(2,1)S(1)}) custom-call(bf16[2048,128]{1,0:T(8,128)(2,1)S(1)} %bitcast.20, bf16[512,512]{1,0:T(8,128)(2,1)S(1)} %copy-done.1, bf16[512,512]{1,0:T(8,128)(2,1)S(1)} %copy-done.2, bf16[1536,1024]{1,0:T(8,128)(2,1)S(1)} %copy-done, f32[1,1024]{1,0:T(1,128)S(1)} %bitcast.25, ...), custom_call_target="tpu_custom_call" | custom-call | flops 1200000000 | bytes 5000000 | tf_op jit(solution)/shard_map/pallas_call | solution.py:29
  76.0 25.9 %all_to_all.16 = bf16[512,2,128]{2,1,0:T(2,128)(2,1)S(1)} all-to-all(bf16[512,2,128]{2,1,0:T(2,128)(2,1)S(1)} %bitcast.23), channel_id=1, replica_groups=mesh['dom'=128,'sub'=4] {'dom','sub'}, dimensions={0} | all-to-all | bytes 524288 | tf_op jit(solution)/shard_map/all_to_all | solution.py:325
  102.0 0.0 copy-done.6
  102.0 1.5 %shard_map.126 = f32[1024,128]{1,0:T(8,128)} custom-call(bf16[1024,128]{1,0:T(8,128)(2,1)S(1)} %bitcast.24, s32[8,128]{1,0:T(8,128)S(1)} %bitcast.29), custom_call_target="tpu_custom_call" | custom-call | flops 268435456 | bytes 1000000 | tf_op jit(solution)/shard_map/pallas_call | solution.py:29
Async XLA Ops:
  3.1 32.7 %all-to-all-start = ((bf16[128,8,128]{2,1,0:T(8,128)(2,1)}), bf16[128,8,128]{2,1,0:T(8,128)(2,1)S(1)}, u32[]{:S(2)}, u32[]{:S(2)}) async-start(bf16[128,8,128]{2,1,0:T(8,128)(2,1)} %bitcast.2), calls=%async_computation | async-start | bytes 524288 | tf_op jit(solution)/shard_map/all_to_all | solution.py:285
  30.8 42.1 %copy-start = (bf16[1536,1024]{1,0:T(8,128)(2,1)S(1)}, bf16[1536,1024]{1,0:T(8,128)(2,1)}, u32[]{:S(2)}) copy-start(bf16[1536,1024]{1,0:T(8,128)(2,1)} %pair_ref.1) | copy-start | bytes 9437188
  30.8 42.1 %copy-start.3 = (f32[1024]{0:T(1024)S(1)}, f32[1024]{0:T(1024)}, u32[]{:S(2)}) copy-start(f32[1024]{0:T(1024)} %param.18) | copy-start | bytes 12292
  30.8 42.1 %copy-start.4 = (s32[128,2]{0,1:T(2,128)S(1)}, s32[128,2]{0,1:T(2,128)}, u32[]{:S(2)}) copy-start(s32[128,2]{0,1:T(2,128)} %param.20) | copy-start | bytes 3076
  30.8 42.0 %copy-start.5 = (s32[128]{0:T(128)S(1)}, s32[128]{0:T(128)}, u32[]{:S(2)}) copy-start(s32[128]{0:T(128)} %param.21) | copy-start | bytes 1540
  35.8 37.1 %copy-start.1 = (bf16[512,512]{1,0:T(8,128)(2,1)S(1)}, bf16[512,512]{1,0:T(8,128)(2,1)}, u32[]{:S(2)}) copy-start(bf16[512,512]{1,0:T(8,128)(2,1)} %self_ref.1) | copy-start | bytes 1572868
  35.8 37.1 %copy-start.2 = (bf16[512,512]{1,0:T(8,128)(2,1)S(1)}, bf16[512,512]{1,0:T(8,128)(2,1)}, u32[]{:S(2)}) copy-start(bf16[512,512]{1,0:T(8,128)(2,1)} %near_ref.1) | copy-start | bytes 1572868
  38.5 63.5 %copy-start.6 = (s32[1,128,4,2]{1,3,2,0:T(2,128)S(1)}, s32[1,128,4,2]{1,3,2,0:T(2,128)}, u32[]{:S(2)}) copy-start(s32[1,128,4,2]{1,3,2,0:T(2,128)} %param.19) | copy-start | bytes 12292

commit v4 on v3

--- a/solution.py
+++ b/solution.py
@@ -55,8 +55,8 @@
 
 
 def count_kernel(
-    act_ref, push_ref, nbr_ref, cnt_ref, near_out, own_out, actp_out, cntp_ref,
-    near_ref, own_ref, actp_ref, pick_ref, mine_ref, where_ref, sems,
+    act_ref, push_ref, nbr_ref, cnt_ref, near_ref, own_ref, actp_ref, cntp_ref,
+    pick_ref, mine_ref, where_ref,
 ):
     groups, parts = push_ref.shape
     firms = act_ref.shape[0]
@@ -78,8 +78,6 @@
         block = chosen[j * parts : (j + 1) * parts, 2 * degree : 3 * degree]
         cntp_ref[j : j + 1, :] = block.T[0:1, :]
     actp_ref[...] = jnp.dot(pick, act_ref[...], preferred_element_type=F32).astype(BF)
-    copies = [pltpu.make_async_copy(actp_ref, actp_out, sems.at[0])]
-    copies[0].start()
     batch = 16
     span = batch * degree
     shape = (2 * degree, 2 * span)
@@ -126,66 +124,42 @@
             near_ref[rows, h * 128 : (h + 1) * 128] = counts[at : at + batch]
         return carry
 
-    parcels = 4
-    each = pushed // batch // parcels
-    for p in range(parcels):
-        lax.fori_loop(p * each, (p + 1) * each, fill, 0, unroll=4)
-        rows = pl.ds(p * each * batch, each * batch)
-        copies.append(pltpu.make_async_copy(near_ref.at[rows, :], near_out.at[rows, :], sems.at[1 + p]))
-        copies[-1].start()
+    lax.fori_loop(0, pushed // batch, fill, 0, unroll=4)
     own_ref[...] = jnp.dot(mine_ref[...], act_ref[...], preferred_element_type=F32)
-    copies.append(pltpu.make_async_copy(own_ref, own_out, sems.at[1 + parcels]))
-    copies[-1].start()
-    for copy in copies:
-        copy.wait()
-
-
-def mean_kernel(
-    halo_ref, near_in, own_in, actp_in, cntp_ref, out_ref, tmp_ref, near_ref, own_ref, actp_ref, sems
-):
+
+
+def mean_kernel(halo_ref, near_ref, own_ref, actp_ref, cntp_ref, out_ref, tmp_ref):
     groups, parts = cntp_ref.shape
-    parcels = 4
-    step = near_ref.shape[0] // parcels
-    act_copy = pltpu.make_async_copy(actp_in, actp_ref, sems.at[parcels])
-    own_copy = pltpu.make_async_copy(own_in, own_ref, sems.at[parcels + 1])
-    copies = [
-        pltpu.make_async_copy(
-            near_in.at[pl.ds(i * step, step), :], near_ref.at[pl.ds(i * step, step), :], sems.at[i]
-        )
-        for i in range(parcels)
-    ]
-    act_copy.start()
-    own_copy.start()
-    for copy in copies:
-        copy.start()
     divisor = cntp_ref[...].T
-    halo = halo_ref[...]
+    summed = own_ref[...] + jnp.dot(near_ref[...], halo_ref[...], preferred_element_type=F32)
 
     def place(b, rows, kind):
         tmp_ref[pl.ds((b // 2) * 4 + kind * 2 + b % 2, parts, stride=2 * groups), :] = rows
 
-    act_copy.wait()
     for b in range(groups):
-        place(b, actp_ref[b * parts : (b + 1) * parts, :].astype(F32), 0)
-    own_copy.wait()
-    for i, copy in enumerate(copies):
-        copy.wait()
-        rows = slice(i * step, (i + 1) * step)
-        summed = own_ref[rows, :] + jnp.dot(near_ref[rows, :], halo, preferred_element_type=F32)
-        for j in range(step // parts):
-            b = i * (step // parts) + j
-            mean = summed[j * parts : (j + 1) * parts] / divisor[:, b : b + 1]
-            place(b, mean.astype(BF).astype(F32), 1)
+        rows = slice(b * parts, (b + 1) * parts)
+        place(b, actp_ref[rows, :].astype(F32), 0)
+        mean = summed[rows] / divisor[:, b : b + 1]
+        place(b, mean.astype(BF).astype(F32), 1)
     out_ref[...] = tmp_ref[...].astype(BF)
 
 
 def decode_kernel(
-    recv_ref, self_ref, near_ref, pair_ref, wout_ref, slots_ref, label_ref,
-    loss_ref, out_ref, tmp_ref, back_ref,
+    recv_ref, self_in, near_in, pair_in, wout_ref, slots_ref, label_ref,
+    loss_ref, out_ref, tmp_ref, back_ref, self_ref, near_ref, pair_ref, sems,
 ):
     parts = recv_ref.shape[0] // 16
     pairs = slots_ref.shape[1]
     width = self_ref.shape[0]
+    copies = [
+        pltpu.make_async_copy(self_in, self_ref, sems.at[3]),
+        pltpu.make_async_copy(near_in, near_ref, sems.at[4]),
+    ]
+    for i in range(3):
+        rows = pl.ds(i * width, width)
+        copies.append(pltpu.make_async_copy(pair_in.at[rows, :], pair_ref.at[rows, :], sems.at[i]))
+    for copy in copies:
+        copy.start()
     tmp_ref[...] = recv_ref[...].astype(F32)
 
     def rows_of(kind):
@@ -201,9 +175,12 @@
         ]
         return jnp.concatenate(halves, 0).astype(BF)
 
+    own, near = rows_of(0), rows_of(1)
+    copies[0].wait()
+    copies[1].wait()
     embed = (
-        jnp.dot(rows_of(0), self_ref[...], preferred_element_type=F32)
-        + jnp.dot(rows_of(1), near_ref[...], preferred_element_type=F32)
+        jnp.dot(own, self_ref[...], preferred_element_type=F32)
+        + jnp.dot(near, near_ref[...], preferred_element_type=F32)
     ).astype(BF)
     place = lax.broadcasted_iota(jnp.int32, (2 * parts, pairs), 0)
     slot = jnp.where(place < parts, 2 * place, 2 * (place - parts) + 1)
@@ -212,11 +189,12 @@
     left = contract_first(left_pick, embed)
     right = contract_first(right_pick, embed)
     product = (left * right).astype(BF)
-    pre_act = (
-        jnp.dot(left.astype(BF), pair_ref[0:width, :], preferred_element_type=F32)
-        + jnp.dot(right.astype(BF), pair_ref[width : 2 * width, :], preferred_element_type=F32)
-        + jnp.dot(product, pair_ref[2 * width : 3 * width, :], preferred_element_type=F32)
-    )
+    pre_act = jnp.zeros((pairs, pair_ref.shape[1]), F32)
+    for i, feature in enumerate((left.astype(BF), right.astype(BF), product)):
+        copies[2 + i].wait()
+        pre_act = pre_act + jnp.dot(
+            feature, pair_ref[i * width : (i + 1) * width, :], preferred_element_type=F32
+        )
     gate = jax.nn.sigmoid(pre_act)
     wout = wout_ref[...]
     logit = jnp.sum(pre_act * gate * wout, axis=1, keepdims=True)
@@ -269,13 +247,12 @@
     both = ("dom", "sub")
     shape = jax.ShapeDtypeStruct
     vmem = pltpu.VMEM
+    sems = pltpu.SemaphoreType.DMA
     halo_t = jnp.transpose(halo_rows[0])
     push_t = jnp.transpose(push_rows[0], (1, 2, 0)).reshape(subs * cap, doms)
     pushed = doms * subs * cap
     halos = doms * slots
 
-    hbm = pltpu.HBM
-    sems = pltpu.SemaphoreType.DMA
     fetch = ("hbm", "vmem")
     outgoing = call(
         halo_kernel, shape((halos, narrow), BF),
@@ -288,27 +265,18 @@
     near_counts, own_sum, push_act, push_count = call(
         count_kernel,
         (
-            hbm((pushed, halos), BF), hbm((pushed, narrow), F32), hbm((pushed, narrow), BF),
+            shape((pushed, halos), BF), shape((pushed, narrow), F32), shape((pushed, narrow), BF),
             shape((subs * cap, doms), F32),
         ),
-        [
-            vmem((pushed, halos), BF), vmem((pushed, narrow), F32), vmem((pushed, narrow), BF),
-            vmem((pushed, firms), BF), vmem((pushed, firms), BF), vmem((pushed // 16, 512), F32),
-            sems((6,)),
-        ],
+        [vmem((pushed, firms), BF), vmem((pushed, firms), BF), vmem((pushed // 16, 512), F32)],
         10_000_000_000, 4_000_000,
         firm_act, push_t, jnp.transpose(nbr_index), nbr_count.reshape(1, firms),
-        in_specs=[fetch] * 4, out_specs=["hbm"] * 3 + ["vmem"],
+        in_specs=[fetch] * 4,
     )
     message = call(
-        mean_kernel, shape((2 * pushed, narrow), BF),
-        [
-            vmem((2 * pushed, narrow), F32), vmem((pushed, halos), BF), vmem((pushed, narrow), F32),
-            vmem((pushed, narrow), BF), sems((6,)),
-        ],
+        mean_kernel, shape((2 * pushed, narrow), BF), [vmem((2 * pushed, narrow), F32)],
         2 * halos * pushed * narrow, 4_000_000,
         incoming, near_counts, own_sum, push_act, push_count,
-        in_specs=[("vmem",)] + [("hbm",)] * 3 + [("vmem",)],
     )
     arrived = lax.all_to_all(
         message.reshape(doms * subs, 2 * cap, narrow), both, 0, 0, tiled=True
@@ -317,10 +285,14 @@
     pair_loss, back = call(
         decode_kernel,
         (shape((1, pairs), F32), shape((pushed, narrow), BF)),
-        [vmem((2 * pushed, narrow), F32), vmem((pushed, narrow), F32)],
+        [
+            vmem((2 * pushed, narrow), F32), vmem((pushed, narrow), F32), vmem(w_self.shape, BF),
+            vmem(w_nbr.shape, BF), vmem(w_pair.shape, BF), sems((5,)),
+        ],
         1_200_000_000, 5_000_000,
         arrived, w_self, w_nbr, w_pair, w_out.reshape(1, -1), jnp.transpose(pair_slots),
         labels.reshape(1, pairs),
+        in_specs=[("vmem",)] + [("hbm",)] * 3 + [("vmem",)] * 3,
     )
     returned = lax.all_to_all(
         back.reshape(doms * subs, cap, narrow), both, 0, 0, tiled=True

time: 104 us -> 102 us (0.981)
  Pallas kernels: 19.1 us -> 17.9 us
    pallas_call x5, Pallas kernels: 19.1 us -> 17.9 us  [call(): pl.pallas_call(kernel, out_shape=out_shape, scratch_shapes=scratch, **spe...]
  transfers between devices with their start and end apart: 1 -> 1, of which waited for: 1 -> 1; matrix products, arithmetic and copies ran while one was open for 0% -> 0% of each run, Pallas kernels for 9% -> 8%
where the time goes in v4:
time: 102 us
  blocking collectives  59.4 us (58%)
  starting transfers between devices  18.4 us (18%)
  Pallas kernels  17.9 us (18%)
  waiting for transfers between devices  5.85 us (6%)
    all_to_all x1, blocking collectives, per_device(): lax.all_to_all(message.reshape(doms * subs, 2 * cap, narrow), both, 0, 0,...  33.4 us
    all_to_all x1, blocking collectives, per_device(): lax.all_to_all(back.reshape(doms * subs, cap, narrow), both, 0, 0, tiled=...  26 us
    all_to_all x1, starting transfers between devices, per_device(): lax.all_to_all(outgoing.reshape(doms, slots, narrow), 'dom', 0, 0, tiled=...  18.4 us
    pallas_call x5, Pallas kernels, call(): pl.pallas_call(kernel, out_shape=out_shape, scratch_shapes=scratch, **spe...  17.9 us
    all_to_all x1, waiting for transfers between devices, per_device(): lax.all_to_all(outgoing.reshape(doms, slots, narrow), 'dom', 0, 0, tiled=...  5.85 us
  transfers between devices with their start and end apart: 1, of which 1 were waited for; matrix products, arithmetic and copies ran while one was open for 0% of the time, Pallas kernels for 8%

profile of v4, /device:TPU:1, one launch (start us, length us, event | category | flops | bytes accessed | tf_op | source)
XLA Modules:
  0.0 102.2 jit_solution(11656951390923447319)
XLA Ops:
  0.6 2.5 %shard_map.122 = bf16[1024,128]{1,0:T(8,128)(2,1)} custom-call(bf16[1024,128]{1,0:T(8,128)(2,1)} %act_ref.3, s32[8,128]{1,0:T(8,128)} %bitcast.31), custom_call_target="tpu_custom_call" | custom-call | flops 268435456 | bytes 600000 | tf_op jit(solution)/shard_map/pallas_call | solution.py:29
  3.1 18.4 %all-to-all-start = ((bf16[128,8,128]{2,1,0:T(8,128)(2,1)}), bf16[128,8,128]{2,1,0:T(8,128)(2,1)S(1)}, u32[]{:S(2)}, u32[]{:S(2)}) async-start(bf16[128,8,128]{2,1,0:T(8,128)(2,1)} %bitcast.2), calls=%async_computation | async-start | bytes 524288 | tf_op jit(solution)/shard_map/all_to_all | solution.py:262
  21.6 8.3 %shard_map.123 = (bf16[1024,1024]{1,0:T(8,128)(2,1)S(1)}, f32[1024,128]{1,0:T(8,128)S(1)}, bf16[1024,128]{1,0:T(8,128)(2,1)S(1)}, f32[8,128]{1,0:T(8,128)S(1)}) custom-call(bf16[1024,128]{1,0:T(8,128)(2,1)} %act_ref.3, s32[8,128]{1,0:T(8,128)} %bitcast.28, s32[16,1024]{1,0:T(8,128)} %bitcast.30, s32[1,1024]{1,0:T(1,128)} %bitcast.32), custom_call_target="tpu_custom_call" | custom-call | flops 10000000000 | bytes 4000000 | tf_op jit(solution)/shard_map/pallas_call | solution.py:29
  29.9 0.0 copy-start
  29.9 0.0 copy-start.1
  29.9 0.0 copy-start.2
  29.9 5.8 %all-to-all-done = bf16[128,8,128]{2,1,0:T(8,128)(2,1)S(1)} async-done(((bf16[128,8,128]{2,1,0:T(8,128)(2,1)}), bf16[128,8,128]{2,1,0:T(8,128)(2,1)S(1)}, u32[]{:S(2)}, u32[]{:S(2)}) %all-to-all-start) | async-done | bytes 262176 | tf_op jit(solution)/shard_map/all_to_all | solution.py:262
  35.8 1.0 shard_map.124
  36.8 0.0 copy-start.3
  36.8 33.4 %all_to_all.15 = bf16[512,4,128]{2,1,0:T(4,128)(2,1)S(1)} all-to-all(bf16[512,4,128]{2,1,0:T(4,128)(2,1)S(1)} %bitcast.21), channel_id=1, replica_groups=mesh['dom'=128,'sub'=4] {'dom','sub'}, dimensions={0} | all-to-all | bytes 1048576 | tf_op jit(solution)/shard_map/all_to_all | solution.py:281
  70.2 0.0 copy-done
  70.2 0.0 copy-done.1
  70.2 0.0 copy-done.2
  70.2 4.5 %shard_map.125 = (f32[1,128]{1,0:T(1,128)}, bf16[1024,128]{1,0:T(8,128)(2,1)S(1)}) custom-call(bf16[2048,128]{1,0:T(8,128)(2,1)S(1)} %bitcast.20, bf16[512,512]{1,0:T(8,128)(2,1)} %self_in.1, bf16[512,512]{1,0:T(8,128)(2,1)} %near_in.1, bf16[1536,1024]{1,0:T(8,128)(2,1)} %pair_in.1, f32[1,1024]{1,0:T(1,128)S(1)} %bitcast.25, s32[2,128]{1,0:T(2,128)S(1)} %bitcast.26, ...), custom_call_target="tpu_custom_call" | custom-call | flops 1200000000 | bytes 5000000 | tf_op jit(solution)/shard_map/pallas_call | solution.py:29
  74.7 26.0 %all_to_all.16 = bf16[512,2,128]{2,1,0:T(2,128)(2,1)S(1)} all-to-all(bf16[512,2,128]{2,1,0:T(2,128)(2,1)S(1)} %bitcast.23), channel_id=1, replica_groups=mesh['dom'=128,'sub'=4] {'dom','sub'}, dimensions={0} | all-to-all | bytes 524288 | tf_op jit(solution)/shard_map/all_to_all | solution.py:297
  100.7 0.0 copy-done.3
  100.7 1.5 %shard_map.126 = f32[1024,128]{1,0:T(8,128)} custom-call(bf16[1024,128]{1,0:T(8,128)(2,1)S(1)} %bitcast.24, s32[8,128]{1,0:T(8,128)S(1)} %bitcast.29), custom_call_target="tpu_custom_call" | custom-call | flops 268435456 | bytes 1000000 | tf_op jit(solution)/shard_map/pallas_call | solution.py:29
Async XLA Ops:
  3.1 32.7 %all-to-all-start = ((bf16[128,8,128]{2,1,0:T(8,128)(2,1)}), bf16[128,8,128]{2,1,0:T(8,128)(2,1)S(1)}, u32[]{:S(2)}, u32[]{:S(2)}) async-start(bf16[128,8,128]{2,1,0:T(8,128)(2,1)} %bitcast.2), calls=%async_computation | async-start | bytes 524288 | tf_op jit(solution)/shard_map/all_to_all | solution.py:262
  29.9 40.3 %copy-start = (f32[1024]{0:T(1024)S(1)}, f32[1024]{0:T(1024)}, u32[]{:S(2)}) copy-start(f32[1024]{0:T(1024)} %param.18) | copy-start | bytes 12292
  29.9 40.3 %copy-start.1 = (s32[128,2]{0,1:T(2,128)S(1)}, s32[128,2]{0,1:T(2,128)}, u32[]{:S(2)}) copy-start(s32[128,2]{0,1:T(2,128)} %param.20) | copy-start | bytes 3076
  29.9 40.2 %copy-start.2 = (s32[128]{0:T(128)S(1)}, s32[128]{0:T(128)}, u32[]{:S(2)}) copy-start(s32[128]{0:T(128)} %param.21) | copy-start | bytes 1540
  36.8 63.9 %copy-start.3 = (s32[1,128,4,2]{1,3,2,0:T(2,128)S(1)}, s32[1,128,4,2]{1,3,2,0:T(2,128)}, u32[]{:S(2)}) copy-start(s32[1,128,4,2]{1,3,2,0:T(2,128)} %param.19) | copy-start | bytes 12292

commit v5 on v4

--- a/solution.py
+++ b/solution.py
@@ -15,7 +15,7 @@
     return lax.dot_general(a, b, (((0,), (0,)), ((), ())), preferred_element_type=F32)
 
 
-def call(kernel, out_shape, scratch, flops, nbytes, *args, in_specs=None, out_specs=None):
+def call(kernel, out_shape, scratch, flops, nbytes, *args, in_specs=None, out_specs=None, alias=None):
     where = {"hbm": pl.ANY, "vmem": pltpu.VMEM}
     specs = {}
     if in_specs is not None:
@@ -30,6 +30,7 @@
         kernel,
         out_shape=out_shape,
         scratch_shapes=scratch,
+        input_output_aliases=alias or {},
         **specs,
         compiler_params=pltpu.CompilerParams(vmem_limit_bytes=24 * MIB),
         cost_estimate=pl.CostEstimate(flops=flops, bytes_accessed=nbytes, transcendentals=0),
@@ -55,9 +56,13 @@
 
 
 def count_kernel(
-    act_ref, push_ref, nbr_ref, cnt_ref, near_ref, own_ref, actp_ref, cntp_ref,
-    pick_ref, mine_ref, where_ref,
+    act_ref, push_ref, nbr_ref, cnt_ref, *refs
 ):
+    weights, (near_ref, own_ref, actp_ref, cntp_ref), held = refs[:3], refs[3:7], refs[7:10]
+    pick_ref, mine_ref, where_ref, sems = refs[10:]
+    copies = [pltpu.make_async_copy(w, h, sems.at[i]) for i, (w, h) in enumerate(zip(weights, held))]
+    for copy in copies:
+        copy.start()
     groups, parts = push_ref.shape
     firms = act_ref.shape[0]
     degree = nbr_ref.shape[0]
@@ -126,9 +131,12 @@
 
     lax.fori_loop(0, pushed // batch, fill, 0, unroll=4)
     own_ref[...] = jnp.dot(mine_ref[...], act_ref[...], preferred_element_type=F32)
-
-
-def mean_kernel(halo_ref, near_ref, own_ref, actp_ref, cntp_ref, out_ref, tmp_ref):
+    for copy in copies:
+        copy.wait()
+
+
+def mean_kernel(halo_ref, near_ref, own_ref, actp_ref, cntp_ref, *refs):
+    out_ref, tmp_ref = refs[3], refs[7]
     groups, parts = cntp_ref.shape
     divisor = cntp_ref[...].T
     summed = own_ref[...] + jnp.dot(near_ref[...], halo_ref[...], preferred_element_type=F32)
@@ -145,21 +153,12 @@
 
 
 def decode_kernel(
-    recv_ref, self_in, near_in, pair_in, wout_ref, slots_ref, label_ref,
-    loss_ref, out_ref, tmp_ref, back_ref, self_ref, near_ref, pair_ref, sems,
+    recv_ref, self_ref, near_ref, pair_ref, wout_ref, slots_ref, label_ref,
+    loss_ref, out_ref, tmp_ref, back_ref,
 ):
     parts = recv_ref.shape[0] // 16
     pairs = slots_ref.shape[1]
     width = self_ref.shape[0]
-    copies = [
-        pltpu.make_async_copy(self_in, self_ref, sems.at[3]),
-        pltpu.make_async_copy(near_in, near_ref, sems.at[4]),
-    ]
-    for i in range(3):
-        rows = pl.ds(i * width, width)
-        copies.append(pltpu.make_async_copy(pair_in.at[rows, :], pair_ref.at[rows, :], sems.at[i]))
-    for copy in copies:
-        copy.start()
     tmp_ref[...] = recv_ref[...].astype(F32)
 
     def rows_of(kind):
@@ -176,8 +175,6 @@
         return jnp.concatenate(halves, 0).astype(BF)
 
     own, near = rows_of(0), rows_of(1)
-    copies[0].wait()
-    copies[1].wait()
     embed = (
         jnp.dot(own, self_ref[...], preferred_element_type=F32)
         + jnp.dot(near, near_ref[...], preferred_element_type=F32)
@@ -191,7 +188,6 @@
     product = (left * right).astype(BF)
     pre_act = jnp.zeros((pairs, pair_ref.shape[1]), F32)
     for i, feature in enumerate((left.astype(BF), right.astype(BF), product)):
-        copies[2 + i].wait()
         pre_act = pre_act + jnp.dot(
             feature, pair_ref[i * width : (i + 1) * width, :], preferred_element_type=F32
         )
@@ -262,21 +258,28 @@
     incoming = lax.all_to_all(
         outgoing.reshape(doms, slots, narrow), "dom", 0, 0, tiled=True
     ).reshape(halos, narrow)
-    near_counts, own_sum, push_act, push_count = call(
+    weights = (w_self, w_nbr, w_pair)
+    held = tuple(pltpu.HBM(w.shape, w.dtype) for w in weights)
+    near_counts, own_sum, push_act, push_count, *copied = call(
         count_kernel,
         (
             shape((pushed, halos), BF), shape((pushed, narrow), F32), shape((pushed, narrow), BF),
-            shape((subs * cap, doms), F32),
+            shape((subs * cap, doms), F32), *held,
         ),
-        [vmem((pushed, firms), BF), vmem((pushed, firms), BF), vmem((pushed // 16, 512), F32)],
+        [
+            vmem((pushed, firms), BF), vmem((pushed, firms), BF), vmem((pushed // 16, 512), F32),
+            sems((3,)),
+        ],
         10_000_000_000, 4_000_000,
         firm_act, push_t, jnp.transpose(nbr_index), nbr_count.reshape(1, firms),
-        in_specs=[fetch] * 4,
-    )
-    message = call(
-        mean_kernel, shape((2 * pushed, narrow), BF), [vmem((2 * pushed, narrow), F32)],
+        *weights, in_specs=[fetch] * 4 + [("hbm",)] * 3, out_specs=["vmem"] * 4 + ["hbm"] * 3,
+    )
+    message, w_self, w_nbr, w_pair = call(
+        mean_kernel, (shape((2 * pushed, narrow), BF), *held), [vmem((2 * pushed, narrow), F32)],
         2 * halos * pushed * narrow, 4_000_000,
-        incoming, near_counts, own_sum, push_act, push_count,
+        incoming, near_counts, own_sum, push_act, push_count, *copied,
+        in_specs=[("vmem",)] * 5 + [("hbm",)] * 3, out_specs=["vmem"] + ["hbm"] * 3,
+        alias={5: 1, 6: 2, 7: 3},
     )
     arrived = lax.all_to_all(
         message.reshape(doms * subs, 2 * cap, narrow), both, 0, 0, tiled=True
@@ -285,14 +288,10 @@
     pair_loss, back = call(
         decode_kernel,
         (shape((1, pairs), F32), shape((pushed, narrow), BF)),
-        [
-            vmem((2 * pushed, narrow), F32), vmem((pushed, narrow), F32), vmem(w_self.shape, BF),
-            vmem(w_nbr.shape, BF), vmem(w_pair.shape, BF), sems((5,)),
-        ],
+        [vmem((2 * pushed, narrow), F32), vmem((pushed, narrow), F32)],
         1_200_000_000, 5_000_000,
         arrived, w_self, w_nbr, w_pair, w_out.reshape(1, -1), jnp.transpose(pair_slots),
         labels.reshape(1, pairs),
-        in_specs=[("vmem",)] + [("hbm",)] * 3 + [("vmem",)] * 3,
     )
     returned = lax.all_to_all(
         back.reshape(doms * subs, cap, narrow), both, 0, 0, tiled=True

time: 102 us -> 226 us (2.22)
  Pallas kernels: 17.9 us -> 137 us
  waiting for transfers between devices: 5.85 us -> 0.01 us
  blocking collectives: 59.4 us -> 65.2 us
  local copies, waits for them, and re-layouts: 0.03 us -> 3.99 us
    pallas_call x5, Pallas kernels: 17.9 us -> 137 us  [call(): pl.pallas_call(kernel, out_shape=out_shape, scratch_shapes=scratch, input...]
    all_to_all x1, waiting for transfers between devices: 5.85 us -> 0.01 us  [per_device(): lax.all_to_all(outgoing.reshape(doms, slots, narrow), 'dom', 0, 0, tiled=...]
    all_to_all x1, blocking collectives: 33.4 us -> 39.2 us  [per_device(): lax.all_to_all(message.reshape(doms * subs, 2 * cap, narrow), both, 0, 0,...]
    unnamed x8 -> x14, local copies, waits for them, and re-layouts: 0.03 us -> 3.99 us
  transfers between devices with their start and end apart: 1 -> 1, of which waited for: 1 -> 0; matrix products, arithmetic and copies ran while one was open for 0% -> 0% of each run, Pallas kernels for 8% -> 57%
where the time goes in v5:
time: 226 us
  Pallas kernels  137 us (61%)
  blocking collectives  65.2 us (29%)
  starting transfers between devices  18.4 us (8%)
  local copies, waits for them, and re-layouts  3.99 us (2%)
    pallas_call x5, Pallas kernels, call(): pl.pallas_call(kernel, out_shape=out_shape, scratch_shapes=scratch, input...  137 us
    all_to_all x1, blocking collectives, per_device(): lax.all_to_all(message.reshape(doms * subs, 2 * cap, narrow), both, 0, 0,...  39.2 us
    all_to_all x1, blocking collectives, per_device(): lax.all_to_all(back.reshape(doms * subs, cap, narrow), both, 0, 0, tiled=...  26 us
    all_to_all x1, starting transfers between devices, per_device(): lax.all_to_all(outgoing.reshape(doms, slots, narrow), 'dom', 0, 0, tiled=...  18.4 us
  transfers between devices with their start and end apart: 1, of which 0 were waited for; matrix products, arithmetic and copies ran while one was open for 0% of the time, Pallas kernels for 57%

profile of v5, /device:TPU:1, one launch (start us, length us, event | category | flops | bytes accessed | tf_op | source)
XLA Modules:
  0.0 225.6 jit_solution(13825007565195672402)
XLA Ops:
  0.6 2.5 %shard_map.122 = bf16[1024,128]{1,0:T(8,128)(2,1)} custom-call(bf16[1024,128]{1,0:T(8,128)(2,1)} %act_ref.3, s32[8,128]{1,0:T(8,128)} %bitcast.31), custom_call_target="tpu_custom_call" | custom-call | flops 268435456 | bytes 600000 | tf_op jit(solution)/shard_map/pallas_call | solution.py:29
  3.1 18.4 %all-to-all-start = ((bf16[128,8,128]{2,1,0:T(8,128)(2,1)}), bf16[128,8,128]{2,1,0:T(8,128)(2,1)S(1)}, u32[]{:S(2)}, u32[]{:S(2)}) async-start(bf16[128,8,128]{2,1,0:T(8,128)(2,1)} %bitcast.2), calls=%async_computation | async-start | bytes 524288 | tf_op jit(solution)/shard_map/all_to_all | solution.py:258
  21.6 129.2 %shard_map.123 = (bf16[1024,1024]{1,0:T(8,128)(2,1)S(1)}, f32[1024,128]{1,0:T(8,128)S(1)}, bf16[1024,128]{1,0:T(8,128)(2,1)S(1)}, f32[8,128]{1,0:T(8,128)S(1)}, ...) custom-call(bf16[1024,128]{1,0:T(8,128)(2,1)} %act_ref.3, s32[8,128]{1,0:T(8,128)} %bitcast.28, ...), custom_call_target="tpu_custom_call" | custom-call | flops 10000000000 | bytes 4000000 | tf_op jit(solution)/shard_map/pallas_call | solution.py:29
  150.7 0.0 all-to-all-done
  150.7 0.0 copy-start.3
  150.8 0.0 copy-start.4
  150.8 0.0 copy-start.5
  150.8 1.0 shard_map.124
  151.8 0.0 copy-start.6
  151.8 39.2 %all_to_all.15 = bf16[512,4,128]{2,1,0:T(4,128)(2,1)S(1)} all-to-all(bf16[512,4,128]{2,1,0:T(4,128)(2,1)S(1)} %bitcast.22), channel_id=1, replica_groups=mesh['dom'=128,'sub'=4] {'dom','sub'}, dimensions={0} | all-to-all | bytes 1048576 | tf_op jit(solution)/shard_map/all_to_all | solution.py:284
  191.0 0.0 copy-done.3
  191.0 0.0 copy-done.4
  191.0 0.0 copy-done.5
  191.0 0.0 copy-start
  191.0 1.9 copy-done
  192.9 0.0 copy-start.1
  192.9 1.0 copy-done.1
  193.9 0.0 copy-start.2
  193.9 1.0 copy-done.2
  195.0 3.1 %shard_map.125 = (f32[1,128]{1,0:T(1,128)}, bf16[1024,128]{1,0:T(8,128)(2,1)S(1)}) custom-call(bf16[2048,128]{1,0:T(8,128)(2,1)S(1)} %bitcast.20, bf16[512,512]{1,0:T(8,128)(2,1)S(1)} %copy-done.1, bf16[512,512]{1,0:T(8,128)(2,1)S(1)} %copy-done.2, bf16[1536,1024]{1,0:T(8,128)(2,1)S(1)} %copy-done, f32[1,1024]{1,0:T(1,128)S(1)} %bitcast.25, ...), custom_call_target="tpu_custom_call" | custom-call | flops 1200000000 | bytes 5000000 | tf_op jit(solution)/shard_map/pallas_call | solution.py:29
  198.1 26.0 %all_to_all.16 = bf16[512,2,128]{2,1,0:T(2,128)(2,1)S(1)} all-to-all(bf16[512,2,128]{2,1,0:T(2,128)(2,1)S(1)} %bitcast.23), channel_id=1, replica_groups=mesh['dom'=128,'sub'=4] {'dom','sub'}, dimensions={0} | all-to-all | bytes 524288 | tf_op jit(solution)/shard_map/all_to_all | solution.py:296
  224.1 0.0 copy-done.6
  224.1 1.5 shard_map.126
Async XLA Ops:
  3.1 147.6 %all-to-all-start = ((bf16[128,8,128]{2,1,0:T(8,128)(2,1)}), bf16[128,8,128]{2,1,0:T(8,128)(2,1)S(1)}, u32[]{:S(2)}, u32[]{:S(2)}) async-start(bf16[128,8,128]{2,1,0:T(8,128)(2,1)} %bitcast.2), calls=%async_computation | async-start | bytes 524288 | tf_op jit(solution)/shard_map/all_to_all | solution.py:258
  150.7 40.3 %copy-start.3 = (f32[1024]{0:T(1024)S(1)}, f32[1024]{0:T(1024)}, u32[]{:S(2)}) copy-start(f32[1024]{0:T(1024)} %param.18) | copy-start | bytes 12292
  150.8 40.2 %copy-start.4 = (s32[128,2]{0,1:T(2,128)S(1)}, s32[128,2]{0,1:T(2,128)}, u32[]{:S(2)}) copy-start(s32[128,2]{0,1:T(2,128)} %param.20) | copy-start | bytes 3076
  150.8 40.2 %copy-start.5 = (s32[128]{0:T(128)S(1)}, s32[128]{0:T(128)}, u32[]{:S(2)}) copy-start(s32[128]{0:T(128)} %param.21) | copy-start | bytes 1540
  151.8 72.3 %copy-start.6 = (s32[1,128,4,2]{1,3,2,0:T(2,128)S(1)}, s32[1,128,4,2]{1,3,2,0:T(2,128)}, u32[]{:S(2)}) copy-start(s32[1,128,4,2]{1,3,2,0:T(2,128)} %param.19) | copy-start | bytes 12292
  191.0 1.9 copy-start
  192.9 1.0 copy-start.1
  193.9 1.0 copy-start.2

commit v6 on v4

--- a/solution.py
+++ b/solution.py
@@ -26,6 +26,8 @@
         specs["in_specs"] = [pl.BlockSpec(memory_space=where[w[-1]]) for w in in_specs]
     if out_specs is not None:
         specs["out_specs"] = [pl.BlockSpec(memory_space=where[w]) for w in out_specs]
+        if len(out_specs) == 1:
+            specs["out_specs"] = specs["out_specs"][0]
     return pl.pallas_call(
         kernel,
         out_shape=out_shape,
@@ -128,7 +130,17 @@
     own_ref[...] = jnp.dot(mine_ref[...], act_ref[...], preferred_element_type=F32)
 
 
-def mean_kernel(halo_ref, near_ref, own_ref, actp_ref, cntp_ref, out_ref, tmp_ref):
+def mean_kernel(
+    halo_ref, near_ref, own_ref, actp_ref, cntp_ref, self_in, nbr_in, pair_in,
+    out_ref, self_ref, nbr_ref, pair_ref, tmp_ref, sems,
+):
+    copies = [
+        pltpu.make_async_copy(self_in, self_ref, sems.at[0]),
+        pltpu.make_async_copy(nbr_in, nbr_ref, sems.at[1]),
+        pltpu.make_async_copy(pair_in.at[pl.ds(0, pair_ref.shape[0]), :], pair_ref, sems.at[2]),
+    ]
+    for copy in copies:
+        copy.start()
     groups, parts = cntp_ref.shape
     divisor = cntp_ref[...].T
     summed = own_ref[...] + jnp.dot(near_ref[...], halo_ref[...], preferred_element_type=F32)
@@ -142,24 +154,26 @@
         mean = summed[rows] / divisor[:, b : b + 1]
         place(b, mean.astype(BF).astype(F32), 1)
     out_ref[...] = tmp_ref[...].astype(BF)
+    for copy in copies:
+        copy.wait()
 
 
 def decode_kernel(
-    recv_ref, self_in, near_in, pair_in, wout_ref, slots_ref, label_ref,
-    loss_ref, out_ref, tmp_ref, back_ref, self_ref, near_ref, pair_ref, sems,
+    recv_ref, self_ref, near_ref, first_ref, pair_in, wout_ref, slots_ref, label_ref,
+    loss_ref, out_ref, tmp_ref, back_ref, rest_ref, sems,
 ):
     parts = recv_ref.shape[0] // 16
     pairs = slots_ref.shape[1]
     width = self_ref.shape[0]
-    copies = [
-        pltpu.make_async_copy(self_in, self_ref, sems.at[3]),
-        pltpu.make_async_copy(near_in, near_ref, sems.at[4]),
-    ]
-    for i in range(3):
+    copies = []
+    for i in range(2):
         rows = pl.ds(i * width, width)
-        copies.append(pltpu.make_async_copy(pair_in.at[rows, :], pair_ref.at[rows, :], sems.at[i]))
-    for copy in copies:
-        copy.start()
+        copies.append(
+            pltpu.make_async_copy(
+                pair_in.at[pl.ds((i + 1) * width, width), :], rest_ref.at[rows, :], sems.at[i]
+            )
+        )
+        copies[-1].start()
     tmp_ref[...] = recv_ref[...].astype(F32)
 
     def rows_of(kind):
@@ -176,8 +190,6 @@
         return jnp.concatenate(halves, 0).astype(BF)
 
     own, near = rows_of(0), rows_of(1)
-    copies[0].wait()
-    copies[1].wait()
     embed = (
         jnp.dot(own, self_ref[...], preferred_element_type=F32)
         + jnp.dot(near, near_ref[...], preferred_element_type=F32)
@@ -189,11 +201,11 @@
     left = contract_first(left_pick, embed)
     right = contract_first(right_pick, embed)
     product = (left * right).astype(BF)
-    pre_act = jnp.zeros((pairs, pair_ref.shape[1]), F32)
-    for i, feature in enumerate((left.astype(BF), right.astype(BF), product)):
-        copies[2 + i].wait()
+    pre_act = jnp.dot(left.astype(BF), first_ref[...], preferred_element_type=F32)
+    for i, feature in enumerate((right.astype(BF), product)):
+        copies[i].wait()
         pre_act = pre_act + jnp.dot(
-            feature, pair_ref[i * width : (i + 1) * width, :], preferred_element_type=F32
+            feature, rest_ref[i * width : (i + 1) * width, :], preferred_element_type=F32
         )
     gate = jax.nn.sigmoid(pre_act)
     wout = wout_ref[...]
@@ -203,12 +215,16 @@
     loss_ref[...] = jnp.broadcast_to(loss, (pairs, pairs)).T[0:1, :]
     outer = jax.nn.sigmoid(logit) - target
     pre_grad = (outer * wout * gate * (1.0 + pre_act * (1.0 - gate))).astype(BF)
-    feat = lax.dot_general(
-        pre_grad, pair_ref[...], (((1,), (1,)), ((), ())), preferred_element_type=F32
-    )
-    third = feat[:, 2 * width :]
-    left_grad = (feat[:, :width] + third * right).astype(BF)
-    right_grad = (feat[:, width : 2 * width] + third * left).astype(BF)
+
+    def back_through(weights):
+        return lax.dot_general(
+            pre_grad, weights, (((1,), (1,)), ((), ())), preferred_element_type=F32
+        )
+
+    feat = back_through(rest_ref[...])
+    third = feat[:, width:]
+    left_grad = (back_through(first_ref[...]) + third * right).astype(BF)
+    right_grad = (feat[:, :width] + third * left).astype(BF)
     back = jnp.dot(left_pick, left_grad, preferred_element_type=F32) + jnp.dot(
         right_pick, right_grad, preferred_element_type=F32
     )
@@ -273,10 +289,14 @@
         firm_act, push_t, jnp.transpose(nbr_index), nbr_count.reshape(1, firms),
         in_specs=[fetch] * 4,
     )
-    message = call(
-        mean_kernel, shape((2 * pushed, narrow), BF), [vmem((2 * pushed, narrow), F32)],
+    first = shape((w_self.shape[1], w_pair.shape[1]), BF)
+    message, self_here, nbr_here, first_here = call(
+        mean_kernel,
+        (shape((2 * pushed, narrow), BF), shape(w_self.shape, BF), shape(w_nbr.shape, BF), first),
+        [vmem((2 * pushed, narrow), F32), sems((3,))],
         2 * halos * pushed * narrow, 4_000_000,
-        incoming, near_counts, own_sum, push_act, push_count,
+        incoming, near_counts, own_sum, push_act, push_count, w_self, w_nbr, w_pair,
+        in_specs=[("vmem",)] * 5 + [("hbm",)] * 3,
     )
     arrived = lax.all_to_all(
         message.reshape(doms * subs, 2 * cap, narrow), both, 0, 0, tiled=True
@@ -286,13 +306,13 @@
         decode_kernel,
         (shape((1, pairs), F32), shape((pushed, narrow), BF)),
         [
-            vmem((2 * pushed, narrow), F32), vmem((pushed, narrow), F32), vmem(w_self.shape, BF),
-            vmem(w_nbr.shape, BF), vmem(w_pair.shape, BF), sems((5,)),
+            vmem((2 * pushed, narrow), F32), vmem((pushed, narrow), F32),
+            vmem((w_pair.shape[0] - first.shape[0], w_pair.shape[1]), BF), sems((2,)),
         ],
         1_200_000_000, 5_000_000,
-        arrived, w_self, w_nbr, w_pair, w_out.reshape(1, -1), jnp.transpose(pair_slots),
+        arrived, self_here, nbr_here, first_here, w_pair, w_out.reshape(1, -1), jnp.transpose(pair_slots),
         labels.reshape(1, pairs),
-        in_specs=[("vmem",)] + [("hbm",)] * 3 + [("vmem",)] * 3,
+        in_specs=[("vmem",)] * 4 + [("hbm",)] + [("vmem",)] * 3,
     )
     returned = lax.all_to_all(
         back.reshape(doms * subs, cap, narrow), both, 0, 0, tiled=True

time: 102 us -> 103 us (level)
  no operation moved by 1% of the time
where the time goes in v6:
time: 103 us
  blocking collectives  59.3 us (58%)
  starting transfers between devices  18.4 us (18%)
  Pallas kernels  18.2 us (18%)
  waiting for transfers between devices  5.88 us (6%)
    all_to_all x1, blocking collectives, per_device(): lax.all_to_all(message.reshape(doms * subs, 2 * cap, narrow), both, 0, 0,...  33.3 us
    all_to_all x1, blocking collectives, per_device(): lax.all_to_all(back.reshape(doms * subs, cap, narrow), both, 0, 0, tiled=...  26 us
    all_to_all x1, starting transfers between devices, per_device(): lax.all_to_all(outgoing.reshape(doms, slots, narrow), 'dom', 0, 0, tiled=...  18.4 us
    pallas_call x5, Pallas kernels, call(): pl.pallas_call(kernel, out_shape=out_shape, scratch_shapes=scratch, **spe...  18.2 us
    all_to_all x1, waiting for transfers between devices, per_device(): lax.all_to_all(outgoing.reshape(doms, slots, narrow), 'dom', 0, 0, tiled=...  5.88 us
  transfers between devices with their start and end apart: 1, of which 1 were waited for; matrix products, arithmetic and copies ran while one was open for 0% of the time, Pallas kernels for 8%

profile of v6, /device:TPU:1, one launch (start us, length us, event | category | flops | bytes accessed | tf_op | source)
XLA Modules:
  0.0 102.5 jit_solution(18207254023404532799)
XLA Ops:
  0.6 2.5 %shard_map.122 = bf16[1024,128]{1,0:T(8,128)(2,1)} custom-call(bf16[1024,128]{1,0:T(8,128)(2,1)} %act_ref.3, s32[8,128]{1,0:T(8,128)} %bitcast.31), custom_call_target="tpu_custom_call" | custom-call | flops 268435456 | bytes 600000 | tf_op jit(solution)/shard_map/pallas_call | solution.py:31
  3.1 18.4 %all-to-all-start = ((bf16[128,8,128]{2,1,0:T(8,128)(2,1)}), bf16[128,8,128]{2,1,0:T(8,128)(2,1)S(1)}, u32[]{:S(2)}, u32[]{:S(2)}) async-start(bf16[128,8,128]{2,1,0:T(8,128)(2,1)} %bitcast.2), calls=%async_computation | async-start | bytes 524288 | tf_op jit(solution)/shard_map/all_to_all | solution.py:278
  21.6 8.3 %shard_map.123 = (bf16[1024,1024]{1,0:T(8,128)(2,1)S(1)}, f32[1024,128]{1,0:T(8,128)S(1)}, bf16[1024,128]{1,0:T(8,128)(2,1)S(1)}, f32[8,128]{1,0:T(8,128)S(1)}) custom-call(bf16[1024,128]{1,0:T(8,128)(2,1)} %act_ref.3, s32[8,128]{1,0:T(8,128)} %bitcast.28, s32[16,1024]{1,0:T(8,128)} %bitcast.30, s32[1,1024]{1,0:T(1,128)} %bitcast.32), custom_call_target="tpu_custom_call" | custom-call | flops 10000000000 | bytes 4000000 | tf_op jit(solution)/shard_map/pallas_call | solution.py:31
  29.9 5.9 %all-to-all-done = bf16[128,8,128]{2,1,0:T(8,128)(2,1)S(1)} async-done(((bf16[128,8,128]{2,1,0:T(8,128)(2,1)}), bf16[128,8,128]{2,1,0:T(8,128)(2,1)S(1)}, u32[]{:S(2)}, u32[]{:S(2)}) %all-to-all-start) | async-done | bytes 262176 | tf_op jit(solution)/shard_map/all_to_all | solution.py:278
  35.8 0.0 copy-start
  35.8 0.0 copy-start.1
  35.8 0.0 copy-start.2
  35.8 1.6 %shard_map.124 = (bf16[2048,128]{1,0:T(8,128)(2,1)S(1)}, bf16[512,512]{1,0:T(8,128)(2,1)S(1)}, bf16[512,512]{1,0:T(8,128)(2,1)S(1)}, bf16[512,1024]{1,0:T(8,128)(2,1)S(1)}) custom-call(bf16[1024,128]{1,0:T(8,128)(2,1)S(1)} %bitcast.21, bf16[1024,1024]{1,0:T(8,128)(2,1)S(1)} %get-tuple-element.12.near_ref, f32[1024,128]{1,0:T(8,128)S(1)} %get-tuple-element.13.own_ref, ...), custom_call_target="tpu_custom_call" | custom-call | flops 268435456 | bytes 4000000 | tf_op jit(solution)/shard_map/pallas_call | solution.py:31
  37.4 33.3 %all_to_all.15 = bf16[512,4,128]{2,1,0:T(4,128)(2,1)S(1)} all-to-all(bf16[512,4,128]{2,1,0:T(4,128)(2,1)S(1)} %bitcast.22), channel_id=1, replica_groups=mesh['dom'=128,'sub'=4] {'dom','sub'}, dimensions={0} | all-to-all | bytes 1048576 | tf_op jit(solution)/shard_map/all_to_all | solution.py:301
  70.8 0.0 copy-done
  70.8 0.0 copy-done.1
  70.8 0.0 copy-done.2
  70.8 0.0 copy-start.3
  70.8 4.2 %shard_map.125 = (f32[1,128]{1,0:T(1,128)}, bf16[1024,128]{1,0:T(8,128)(2,1)S(1)}) custom-call(bf16[2048,128]{1,0:T(8,128)(2,1)S(1)} %bitcast.20, bf16[512,512]{1,0:T(8,128)(2,1)S(1)} %get-tuple-element.17.self_ref, bf16[512,512]{1,0:T(8,128)(2,1)S(1)} %get-tuple-element.18.near_ref, bf16[512,1024]{1,0:T(8,128)(2,1)S(1)} %get-tuple-element.19.first_ref, ...), custom_call_target="tpu_custom_call" | custom-call | flops 1200000000 | bytes 5000000 | tf_op jit(solution)/shard_map/pallas_call | solution.py:31
  75.0 26.0 %all_to_all.16 = bf16[512,2,128]{2,1,0:T(2,128)(2,1)S(1)} all-to-all(bf16[512,2,128]{2,1,0:T(2,128)(2,1)S(1)} %bitcast.23), channel_id=1, replica_groups=mesh['dom'=128,'sub'=4] {'dom','sub'}, dimensions={0} | all-to-all | bytes 524288 | tf_op jit(solution)/shard_map/all_to_all | solution.py:317
  101.0 0.0 copy-done.3
  101.0 1.5 %shard_map.126 = f32[1024,128]{1,0:T(8,128)} custom-call(bf16[1024,128]{1,0:T(8,128)(2,1)S(1)} %bitcast.24, s32[8,128]{1,0:T(8,128)S(1)} %bitcast.29), custom_call_target="tpu_custom_call" | custom-call | flops 268435456 | bytes 1000000 | tf_op jit(solution)/shard_map/pallas_call | solution.py:31
Async XLA Ops:
  3.1 32.7 %all-to-all-start = ((bf16[128,8,128]{2,1,0:T(8,128)(2,1)}), bf16[128,8,128]{2,1,0:T(8,128)(2,1)S(1)}, u32[]{:S(2)}, u32[]{:S(2)}) async-start(bf16[128,8,128]{2,1,0:T(8,128)(2,1)} %bitcast.2), calls=%async_computation | async-start | bytes 524288 | tf_op jit(solution)/shard_map/all_to_all | solution.py:278
  35.8 35.0 %copy-start = (f32[1024]{0:T(1024)S(1)}, f32[1024]{0:T(1024)}, u32[]{:S(2)}) copy-start(f32[1024]{0:T(1024)} %param.18) | copy-start | bytes 12292
  35.8 35.0 %copy-start.1 = (s32[128,2]{0,1:T(2,128)S(1)}, s32[128,2]{0,1:T(2,128)}, u32[]{:S(2)}) copy-start(s32[128,2]{0,1:T(2,128)} %param.20) | copy-start | bytes 3076
  35.8 35.0 %copy-start.2 = (s32[128]{0:T(128)S(1)}, s32[128]{0:T(128)}, u32[]{:S(2)}) copy-start(s32[128]{0:T(128)} %param.21) | copy-start | bytes 1540
  70.8 30.2 %copy-start.3 = (s32[1,128,4,2]{1,3,2,0:T(2,128)S(1)}, s32[1,128,4,2]{1,3,2,0:T(2,128)}, u32[]{:S(2)}) copy-start(s32[1,128,4,2]{1,3,2,0:T(2,128)} %param.19) | copy-start | bytes 12292

commit v7 on v4

--- a/solution.py
+++ b/solution.py
@@ -145,21 +145,12 @@
 
 
 def decode_kernel(
-    recv_ref, self_in, near_in, pair_in, wout_ref, slots_ref, label_ref,
-    loss_ref, out_ref, tmp_ref, back_ref, self_ref, near_ref, pair_ref, sems,
+    recv_ref, self_ref, near_ref, pair_ref, wout_ref, slots_ref, label_ref,
+    loss_ref, out_ref, tmp_ref, back_ref,
 ):
     parts = recv_ref.shape[0] // 16
     pairs = slots_ref.shape[1]
     width = self_ref.shape[0]
-    copies = [
-        pltpu.make_async_copy(self_in, self_ref, sems.at[3]),
-        pltpu.make_async_copy(near_in, near_ref, sems.at[4]),
-    ]
-    for i in range(3):
-        rows = pl.ds(i * width, width)
-        copies.append(pltpu.make_async_copy(pair_in.at[rows, :], pair_ref.at[rows, :], sems.at[i]))
-    for copy in copies:
-        copy.start()
     tmp_ref[...] = recv_ref[...].astype(F32)
 
     def rows_of(kind):
@@ -175,12 +166,9 @@
         ]
         return jnp.concatenate(halves, 0).astype(BF)
 
-    own, near = rows_of(0), rows_of(1)
-    copies[0].wait()
-    copies[1].wait()
     embed = (
-        jnp.dot(own, self_ref[...], preferred_element_type=F32)
-        + jnp.dot(near, near_ref[...], preferred_element_type=F32)
+        jnp.dot(rows_of(0), self_ref[...], preferred_element_type=F32)
+        + jnp.dot(rows_of(1), near_ref[...], preferred_element_type=F32)
     ).astype(BF)
     place = lax.broadcasted_iota(jnp.int32, (2 * parts, pairs), 0)
     slot = jnp.where(place < parts, 2 * place, 2 * (place - parts) + 1)
@@ -189,12 +177,11 @@
     left = contract_first(left_pick, embed)
     right = contract_first(right_pick, embed)
     product = (left * right).astype(BF)
-    pre_act = jnp.zeros((pairs, pair_ref.shape[1]), F32)
-    for i, feature in enumerate((left.astype(BF), right.astype(BF), product)):
-        copies[2 + i].wait()
-        pre_act = pre_act + jnp.dot(
-            feature, pair_ref[i * width : (i + 1) * width, :], preferred_element_type=F32
-        )
+    pre_act = (
+        jnp.dot(left.astype(BF), pair_ref[0:width, :], preferred_element_type=F32)
+        + jnp.dot(right.astype(BF), pair_ref[width : 2 * width, :], preferred_element_type=F32)
+        + jnp.dot(product, pair_ref[2 * width : 3 * width, :], preferred_element_type=F32)
+    )
     gate = jax.nn.sigmoid(pre_act)
     wout = wout_ref[...]
     logit = jnp.sum(pre_act * gate * wout, axis=1, keepdims=True)
@@ -247,7 +234,6 @@
     both = ("dom", "sub")
     shape = jax.ShapeDtypeStruct
     vmem = pltpu.VMEM
-    sems = pltpu.SemaphoreType.DMA
     halo_t = jnp.transpose(halo_rows[0])
     push_t = jnp.transpose(push_rows[0], (1, 2, 0)).reshape(subs * cap, doms)
     pushed = doms * subs * cap
@@ -285,14 +271,10 @@
     pair_loss, back = call(
         decode_kernel,
         (shape((1, pairs), F32), shape((pushed, narrow), BF)),
-        [
-            vmem((2 * pushed, narrow), F32), vmem((pushed, narrow), F32), vmem(w_self.shape, BF),
-            vmem(w_nbr.shape, BF), vmem(w_pair.shape, BF), sems((5,)),
-        ],
-        1_200_000_000, 5_000_000,
+        [vmem((2 * pushed, narrow), F32), vmem((pushed, narrow), F32)],
+        5_000_000_000, 5_000_000,
         arrived, w_self, w_nbr, w_pair, w_out.reshape(1, -1), jnp.transpose(pair_slots),
         labels.reshape(1, pairs),
-        in_specs=[("vmem",)] + [("hbm",)] * 3 + [("vmem",)] * 3,
     )
     returned = lax.all_to_all(
         back.reshape(doms * subs, cap, narrow), both, 0, 0, tiled=True

time: 102 us -> 101 us (level)
  Pallas kernels: 17.9 us -> 16.5 us
    pallas_call x5, Pallas kernels: 17.9 us -> 16.5 us  [call(): pl.pallas_call(kernel, out_shape=out_shape, scratch_shapes=scratch, **spe...]
where the time goes in v7:
time: 101 us
  blocking collectives  59.4 us (59%)
  starting transfers between devices  18.4 us (18%)
  Pallas kernels  16.5 us (16%)
  waiting for transfers between devices  5.85 us (6%)
    all_to_all x1, blocking collectives, per_device(): lax.all_to_all(message.reshape(doms * subs, 2 * cap, narrow), both, 0, 0,...  33.4 us
    all_to_all x1, blocking collectives, per_device(): lax.all_to_all(back.reshape(doms * subs, cap, narrow), both, 0, 0, tiled=...  26 us
    all_to_all x1, starting transfers between devices, per_device(): lax.all_to_all(outgoing.reshape(doms, slots, narrow), 'dom', 0, 0, tiled=...  18.4 us
    pallas_call x5, Pallas kernels, call(): pl.pallas_call(kernel, out_shape=out_shape, scratch_shapes=scratch, **spe...  16.5 us
    all_to_all x1, waiting for transfers between devices, per_device(): lax.all_to_all(outgoing.reshape(doms, slots, narrow), 'dom', 0, 0, tiled=...  5.85 us
  transfers between devices with their start and end apart: 1, of which 1 were waited for; matrix products, arithmetic and copies ran while one was open for 0% of the time, Pallas kernels for 8%

profile of v7, /device:TPU:1, one launch (start us, length us, event | category | flops | bytes accessed | tf_op | source)
XLA Modules:
  0.0 100.9 jit_solution(2156249945727749891)
XLA Ops:
  0.6 2.5 %shard_map.122 = bf16[1024,128]{1,0:T(8,128)(2,1)} custom-call(bf16[1024,128]{1,0:T(8,128)(2,1)} %act_ref.3, s32[8,128]{1,0:T(8,128)} %bitcast.31), custom_call_target="tpu_custom_call" | custom-call | flops 268435456 | bytes 600000 | tf_op jit(solution)/shard_map/pallas_call | solution.py:29
  3.1 18.4 %all-to-all-start = ((bf16[128,8,128]{2,1,0:T(8,128)(2,1)}), bf16[128,8,128]{2,1,0:T(8,128)(2,1)S(1)}, u32[]{:S(2)}, u32[]{:S(2)}) async-start(bf16[128,8,128]{2,1,0:T(8,128)(2,1)} %bitcast.2), calls=%async_computation | async-start | bytes 524288 | tf_op jit(solution)/shard_map/all_to_all | solution.py:248
  21.6 8.3 %shard_map.123 = (bf16[1024,1024]{1,0:T(8,128)(2,1)S(1)}, f32[1024,128]{1,0:T(8,128)S(1)}, bf16[1024,128]{1,0:T(8,128)(2,1)S(1)}, f32[8,128]{1,0:T(8,128)S(1)}) custom-call(bf16[1024,128]{1,0:T(8,128)(2,1)} %act_ref.3, s32[8,128]{1,0:T(8,128)} %bitcast.26, s32[16,1024]{1,0:T(8,128)} %bitcast.30, s32[1,1024]{1,0:T(1,128)} %bitcast.32), custom_call_target="tpu_custom_call" | custom-call | flops 10000000000 | bytes 4000000 | tf_op jit(solution)/shard_map/pallas_call | solution.py:29
  29.9 0.0 copy-start.3
  29.9 0.0 copy-start.5
  29.9 0.0 copy-start.6
  29.9 5.8 %all-to-all-done = bf16[128,8,128]{2,1,0:T(8,128)(2,1)S(1)} async-done(((bf16[128,8,128]{2,1,0:T(8,128)(2,1)}), bf16[128,8,128]{2,1,0:T(8,128)(2,1)S(1)}, u32[]{:S(2)}, u32[]{:S(2)}) %all-to-all-start) | async-done | bytes 262176 | tf_op jit(solution)/shard_map/all_to_all | solution.py:248
  35.8 0.0 copy-start
  35.8 0.0 copy-start.1
  35.8 0.0 copy-start.2
  35.8 1.0 shard_map.124
  36.8 33.4 %all_to_all.15 = bf16[512,4,128]{2,1,0:T(4,128)(2,1)S(1)} all-to-all(bf16[512,4,128]{2,1,0:T(4,128)(2,1)S(1)} %bitcast.20), channel_id=1, replica_groups=mesh['dom'=128,'sub'=4] {'dom','sub'}, dimensions={0} | all-to-all | bytes 1048576 | tf_op jit(solution)/shard_map/all_to_all | solution.py:267
  70.2 0.0 copy-done.3
  70.2 0.0 copy-done.5
  70.2 0.0 copy-done.6
  70.2 0.0 copy-done
  70.2 0.0 copy-done.1
  70.2 0.0 copy-done.2
  70.2 0.0 copy-start.4
  70.2 3.1 %shard_map.125 = (f32[1,128]{1,0:T(1,128)}, bf16[1024,128]{1,0:T(8,128)(2,1)S(1)}) custom-call(bf16[2048,128]{1,0:T(8,128)(2,1)S(1)} %bitcast.22, bf16[512,512]{1,0:T(8,128)(2,1)S(1)} %copy-done.1, bf16[512,512]{1,0:T(8,128)(2,1)S(1)} %copy-done.2, bf16[1536,1024]{1,0:T(8,128)(2,1)S(1)} %copy-done, f32[1,1024]{1,0:T(1,128)S(1)} %bitcast.25, ...), custom_call_target="tpu_custom_call" | custom-call | flops 5000000000 | bytes 5000000 | tf_op jit(solution)/shard_map/pallas_call | solution.py:29
  73.4 26.0 %all_to_all.16 = bf16[512,2,128]{2,1,0:T(2,128)(2,1)S(1)} all-to-all(bf16[512,2,128]{2,1,0:T(2,128)(2,1)S(1)} %bitcast.23), channel_id=1, replica_groups=mesh['dom'=128,'sub'=4] {'dom','sub'}, dimensions={0} | all-to-all | bytes 524288 | tf_op jit(solution)/shard_map/all_to_all | solution.py:279
  99.3 0.0 copy-done.4
  99.3 1.5 %shard_map.126 = f32[1024,128]{1,0:T(8,128)} custom-call(bf16[1024,128]{1,0:T(8,128)(2,1)S(1)} %bitcast.24, s32[8,128]{1,0:T(8,128)S(1)} %bitcast.27), custom_call_target="tpu_custom_call" | custom-call | flops 268435456 | bytes 1000000 | tf_op jit(solution)/shard_map/pallas_call | solution.py:29
Async XLA Ops:
  3.1 32.7 %all-to-all-start = ((bf16[128,8,128]{2,1,0:T(8,128)(2,1)}), bf16[128,8,128]{2,1,0:T(8,128)(2,1)S(1)}, u32[]{:S(2)}, u32[]{:S(2)}) async-start(bf16[128,8,128]{2,1,0:T(8,128)(2,1)} %bitcast.2), calls=%async_computation | async-start | bytes 524288 | tf_op jit(solution)/shard_map/all_to_all | solution.py:248
  29.9 40.3 %copy-start.3 = (f32[1024]{0:T(1024)S(1)}, f32[1024]{0:T(1024)}, u32[]{:S(2)}) copy-start(f32[1024]{0:T(1024)} %param.18) | copy-start | bytes 12292
  29.9 40.3 %copy-start.5 = (s32[128,2]{0,1:T(2,128)S(1)}, s32[128,2]{0,1:T(2,128)}, u32[]{:S(2)}) copy-start(s32[128,2]{0,1:T(2,128)} %param.20) | copy-start | bytes 3076
  29.9 40.3 %copy-start.6 = (s32[128]{0:T(128)S(1)}, s32[128]{0:T(128)}, u32[]{:S(2)}) copy-start(s32[128]{0:T(128)} %param.21) | copy-start | bytes 1540
  35.8 34.4 %copy-start = (bf16[1536,1024]{1,0:T(8,128)(2,1)S(1)}, bf16[1536,1024]{1,0:T(8,128)(2,1)}, u32[]{:S(2)}) copy-start(bf16[1536,1024]{1,0:T(8,128)(2,1)} %pair_ref.1) | copy-start | bytes 9437188
  35.8 34.4 %copy-start.1 = (bf16[512,512]{1,0:T(8,128)(2,1)S(1)}, bf16[512,512]{1,0:T(8,128)(2,1)}, u32[]{:S(2)}) copy-start(bf16[512,512]{1,0:T(8,128)(2,1)} %self_ref.1) | copy-start | bytes 1572868
  35.8 34.4 %copy-start.2 = (bf16[512,512]{1,0:T(8,128)(2,1)S(1)}, bf16[512,512]{1,0:T(8,128)(2,1)}, u32[]{:S(2)}) copy-start(bf16[512,512]{1,0:T(8,128)(2,1)} %near_ref.1) | copy-start | bytes 1572868
  70.2 29.1 %copy-start.4 = (s32[1,128,4,2]{1,3,2,0:T(2,128)S(1)}, s32[1,128,4,2]{1,3,2,0:T(2,128)}, u32[]{:S(2)}) copy-start(s32[1,128,4,2]{1,3,2,0:T(2,128)} %param.19) | copy-start | bytes 12292

commit v8 on v7

--- a/solution.py
+++ b/solution.py
@@ -26,6 +26,8 @@
         specs["in_specs"] = [pl.BlockSpec(memory_space=where[w[-1]]) for w in in_specs]
     if out_specs is not None:
         specs["out_specs"] = [pl.BlockSpec(memory_space=where[w]) for w in out_specs]
+        if len(out_specs) == 1:
+            specs["out_specs"] = specs["out_specs"][0]
     return pl.pallas_call(
         kernel,
         out_shape=out_shape,
@@ -174,8 +176,9 @@
     slot = jnp.where(place < parts, 2 * place, 2 * (place - parts) + 1)
     left_pick = jnp.where(slot == slots_ref[0:1, :], 1.0, 0.0).astype(BF)
     right_pick = jnp.where(slot == slots_ref[1:2, :], 1.0, 0.0).astype(BF)
-    left = contract_first(left_pick, embed)
-    right = contract_first(right_pick, embed)
+    picks = jnp.concatenate([left_pick, right_pick], 1)
+    ends = contract_first(picks, embed)
+    left, right = ends[:pairs], ends[pairs:]
     product = (left * right).astype(BF)
     pre_act = (
         jnp.dot(left.astype(BF), pair_ref[0:width, :], preferred_element_type=F32)
@@ -183,21 +186,26 @@
         + jnp.dot(product, pair_ref[2 * width : 3 * width, :], preferred_element_type=F32)
     )
     gate = jax.nn.sigmoid(pre_act)
+    active = pre_act * gate
     wout = wout_ref[...]
-    logit = jnp.sum(pre_act * gate * wout, axis=1, keepdims=True)
+    logit = jnp.sum(active * wout, axis=1, keepdims=True)
     target = jnp.broadcast_to(label_ref[...].astype(F32), (pairs, pairs)).T[:, 0:1]
     loss = jnp.maximum(logit, 0.0) + jnp.log1p(jnp.exp(-jnp.abs(logit))) - target * logit
     loss_ref[...] = jnp.broadcast_to(loss, (pairs, pairs)).T[0:1, :]
     outer = jax.nn.sigmoid(logit) - target
-    pre_grad = (outer * wout * gate * (1.0 + pre_act * (1.0 - gate))).astype(BF)
-    feat = lax.dot_general(
-        pre_grad, pair_ref[...], (((1,), (1,)), ((), ())), preferred_element_type=F32
-    )
-    third = feat[:, 2 * width :]
-    left_grad = (feat[:, :width] + third * right).astype(BF)
-    right_grad = (feat[:, width : 2 * width] + third * left).astype(BF)
-    back = jnp.dot(left_pick, left_grad, preferred_element_type=F32) + jnp.dot(
-        right_pick, right_grad, preferred_element_type=F32
+    pre_grad = (wout * (gate + active * (1.0 - gate))).astype(BF)
+    feat = [
+        lax.dot_general(
+            pre_grad, pair_ref[i * width : (i + 1) * width, :], (((1,), (1,)), ((), ())),
+            preferred_element_type=F32,
+        )
+        for i in (2, 0, 1)
+    ]
+    third = outer * feat[0]
+    left_grad = (outer * feat[1] + third * right).astype(BF)
+    right_grad = (outer * feat[2] + third * left).astype(BF)
+    back = jnp.dot(
+        picks, jnp.concatenate([left_grad, right_grad], 0), preferred_element_type=F32
     )
     for s in range(4):
         for c in range(2):
@@ -207,21 +215,30 @@
     out_ref[...] = back_ref[...].astype(BF)
 
 
-def owner_kernel(recv_ref, push_ref, out_ref, tmp_ref):
+def owner_kernel(recv_ref, push_ref, out_ref, tmp_ref, sum_ref, sems):
     groups, parts = push_ref.shape
     tmp_ref[...] = recv_ref[...].astype(F32)
     grads = jnp.concatenate(
         [tmp_ref[pl.ds(b, parts, stride=groups), :] for b in range(groups)], 0
     ).astype(BF)
-    firm = lax.broadcasted_iota(jnp.int32, (out_ref.shape[0], parts), 0)
-    pick = jnp.concatenate(
-        [
-            jnp.where(firm == push_ref[b : b + 1, :], 1.0, 0.0).astype(BF)
-            for b in range(groups)
-        ],
-        1,
-    )
-    out_ref[...] = jnp.dot(pick, grads, preferred_element_type=F32)
+    parcels = sems.shape[0]
+    step = sum_ref.shape[0] // parcels
+    firm = lax.broadcasted_iota(jnp.int32, (step, parts), 0)
+    copies = []
+    for p in range(parcels):
+        pick = jnp.concatenate(
+            [
+                jnp.where(firm + p * step == push_ref[b : b + 1, :], 1.0, 0.0).astype(BF)
+                for b in range(groups)
+            ],
+            1,
+        )
+        rows = pl.ds(p * step, step)
+        sum_ref[rows, :] = jnp.dot(pick, grads, preferred_element_type=F32)
+        copies.append(pltpu.make_async_copy(sum_ref.at[rows, :], out_ref.at[rows, :], sems.at[p]))
+        copies[-1].start()
+    for copy in copies:
+        copy.wait()
 
 
 def per_device(
@@ -280,8 +297,10 @@
         back.reshape(doms * subs, cap, narrow), both, 0, 0, tiled=True
     ).reshape(pushed, narrow)
     embed_grad = call(
-        owner_kernel, shape((firms, narrow), F32), [vmem((pushed, narrow), F32)],
+        owner_kernel, pltpu.HBM((firms, narrow), F32),
+        [vmem((pushed, narrow), F32), vmem((firms, narrow), F32), pltpu.SemaphoreType.DMA((4,))],
         2 * pushed * firms * narrow, 1_000_000, returned, push_t,
+        in_specs=[("vmem",)] * 2, out_specs=["hbm"],
     )
     return (pair_loss.reshape(pairs), embed_grad)
 

time: 101 us -> 101 us (level)
  no operation moved by 1% of the time
where the time goes in v8:
time: 101 us
  blocking collectives  59.4 us (59%)
  starting transfers between devices  18.4 us (18%)
  Pallas kernels  16.1 us (16%)
  waiting for transfers between devices  5.85 us (6%)
    all_to_all x1, blocking collectives, per_device(): lax.all_to_all(message.reshape(doms * subs, 2 * cap, narrow), both, 0, 0,...  33.4 us
    all_to_all x1, blocking collectives, per_device(): lax.all_to_all(back.reshape(doms * subs, cap, narrow), both, 0, 0, tiled=...  26 us
    all_to_all x1, starting transfers between devices, per_device(): lax.all_to_all(outgoing.reshape(doms, slots, narrow), 'dom', 0, 0, tiled=...  18.4 us
    pallas_call x5, Pallas kernels, call(): pl.pallas_call(kernel, out_shape=out_shape, scratch_shapes=scratch, **spe...  16.1 us
    all_to_all x1, waiting for transfers between devices, per_device(): lax.all_to_all(outgoing.reshape(doms, slots, narrow), 'dom', 0, 0, tiled=...  5.85 us
  transfers between devices with their start and end apart: 1, of which 1 were waited for; matrix products, arithmetic and copies ran while one was open for 0% of the time, Pallas kernels for 8%

profile of v8, /device:TPU:1, one launch (start us, length us, event | category | flops | bytes accessed | tf_op | source)
XLA Modules:
  0.0 100.7 jit_solution(10823627395627191848)
XLA Ops:
  0.6 2.5 %shard_map.122 = bf16[1024,128]{1,0:T(8,128)(2,1)} custom-call(bf16[1024,128]{1,0:T(8,128)(2,1)} %act_ref.3, s32[8,128]{1,0:T(8,128)} %bitcast.31), custom_call_target="tpu_custom_call" | custom-call | flops 268435456 | bytes 600000 | tf_op jit(solution)/shard_map/pallas_call | solution.py:31
  3.1 18.4 %all-to-all-start = ((bf16[128,8,128]{2,1,0:T(8,128)(2,1)}), bf16[128,8,128]{2,1,0:T(8,128)(2,1)S(1)}, u32[]{:S(2)}, u32[]{:S(2)}) async-start(bf16[128,8,128]{2,1,0:T(8,128)(2,1)} %bitcast.2), calls=%async_computation | async-start | bytes 524288 | tf_op jit(solution)/shard_map/all_to_all | solution.py:265
  21.6 8.3 %shard_map.123 = (bf16[1024,1024]{1,0:T(8,128)(2,1)S(1)}, f32[1024,128]{1,0:T(8,128)S(1)}, bf16[1024,128]{1,0:T(8,128)(2,1)S(1)}, f32[8,128]{1,0:T(8,128)S(1)}) custom-call(bf16[1024,128]{1,0:T(8,128)(2,1)} %act_ref.3, s32[8,128]{1,0:T(8,128)} %bitcast.26, s32[16,1024]{1,0:T(8,128)} %bitcast.30, s32[1,1024]{1,0:T(1,128)} %bitcast.32), custom_call_target="tpu_custom_call" | custom-call | flops 10000000000 | bytes 4000000 | tf_op jit(solution)/shard_map/pallas_call | solution.py:31
  29.9 0.0 copy-start.3
  29.9 0.0 copy-start.5
  29.9 0.0 copy-start.6
  29.9 5.8 %all-to-all-done = bf16[128,8,128]{2,1,0:T(8,128)(2,1)S(1)} async-done(((bf16[128,8,128]{2,1,0:T(8,128)(2,1)}), bf16[128,8,128]{2,1,0:T(8,128)(2,1)S(1)}, u32[]{:S(2)}, u32[]{:S(2)}) %all-to-all-start) | async-done | bytes 262176 | tf_op jit(solution)/shard_map/all_to_all | solution.py:265
  35.8 0.0 copy-start
  35.8 0.0 copy-start.1
  35.8 0.0 copy-start.2
  35.8 1.0 shard_map.124
  36.8 33.4 %all_to_all.15 = bf16[512,4,128]{2,1,0:T(4,128)(2,1)S(1)} all-to-all(bf16[512,4,128]{2,1,0:T(4,128)(2,1)S(1)} %bitcast.20), channel_id=1, replica_groups=mesh['dom'=128,'sub'=4] {'dom','sub'}, dimensions={0} | all-to-all | bytes 1048576 | tf_op jit(solution)/shard_map/all_to_all | solution.py:284
  70.2 0.0 copy-done.3
  70.2 0.0 copy-done.5
  70.2 0.0 copy-done.6
  70.2 0.0 copy-done
  70.2 0.0 copy-done.1
  70.2 0.0 copy-done.2
  70.2 0.0 copy-start.4
  70.2 2.9 %shard_map.125 = (f32[1,128]{1,0:T(1,128)}, bf16[1024,128]{1,0:T(8,128)(2,1)S(1)}) custom-call(bf16[2048,128]{1,0:T(8,128)(2,1)S(1)} %bitcast.22, bf16[512,512]{1,0:T(8,128)(2,1)S(1)} %copy-done.1, bf16[512,512]{1,0:T(8,128)(2,1)S(1)} %copy-done.2, bf16[1536,1024]{1,0:T(8,128)(2,1)S(1)} %copy-done, f32[1,1024]{1,0:T(1,128)S(1)} %bitcast.25, ...), custom_call_target="tpu_custom_call" | custom-call | flops 5000000000 | bytes 5000000 | tf_op jit(solution)/shard_map/pallas_call | solution.py:31
  73.1 26.0 %all_to_all.16 = bf16[512,2,128]{2,1,0:T(2,128)(2,1)S(1)} all-to-all(bf16[512,2,128]{2,1,0:T(2,128)(2,1)S(1)} %bitcast.23), channel_id=1, replica_groups=mesh['dom'=128,'sub'=4] {'dom','sub'}, dimensions={0} | all-to-all | bytes 524288 | tf_op jit(solution)/shard_map/all_to_all | solution.py:296
  99.1 0.0 copy-done.4
  99.1 1.5 %shard_map.126 = f32[1024,128]{1,0:T(8,128)} custom-call(bf16[1024,128]{1,0:T(8,128)(2,1)S(1)} %bitcast.24, s32[8,128]{1,0:T(8,128)S(1)} %bitcast.27), custom_call_target="tpu_custom_call" | custom-call | flops 268435456 | bytes 1000000 | tf_op jit(solution)/shard_map/pallas_call | solution.py:31
Async XLA Ops:
  3.1 32.7 %all-to-all-start = ((bf16[128,8,128]{2,1,0:T(8,128)(2,1)}), bf16[128,8,128]{2,1,0:T(8,128)(2,1)S(1)}, u32[]{:S(2)}, u32[]{:S(2)}) async-start(bf16[128,8,128]{2,1,0:T(8,128)(2,1)} %bitcast.2), calls=%async_computation | async-start | bytes 524288 | tf_op jit(solution)/shard_map/all_to_all | solution.py:265
  29.9 40.3 %copy-start.3 = (f32[1024]{0:T(1024)S(1)}, f32[1024]{0:T(1024)}, u32[]{:S(2)}) copy-start(f32[1024]{0:T(1024)} %param.18) | copy-start | bytes 12292
  29.9 40.3 %copy-start.5 = (s32[128,2]{0,1:T(2,128)S(1)}, s32[128,2]{0,1:T(2,128)}, u32[]{:S(2)}) copy-start(s32[128,2]{0,1:T(2,128)} %param.20) | copy-start | bytes 3076
  29.9 40.3 %copy-start.6 = (s32[128]{0:T(128)S(1)}, s32[128]{0:T(128)}, u32[]{:S(2)}) copy-start(s32[128]{0:T(128)} %param.21) | copy-start | bytes 1540
  35.8 34.4 %copy-start = (bf16[1536,1024]{1,0:T(8,128)(2,1)S(1)}, bf16[1536,1024]{1,0:T(8,128)(2,1)}, u32[]{:S(2)}) copy-start(bf16[1536,1024]{1,0:T(8,128)(2,1)} %pair_ref.1) | copy-start | bytes 9437188
  35.8 34.4 %copy-start.1 = (bf16[512,512]{1,0:T(8,128)(2,1)S(1)}, bf16[512,512]{1,0:T(8,128)(2,1)}, u32[]{:S(2)}) copy-start(bf16[512,512]{1,0:T(8,128)(2,1)} %self_ref.1) | copy-start | bytes 1572868
  35.8 34.4 %copy-start.2 = (bf16[512,512]{1,0:T(8,128)(2,1)S(1)}, bf16[512,512]{1,0:T(8,128)(2,1)}, u32[]{:S(2)}) copy-start(bf16[512,512]{1,0:T(8,128)(2,1)} %near_ref.1) | copy-start | bytes 1572868
  70.2 28.8 %copy-start.4 = (s32[1,128,4,2]{1,3,2,0:T(2,128)S(1)}, s32[1,128,4,2]{1,3,2,0:T(2,128)}, u32[]{:S(2)}) copy-start(s32[1,128,4,2]{1,3,2,0:T(2,128)} %param.19) | copy-start | bytes 12292

commit v9 on v8

--- a/solution.py
+++ b/solution.py
@@ -7,6 +7,8 @@
 
 BF = jnp.bfloat16
 F32 = jnp.float32
+CORES = 2
+YS = 8
 DEAD = 4095
 MIB = 1024 * 1024
 
@@ -57,15 +59,25 @@
 
 
 def count_kernel(
-    act_ref, push_ref, nbr_ref, cnt_ref, near_ref, own_ref, actp_ref, cntp_ref,
-    pick_ref, mine_ref, where_ref,
+    act_ref, push_ref, nbr_ref, cnt_ref, near_ref, own_ref, actp_ref, cntp_ref, order_ref,
+    pick_ref, mine_ref, where_ref, turn_ref,
 ):
     groups, parts = push_ref.shape
     firms = act_ref.shape[0]
     degree = nbr_ref.shape[0]
     pushed = groups * parts
     i32, i16 = jnp.int32, jnp.int16
-    for j, rows in enumerate(one_hot_rows(push_ref[...].T, firms)):
+    turn_ref[...] = push_ref[...].T
+    order = jnp.concatenate(
+        [
+            turn_ref[pl.ds(z * CORES + c, YS, stride=parts // YS), :]
+            for c in range(CORES)
+            for z in range(parts // YS // CORES)
+        ],
+        0,
+    )
+    order_ref[...] = order.T
+    for j, rows in enumerate(one_hot_rows(order, firms)):
         pick_ref[j * parts : (j + 1) * parts, :] = rows
     pick = pick_ref[...]
     count = cnt_ref[...]
@@ -135,8 +147,12 @@
     divisor = cntp_ref[...].T
     summed = own_ref[...] + jnp.dot(near_ref[...], halo_ref[...], preferred_element_type=F32)
 
+    half = parts // CORES
+
     def place(b, rows, kind):
-        tmp_ref[pl.ds((b // 2) * 4 + kind * 2 + b % 2, parts, stride=2 * groups), :] = rows
+        for c in range(CORES):
+            at = (c * groups // 2 + b // 2) * half * 4 + kind * 2 + b % 2
+            tmp_ref[pl.ds(at, half, stride=4), :] = rows[c * half : (c + 1) * half]
 
     for b in range(groups):
         rows = slice(b * parts, (b + 1) * parts)
@@ -155,25 +171,31 @@
     width = self_ref.shape[0]
     tmp_ref[...] = recv_ref[...].astype(F32)
 
+    half = parts // CORES
+
     def rows_of(kind):
-        halves = [
-            jnp.concatenate(
-                [
-                    tmp_ref[pl.ds(s * 4 + kind * 2 + c, parts, stride=16), :]
-                    for s in range(4)
-                ],
-                1,
-            )
-            for c in range(2)
-        ]
-        return jnp.concatenate(halves, 0).astype(BF)
+        return jnp.concatenate(
+            [
+                jnp.concatenate(
+                    [
+                        tmp_ref[pl.ds((c * 4 + s) * half * 4 + kind * 2 + cap, half, stride=4), :]
+                        for s in range(4)
+                    ],
+                    1,
+                )
+                for cap in range(2)
+                for c in range(CORES)
+            ],
+            0,
+        ).astype(BF)
 
     embed = (
         jnp.dot(rows_of(0), self_ref[...], preferred_element_type=F32)
         + jnp.dot(rows_of(1), near_ref[...], preferred_element_type=F32)
     ).astype(BF)
     place = lax.broadcasted_iota(jnp.int32, (2 * parts, pairs), 0)
-    slot = jnp.where(place < parts, 2 * place, 2 * (place - parts) + 1)
+    y, z, c = place % YS, place % half // YS, place % parts // half
+    slot = ((y * (half // YS) + z) * CORES + c) * 2 + place // parts
     left_pick = jnp.where(slot == slots_ref[0:1, :], 1.0, 0.0).astype(BF)
     right_pick = jnp.where(slot == slots_ref[1:2, :], 1.0, 0.0).astype(BF)
     picks = jnp.concatenate([left_pick, right_pick], 1)
@@ -208,18 +230,26 @@
         picks, jnp.concatenate([left_grad, right_grad], 0), preferred_element_type=F32
     )
     for s in range(4):
-        for c in range(2):
-            back_ref[pl.ds(s * 2 + c, parts, stride=8), :] = back[
-                c * parts : (c + 1) * parts, s * 128 : (s + 1) * 128
-            ]
+        for cap in range(2):
+            for c in range(CORES):
+                at = cap * parts + c * half
+                back_ref[pl.ds((c * 4 + s) * half * 2 + cap, half, stride=2), :] = back[
+                    at : at + half, s * 128 : (s + 1) * 128
+                ]
     out_ref[...] = back_ref[...].astype(BF)
 
 
 def owner_kernel(recv_ref, push_ref, out_ref, tmp_ref, sum_ref, sems):
     groups, parts = push_ref.shape
     tmp_ref[...] = recv_ref[...].astype(F32)
+    half = parts // CORES
     grads = jnp.concatenate(
-        [tmp_ref[pl.ds(b, parts, stride=groups), :] for b in range(groups)], 0
+        [
+            tmp_ref[pl.ds((c * groups // 2 + b // 2) * half * 2 + b % 2, half, stride=2), :]
+            for b in range(groups)
+            for c in range(CORES)
+        ],
+        0,
     ).astype(BF)
     parcels = sems.shape[0]
     step = sum_ref.shape[0] // parcels
@@ -248,7 +278,7 @@
     firms, narrow = firm_act.shape
     doms, subs, cap = push_rows.shape[1:]
     slots = halo_rows.shape[2]
-    both = ("dom", "sub")
+    dom, everyone = ("y", "z", "c"), ("c", "x", "z", "y")
     shape = jax.ShapeDtypeStruct
     vmem = pltpu.VMEM
     halo_t = jnp.transpose(halo_rows[0])
@@ -263,15 +293,18 @@
         2 * halos * firms * narrow, 600_000, firm_act, halo_t, in_specs=[fetch, fetch],
     )
     incoming = lax.all_to_all(
-        outgoing.reshape(doms, slots, narrow), "dom", 0, 0, tiled=True
+        outgoing.reshape(doms, slots, narrow), dom, 0, 0, tiled=True
     ).reshape(halos, narrow)
-    near_counts, own_sum, push_act, push_count = call(
+    near_counts, own_sum, push_act, push_count, push_order = call(
         count_kernel,
         (
             shape((pushed, halos), BF), shape((pushed, narrow), F32), shape((pushed, narrow), BF),
-            shape((subs * cap, doms), F32),
+            shape((subs * cap, doms), F32), shape((subs * cap, doms), jnp.int32),
         ),
-        [vmem((pushed, firms), BF), vmem((pushed, firms), BF), vmem((pushed // 16, 512), F32)],
+        [
+            vmem((pushed, firms), BF), vmem((pushed, firms), BF), vmem((pushed // 16, 512), F32),
+            vmem((doms, subs * cap), jnp.int32),
+        ],
         10_000_000_000, 4_000_000,
         firm_act, push_t, jnp.transpose(nbr_index), nbr_count.reshape(1, firms),
         in_specs=[fetch] * 4,
@@ -282,7 +315,7 @@
         incoming, near_counts, own_sum, push_act, push_count,
     )
     arrived = lax.all_to_all(
-        message.reshape(doms * subs, 2 * cap, narrow), both, 0, 0, tiled=True
+        message.reshape(doms * subs, 2 * cap, narrow), everyone, 0, 0, tiled=True
     ).reshape(2 * pushed, narrow)
     pairs = labels.shape[0]
     pair_loss, back = call(
@@ -294,23 +327,27 @@
         labels.reshape(1, pairs),
     )
     returned = lax.all_to_all(
-        back.reshape(doms * subs, cap, narrow), both, 0, 0, tiled=True
+        back.reshape(doms * subs, cap, narrow), everyone, 0, 0, tiled=True
     ).reshape(pushed, narrow)
     embed_grad = call(
         owner_kernel, pltpu.HBM((firms, narrow), F32),
         [vmem((pushed, narrow), F32), vmem((firms, narrow), F32), pltpu.SemaphoreType.DMA((4,))],
-        2 * pushed * firms * narrow, 1_000_000, returned, push_t,
+        2 * pushed * firms * narrow, 1_000_000, returned, push_order,
         in_specs=[("vmem",)] * 2, out_specs=["hbm"],
     )
     return (pair_loss.reshape(pairs), embed_grad)
 
 
 def solution(mesh):
+    subs = mesh.shape["sub"]
+    zs = mesh.shape["dom"] // YS // CORES
+    cut = jax.sharding.Mesh(mesh.devices.reshape(YS, zs, CORES, subs), ("y", "z", "c", "x"))
+    dom, every = ("y", "z", "c"), ("y", "z", "c", "x")
     in_specs = (
-        P("dom", "sub"), P(), P(), P("dom", None, None), P("dom", None), P("dom"), P(), P(),
-        P("dom", None, None, None), P(("dom", "sub"), None), P(("dom", "sub")),
-    )
-    out_specs = (P(("dom", "sub")), P("dom", "sub"))
+        P(dom, "x"), P(), P(), P(dom, None, None), P(dom, None), P(dom), P(), P(),
+        P(dom, None, None, None), P(every, None), P(every),
+    )
+    out_specs = (P(every), P(dom, "x"))
     return jax.shard_map(
-        per_device, mesh=mesh, in_specs=in_specs, out_specs=out_specs, check_vma=False
-    )
+        per_device, mesh=cut, in_specs=in_specs, out_specs=out_specs, check_vma=False
+    )

time: 101 us -> 102 us (level)
  blocking collectives: 59.4 us -> 61.2 us
    all_to_all x2, blocking collectives: 59.4 us -> 61.2 us  [the longest x1 34.6 us: per_device(): lax.all_to_all(message.reshape(doms * subs, 2 * cap, narrow), everyone, 0...]
where the time goes in v9:
time: 102 us
  blocking collectives  61.2 us (60%)
  starting transfers between devices  18.4 us (18%)
  Pallas kernels  15.9 us (16%)
  waiting for transfers between devices  5.8 us (6%)
    all_to_all x1, blocking collectives, per_device(): lax.all_to_all(message.reshape(doms * subs, 2 * cap, narrow), everyone, 0...  34.6 us
    all_to_all x1, blocking collectives, per_device(): lax.all_to_all(back.reshape(doms * subs, cap, narrow), everyone, 0, 0, ti...  26.7 us
    all_to_all x1, starting transfers between devices, per_device(): lax.all_to_all(outgoing.reshape(doms, slots, narrow), dom, 0, 0, tiled=True)  18.4 us
    pallas_call x5, Pallas kernels, call(): pl.pallas_call(kernel, out_shape=out_shape, scratch_shapes=scratch, **spe...  15.9 us
    all_to_all x1, waiting for transfers between devices, per_device(): lax.all_to_all(outgoing.reshape(doms, slots, narrow), dom, 0, 0, tiled=True)  5.8 us
  transfers between devices with their start and end apart: 1, of which 1 were waited for; matrix products, arithmetic and copies ran while one was open for 0% of the time, Pallas kernels for 8%

profile of v9, /device:TPU:1, one launch (start us, length us, event | category | flops | bytes accessed | tf_op | source)
XLA Modules:
  0.0 102.2 jit_solution(4822952726987067)
XLA Ops:
  0.6 2.5 %shard_map.122 = bf16[1024,128]{1,0:T(8,128)(2,1)} custom-call(bf16[1024,128]{1,0:T(8,128)(2,1)} %act_ref.3, s32[8,128]{1,0:T(8,128)} %bitcast.29), custom_call_target="tpu_custom_call" | custom-call | flops 268435456 | bytes 600000 | tf_op jit(solution)/shard_map/pallas_call | solution.py:33
  3.1 18.4 %all-to-all-start = ((bf16[128,8,128]{2,1,0:T(8,128)(2,1)}), bf16[128,8,128]{2,1,0:T(8,128)(2,1)S(1)}, u32[]{:S(2)}, u32[]{:S(2)}) async-start(bf16[128,8,128]{2,1,0:T(8,128)(2,1)} %bitcast.2), calls=%async_computation | async-start | bytes 524288 | tf_op jit(solution)/shard_map/all_to_all | solution.py:295
  21.6 8.4 %shard_map.123 = (bf16[1024,1024]{1,0:T(8,128)(2,1)S(1)}, f32[1024,128]{1,0:T(8,128)S(1)}, bf16[1024,128]{1,0:T(8,128)(2,1)S(1)}, f32[8,128]{1,0:T(8,128)S(1)}, s32[8,128]{1,0:T(8,128)S(1)}) custom-call(bf16[1024,128]{1,0:T(8,128)(2,1)} %act_ref.3, s32[8,128]{1,0:T(8,128)} %bitcast.30, s32[16,1024]{1,0:T(8,128)} %bitcast.28, s32[1,1024]{1,0:T(1,128)} %bitcast.31), custom_call_target="tpu_custom_call" | custom-call | flops 10000000000 | bytes 4000000 | tf_op jit(solution)/shard_map/pallas_call | solution.py:33
  29.9 0.0 copy-start.3
  30.0 0.0 copy-start.4
  30.0 0.0 copy-start.5
  30.0 5.8 %all-to-all-done = bf16[128,8,128]{2,1,0:T(8,128)(2,1)S(1)} async-done(((bf16[128,8,128]{2,1,0:T(8,128)(2,1)}), bf16[128,8,128]{2,1,0:T(8,128)(2,1)S(1)}, u32[]{:S(2)}, u32[]{:S(2)}) %all-to-all-start) | async-done | bytes 262176 | tf_op jit(solution)/shard_map/all_to_all | solution.py:295
  35.8 0.0 copy-start
  35.8 0.0 copy-start.1
  35.8 0.0 copy-start.2
  35.8 0.8 shard_map.124
  36.6 34.6 %all_to_all.15 = bf16[512,4,128]{2,1,0:T(4,128)(2,1)S(1)} all-to-all(bf16[512,4,128]{2,1,0:T(4,128)(2,1)S(1)} %bitcast.20), channel_id=1, replica_groups=mesh['y'=8,'z'=8,'c'=2,'x'=4] {'c','x','z','y'}, dimensions={0} | all-to-all | bytes 1048576 | tf_op jit(solution)/shard_map/all_to_all | solution.py:317
  71.2 0.0 copy-done.3
  71.2 0.0 copy-done.4
  71.2 0.0 copy-done.5
  71.2 0.0 copy-done
  71.2 0.0 copy-done.1
  71.2 0.0 copy-done.2
  71.2 2.8 %shard_map.125 = (f32[1,128]{1,0:T(1,128)}, bf16[1024,128]{1,0:T(8,128)(2,1)S(1)}) custom-call(bf16[2048,128]{1,0:T(8,128)(2,1)S(1)} %bitcast.22, bf16[512,512]{1,0:T(8,128)(2,1)S(1)} %copy-done.1, bf16[512,512]{1,0:T(8,128)(2,1)S(1)} %copy-done.2, bf16[1536,1024]{1,0:T(8,128)(2,1)S(1)} %copy-done, f32[1,1024]{1,0:T(1,128)S(1)} %bitcast.25, ...), custom_call_target="tpu_custom_call" | custom-call | flops 5000000000 | bytes 5000000 | tf_op jit(solution)/shard_map/pallas_call | solution.py:33
  74.0 26.7 %all_to_all.16 = bf16[512,2,128]{2,1,0:T(2,128)(2,1)S(1)} all-to-all(bf16[512,2,128]{2,1,0:T(2,128)(2,1)S(1)} %bitcast.23), channel_id=1, replica_groups=mesh['y'=8,'z'=8,'c'=2,'x'=4] {'c','x','z','y'}, dimensions={0} | all-to-all | bytes 524288 | tf_op jit(solution)/shard_map/all_to_all | solution.py:329
  100.6 1.4 %shard_map.126 = f32[1024,128]{1,0:T(8,128)} custom-call(bf16[1024,128]{1,0:T(8,128)(2,1)S(1)} %bitcast.24, s32[8,128]{1,0:T(8,128)S(1)} %get-tuple-element.15.push_ref), custom_call_target="tpu_custom_call" | custom-call | flops 268435456 | bytes 1000000 | tf_op jit(solution)/shard_map/pallas_call | solution.py:33
Async XLA Ops:
  3.1 32.7 %all-to-all-start = ((bf16[128,8,128]{2,1,0:T(8,128)(2,1)}), bf16[128,8,128]{2,1,0:T(8,128)(2,1)S(1)}, u32[]{:S(2)}, u32[]{:S(2)}) async-start(bf16[128,8,128]{2,1,0:T(8,128)(2,1)} %bitcast.2), calls=%async_computation | async-start | bytes 524288 | tf_op jit(solution)/shard_map/all_to_all | solution.py:295
  29.9 41.2 %copy-start.3 = (f32[1024]{0:T(1024)S(1)}, f32[1024]{0:T(1024)}, u32[]{:S(2)}) copy-start(f32[1024]{0:T(1024)} %param.18) | copy-start | bytes 12292
  30.0 41.2 %copy-start.4 = (s32[128,2]{0,1:T(2,128)S(1)}, s32[128,2]{0,1:T(2,128)}, u32[]{:S(2)}) copy-start(s32[128,2]{0,1:T(2,128)} %param.20) | copy-start | bytes 3076
  30.0 41.2 %copy-start.5 = (s32[128]{0:T(128)S(1)}, s32[128]{0:T(128)}, u32[]{:S(2)}) copy-start(s32[128]{0:T(128)} %param.21) | copy-start | bytes 1540
  35.8 35.4 %copy-start = (bf16[1536,1024]{1,0:T(8,128)(2,1)S(1)}, bf16[1536,1024]{1,0:T(8,128)(2,1)}, u32[]{:S(2)}) copy-start(bf16[1536,1024]{1,0:T(8,128)(2,1)} %pair_ref.1) | copy-start | bytes 9437188
  35.8 35.4 %copy-start.1 = (bf16[512,512]{1,0:T(8,128)(2,1)S(1)}, bf16[512,512]{1,0:T(8,128)(2,1)}, u32[]{:S(2)}) copy-start(bf16[512,512]{1,0:T(8,128)(2,1)} %self_ref.1) | copy-start | bytes 1572868
  35.8 35.4 %copy-start.2 = (bf16[512,512]{1,0:T(8,128)(2,1)S(1)}, bf16[512,512]{1,0:T(8,128)(2,1)}, u32[]{:S(2)}) copy-start(bf16[512,512]{1,0:T(8,128)(2,1)} %near_ref.1) | copy-start | bytes 1572868

commit v10 on v8

--- a/solution.py
+++ b/solution.py
@@ -136,7 +136,7 @@
     summed = own_ref[...] + jnp.dot(near_ref[...], halo_ref[...], preferred_element_type=F32)
 
     def place(b, rows, kind):
-        tmp_ref[pl.ds((b // 2) * 4 + kind * 2 + b % 2, parts, stride=2 * groups), :] = rows
+        tmp_ref[pl.ds((b // 2) * parts * 4 + kind * 2 + b % 2, parts, stride=4), :] = rows
 
     for b in range(groups):
         rows = slice(b * parts, (b + 1) * parts)
@@ -159,7 +159,7 @@
         halves = [
             jnp.concatenate(
                 [
-                    tmp_ref[pl.ds(s * 4 + kind * 2 + c, parts, stride=16), :]
+                    tmp_ref[pl.ds(s * parts * 4 + kind * 2 + c, parts, stride=4), :]
                     for s in range(4)
                 ],
                 1,
@@ -209,7 +209,7 @@
     )
     for s in range(4):
         for c in range(2):
-            back_ref[pl.ds(s * 2 + c, parts, stride=8), :] = back[
+            back_ref[pl.ds(s * parts * 2 + c, parts, stride=2), :] = back[
                 c * parts : (c + 1) * parts, s * 128 : (s + 1) * 128
             ]
     out_ref[...] = back_ref[...].astype(BF)
@@ -219,7 +219,8 @@
     groups, parts = push_ref.shape
     tmp_ref[...] = recv_ref[...].astype(F32)
     grads = jnp.concatenate(
-        [tmp_ref[pl.ds(b, parts, stride=groups), :] for b in range(groups)], 0
+        [tmp_ref[pl.ds((b // 2) * parts * 2 + b % 2, parts, stride=2), :]
+            for b in range(groups)], 0
     ).astype(BF)
     parcels = sems.shape[0]
     step = sum_ref.shape[0] // parcels
@@ -248,7 +249,7 @@
     firms, narrow = firm_act.shape
     doms, subs, cap = push_rows.shape[1:]
     slots = halo_rows.shape[2]
-    both = ("dom", "sub")
+    both = ("sub", "dom")
     shape = jax.ShapeDtypeStruct
     vmem = pltpu.VMEM
     halo_t = jnp.transpose(halo_rows[0])

time: 101 us -> 101 us (level)
  no operation moved by 1% of the time
where the time goes in v10:
time: 101 us; the launch traced here: 100 us
  blocking collectives  59.4 us (59%)
  starting transfers between devices  18.4 us (18%)
  Pallas kernels  15.8 us (16%)
  waiting for transfers between devices  5.85 us (6%)
    all_to_all x1, blocking collectives, per_device(): lax.all_to_all(message.reshape(doms * subs, 2 * cap, narrow), both, 0, 0,...  33.4 us
    all_to_all x1, blocking collectives, per_device(): lax.all_to_all(back.reshape(doms * subs, cap, narrow), both, 0, 0, tiled=...  26.1 us
    all_to_all x1, starting transfers between devices, per_device(): lax.all_to_all(outgoing.reshape(doms, slots, narrow), 'dom', 0, 0, tiled=...  18.4 us
    pallas_call x5, Pallas kernels, call(): pl.pallas_call(kernel, out_shape=out_shape, scratch_shapes=scratch, **spe...  15.8 us
    all_to_all x1, waiting for transfers between devices, per_device(): lax.all_to_all(outgoing.reshape(doms, slots, narrow), 'dom', 0, 0, tiled=...  5.85 us
  transfers between devices with their start and end apart: 1, of which 1 were waited for; matrix products, arithmetic and copies ran while one was open for 0% of the time, Pallas kernels for 8%

profile of v10, /device:TPU:1, one launch (start us, length us, event | category | flops | bytes accessed | tf_op | source)
XLA Modules:
  0.0 100.5 jit_solution(11248818297694328506)
XLA Ops:
  0.6 2.5 %shard_map.122 = bf16[1024,128]{1,0:T(8,128)(2,1)} custom-call(bf16[1024,128]{1,0:T(8,128)(2,1)} %act_ref.3, s32[8,128]{1,0:T(8,128)} %bitcast.31), custom_call_target="tpu_custom_call" | custom-call | flops 268435456 | bytes 600000 | tf_op jit(solution)/shard_map/pallas_call | solution.py:31
  3.1 18.4 %all-to-all-start = ((bf16[128,8,128]{2,1,0:T(8,128)(2,1)}), bf16[128,8,128]{2,1,0:T(8,128)(2,1)S(1)}, u32[]{:S(2)}, u32[]{:S(2)}) async-start(bf16[128,8,128]{2,1,0:T(8,128)(2,1)} %bitcast.2), calls=%async_computation | async-start | bytes 524288 | tf_op jit(solution)/shard_map/all_to_all | solution.py:266
  21.6 8.3 %shard_map.123 = (bf16[1024,1024]{1,0:T(8,128)(2,1)S(1)}, f32[1024,128]{1,0:T(8,128)S(1)}, bf16[1024,128]{1,0:T(8,128)(2,1)S(1)}, f32[8,128]{1,0:T(8,128)S(1)}) custom-call(bf16[1024,128]{1,0:T(8,128)(2,1)} %act_ref.3, s32[8,128]{1,0:T(8,128)} %bitcast.26, s32[16,1024]{1,0:T(8,128)} %bitcast.30, s32[1,1024]{1,0:T(1,128)} %bitcast.32), custom_call_target="tpu_custom_call" | custom-call | flops 10000000000 | bytes 4000000 | tf_op jit(solution)/shard_map/pallas_call | solution.py:31
  29.9 0.0 copy-start.3
  29.9 0.0 copy-start.5
  29.9 0.0 copy-start.6
  29.9 5.8 %all-to-all-done = bf16[128,8,128]{2,1,0:T(8,128)(2,1)S(1)} async-done(((bf16[128,8,128]{2,1,0:T(8,128)(2,1)}), bf16[128,8,128]{2,1,0:T(8,128)(2,1)S(1)}, u32[]{:S(2)}, u32[]{:S(2)}) %all-to-all-start) | async-done | bytes 262176 | tf_op jit(solution)/shard_map/all_to_all | solution.py:266
  35.8 0.0 copy-start
  35.8 0.0 copy-start.1
  35.8 0.0 copy-start.2
  35.8 0.8 shard_map.124
  36.6 33.4 %all_to_all.15 = bf16[512,4,128]{2,1,0:T(4,128)(2,1)S(1)} all-to-all(bf16[512,4,128]{2,1,0:T(4,128)(2,1)S(1)} %bitcast.20), channel_id=1, replica_groups=mesh['dom'=128,'sub'=4] {'sub','dom'}, dimensions={0} | all-to-all | bytes 1048576 | tf_op jit(solution)/shard_map/all_to_all | solution.py:285
  70.0 0.0 copy-done.3
  70.0 0.0 copy-done.5
  70.0 0.0 copy-done.6
  70.0 0.0 copy-done
  70.0 0.0 copy-done.1
  70.0 0.0 copy-done.2
  70.0 0.0 copy-start.4
  70.0 2.8 %shard_map.125 = (f32[1,128]{1,0:T(1,128)}, bf16[1024,128]{1,0:T(8,128)(2,1)S(1)}) custom-call(bf16[2048,128]{1,0:T(8,128)(2,1)S(1)} %bitcast.22, bf16[512,512]{1,0:T(8,128)(2,1)S(1)} %copy-done.1, bf16[512,512]{1,0:T(8,128)(2,1)S(1)} %copy-done.2, bf16[1536,1024]{1,0:T(8,128)(2,1)S(1)} %copy-done, f32[1,1024]{1,0:T(1,128)S(1)} %bitcast.25, ...), custom_call_target="tpu_custom_call" | custom-call | flops 5000000000 | bytes 5000000 | tf_op jit(solution)/shard_map/pallas_call | solution.py:31
  72.8 26.1 %all_to_all.16 = bf16[512,2,128]{2,1,0:T(2,128)(2,1)S(1)} all-to-all(bf16[512,2,128]{2,1,0:T(2,128)(2,1)S(1)} %bitcast.23), channel_id=1, replica_groups=mesh['dom'=128,'sub'=4] {'sub','dom'}, dimensions={0} | all-to-all | bytes 524288 | tf_op jit(solution)/shard_map/all_to_all | solution.py:297
  98.9 0.0 copy-done.4
  98.9 1.4 %shard_map.126 = f32[1024,128]{1,0:T(8,128)} custom-call(bf16[1024,128]{1,0:T(8,128)(2,1)S(1)} %bitcast.24, s32[8,128]{1,0:T(8,128)S(1)} %bitcast.27), custom_call_target="tpu_custom_call" | custom-call | flops 268435456 | bytes 1000000 | tf_op jit(solution)/shard_map/pallas_call | solution.py:31
Async XLA Ops:
  3.1 32.7 %all-to-all-start = ((bf16[128,8,128]{2,1,0:T(8,128)(2,1)}), bf16[128,8,128]{2,1,0:T(8,128)(2,1)S(1)}, u32[]{:S(2)}, u32[]{:S(2)}) async-start(bf16[128,8,128]{2,1,0:T(8,128)(2,1)} %bitcast.2), calls=%async_computation | async-start | bytes 524288 | tf_op jit(solution)/shard_map/all_to_all | solution.py:266
  29.9 40.1 %copy-start.3 = (f32[1024]{0:T(1024)S(1)}, f32[1024]{0:T(1024)}, u32[]{:S(2)}) copy-start(f32[1024]{0:T(1024)} %param.18) | copy-start | bytes 12292
  29.9 40.0 %copy-start.5 = (s32[128,2]{0,1:T(2,128)S(1)}, s32[128,2]{0,1:T(2,128)}, u32[]{:S(2)}) copy-start(s32[128,2]{0,1:T(2,128)} %param.20) | copy-start | bytes 3076
  29.9 40.0 %copy-start.6 = (s32[128]{0:T(128)S(1)}, s32[128]{0:T(128)}, u32[]{:S(2)}) copy-start(s32[128]{0:T(128)} %param.21) | copy-start | bytes 1540
  35.8 34.2 %copy-start = (bf16[1536,1024]{1,0:T(8,128)(2,1)S(1)}, bf16[1536,1024]{1,0:T(8,128)(2,1)}, u32[]{:S(2)}) copy-start(bf16[1536,1024]{1,0:T(8,128)(2,1)} %pair_ref.1) | copy-start | bytes 9437188
  35.8 34.2 %copy-start.1 = (bf16[512,512]{1,0:T(8,128)(2,1)S(1)}, bf16[512,512]{1,0:T(8,128)(2,1)}, u32[]{:S(2)}) copy-start(bf16[512,512]{1,0:T(8,128)(2,1)} %self_ref.1) | copy-start | bytes 1572868
  35.8 34.2 %copy-start.2 = (bf16[512,512]{1,0:T(8,128)(2,1)S(1)}, bf16[512,512]{1,0:T(8,128)(2,1)}, u32[]{:S(2)}) copy-start(bf16[512,512]{1,0:T(8,128)(2,1)} %near_ref.1) | copy-start | bytes 1572868
  70.0 28.9 %copy-start.4 = (s32[1,128,4,2]{1,3,2,0:T(2,128)S(1)}, s32[1,128,4,2]{1,3,2,0:T(2,128)}, u32[]{:S(2)}) copy-start(s32[1,128,4,2]{1,3,2,0:T(2,128)} %param.19) | copy-start | bytes 12292

commit v11 on v10

--- a/solution.py
+++ b/solution.py
@@ -7,6 +7,8 @@
 
 BF = jnp.bfloat16
 F32 = jnp.float32
+CORES = 2
+YS = 8
 DEAD = 4095
 MIB = 1024 * 1024
 
@@ -46,14 +48,18 @@
     ]
 
 
-def halo_kernel(act_ref, rows_ref, out_ref, tmp_ref, pick_ref):
+def halo_kernel(act_ref, rows_ref, out_ref, pick_ref):
     slots, parts = rows_ref.shape
-    for j, rows in enumerate(one_hot_rows(rows_ref[...].T, act_ref.shape[0])):
-        pick_ref[j * parts : (j + 1) * parts, :] = rows
-    picked = jnp.dot(pick_ref[...], act_ref[...], preferred_element_type=F32)
-    for j in range(slots):
-        tmp_ref[pl.ds(j, parts, stride=slots), :] = picked[j * parts : (j + 1) * parts]
-    out_ref[...] = tmp_ref[...].astype(BF)
+    rows = rows_ref[...]
+    number = lax.broadcasted_iota(jnp.int32, (slots, act_ref.shape[0]), 1)
+    zs = parts // YS // CORES
+    order = [(y * zs + z) * CORES + c for z in range(zs) for y in range(YS) for c in range(CORES)]
+    for at in range(0, parts, 2):
+        pair = [
+            jnp.where(rows[:, p : p + 1] == number, 1.0, 0.0) for p in order[at : at + 2]
+        ]
+        pick_ref[at * slots : (at + 2) * slots, :] = jnp.concatenate(pair, 0).astype(BF)
+    out_ref[...] = jnp.dot(pick_ref[...], act_ref[...], preferred_element_type=F32).astype(BF)
 
 
 def count_kernel(
@@ -70,7 +76,13 @@
     pick = pick_ref[...]
     count = cnt_ref[...]
     live = lax.broadcasted_iota(i32, (degree, firms), 0) < count
-    slot = jnp.where(live, nbr_ref[...], DEAD)
+    slot = nbr_ref[...]
+    cell = (near_ref.shape[1] // parts) * CORES
+    zs = parts // YS // CORES
+    past = slot - firms
+    y, z = past // (cell * zs), past // cell % zs
+    moved = firms + (z * YS + y) * cell + past % cell
+    slot = jnp.where(live, jnp.where(past >= 0, moved, slot), DEAD)
     counts = jnp.broadcast_to(count, (degree, firms))
     stack = jnp.concatenate([slot >> 7, slot & 127, counts], 0).astype(F32).astype(BF)
     chosen = lax.dot_general(
@@ -249,7 +261,7 @@
     firms, narrow = firm_act.shape
     doms, subs, cap = push_rows.shape[1:]
     slots = halo_rows.shape[2]
-    both = ("sub", "dom")
+    both = ("x", "y", "z", "c")
     shape = jax.ShapeDtypeStruct
     vmem = pltpu.VMEM
     halo_t = jnp.transpose(halo_rows[0])
@@ -259,12 +271,11 @@
 
     fetch = ("hbm", "vmem")
     outgoing = call(
-        halo_kernel, shape((halos, narrow), BF),
-        [vmem((halos, narrow), F32), vmem((halos, firms), BF)],
+        halo_kernel, shape((halos, narrow), BF), [vmem((halos, firms), BF)],
         2 * halos * firms * narrow, 600_000, firm_act, halo_t, in_specs=[fetch, fetch],
     )
     incoming = lax.all_to_all(
-        outgoing.reshape(doms, slots, narrow), "dom", 0, 0, tiled=True
+        outgoing.reshape(doms, slots, narrow), ("z", "y", "c"), 0, 0, tiled=True
     ).reshape(halos, narrow)
     near_counts, own_sum, push_act, push_count = call(
         count_kernel,
@@ -307,11 +318,15 @@
 
 
 def solution(mesh):
+    subs = mesh.shape["sub"]
+    zs = mesh.shape["dom"] // YS // CORES
+    cut = jax.sharding.Mesh(mesh.devices.reshape(YS, zs, CORES, subs), ("y", "z", "c", "x"))
+    dom, every = ("y", "z", "c"), ("y", "z", "c", "x")
     in_specs = (
-        P("dom", "sub"), P(), P(), P("dom", None, None), P("dom", None), P("dom"), P(), P(),
-        P("dom", None, None, None), P(("dom", "sub"), None), P(("dom", "sub")),
-    )
-    out_specs = (P(("dom", "sub")), P("dom", "sub"))
+        P(dom, "x"), P(), P(), P(dom, None, None), P(dom, None), P(dom), P(), P(),
+        P(dom, None, None, None), P(every, None), P(every),
+    )
+    out_specs = (P(every), P(dom, "x"))
     return jax.shard_map(
-        per_device, mesh=mesh, in_specs=in_specs, out_specs=out_specs, check_vma=False
-    )
+        per_device, mesh=cut, in_specs=in_specs, out_specs=out_specs, check_vma=False
+    )

time: 101 us -> 101 us (level)
  waiting for transfers between devices: 5.85 us -> 6.86 us
    all_to_all x1, blocking collectives: 33.4 us -> 32.3 us  [per_device(): lax.all_to_all(message.reshape(doms * subs, 2 * cap, narrow), both, 0, 0,...]
where the time goes in v11:
time: 101 us; the launch traced here: 100 us
  blocking collectives  58.4 us (58%)
  starting transfers between devices  18.4 us (18%)
  Pallas kernels  15.8 us (16%)
  waiting for transfers between devices  6.86 us (7%)
    all_to_all x1, blocking collectives, per_device(): lax.all_to_all(message.reshape(doms * subs, 2 * cap, narrow), both, 0, 0,...  32.3 us
    all_to_all x1, blocking collectives, per_device(): lax.all_to_all(back.reshape(doms * subs, cap, narrow), both, 0, 0, tiled=...  26.1 us
    all_to_all x1, starting transfers between devices, per_device(): lax.all_to_all(outgoing.reshape(doms, slots, narrow), ('z', 'y', 'c'), 0,...  18.4 us
    pallas_call x5, Pallas kernels, call(): pl.pallas_call(kernel, out_shape=out_shape, scratch_shapes=scratch, **spe...  15.8 us
    all_to_all x1, waiting for transfers between devices, per_device(): lax.all_to_all(outgoing.reshape(doms, slots, narrow), ('z', 'y', 'c'), 0,...  6.86 us
  transfers between devices with their start and end apart: 1, of which 1 were waited for; matrix products, arithmetic and copies ran while one was open for 0% of the time, Pallas kernels for 8%

profile of v11, /device:TPU:1, one launch (start us, length us, event | category | flops | bytes accessed | tf_op | source)
XLA Modules:
  0.0 100.4 jit_solution(17349788763497045650)
XLA Ops:
  0.6 2.4 %shard_map.122 = bf16[1024,128]{1,0:T(8,128)(2,1)} custom-call(bf16[1024,128]{1,0:T(8,128)(2,1)} %act_ref.3, s32[8,128]{1,0:T(8,128)} %bitcast.31), custom_call_target="tpu_custom_call" | custom-call | flops 268435456 | bytes 600000 | tf_op jit(solution)/shard_map/pallas_call | solution.py:33
  3.0 18.4 %all-to-all-start = ((bf16[128,8,128]{2,1,0:T(8,128)(2,1)}), bf16[128,8,128]{2,1,0:T(8,128)(2,1)S(1)}, u32[]{:S(2)}, u32[]{:S(2)}) async-start(bf16[128,8,128]{2,1,0:T(8,128)(2,1)} %bitcast.2), calls=%async_computation | async-start | bytes 524288 | tf_op jit(solution)/shard_map/all_to_all | solution.py:277
  21.5 8.4 %shard_map.123 = (bf16[1024,1024]{1,0:T(8,128)(2,1)S(1)}, f32[1024,128]{1,0:T(8,128)S(1)}, bf16[1024,128]{1,0:T(8,128)(2,1)S(1)}, f32[8,128]{1,0:T(8,128)S(1)}) custom-call(bf16[1024,128]{1,0:T(8,128)(2,1)} %act_ref.3, s32[8,128]{1,0:T(8,128)} %bitcast.26, s32[16,1024]{1,0:T(8,128)} %bitcast.30, s32[1,1024]{1,0:T(1,128)} %bitcast.32), custom_call_target="tpu_custom_call" | custom-call | flops 10000000000 | bytes 4000000 | tf_op jit(solution)/shard_map/pallas_call | solution.py:33
  29.8 0.0 copy-start.3
  29.9 0.0 copy-start.5
  29.9 0.0 copy-start.6
  29.9 6.9 %all-to-all-done = bf16[128,8,128]{2,1,0:T(8,128)(2,1)S(1)} async-done(((bf16[128,8,128]{2,1,0:T(8,128)(2,1)}), bf16[128,8,128]{2,1,0:T(8,128)(2,1)S(1)}, u32[]{:S(2)}, u32[]{:S(2)}) %all-to-all-start) | async-done | bytes 262176 | tf_op jit(solution)/shard_map/all_to_all | solution.py:277
  36.7 0.0 copy-start
  36.7 0.0 copy-start.1
  36.7 0.0 copy-start.2
  36.7 0.8 shard_map.124
  37.6 32.3 %all_to_all.15 = bf16[512,4,128]{2,1,0:T(4,128)(2,1)S(1)} all-to-all(bf16[512,4,128]{2,1,0:T(4,128)(2,1)S(1)} %bitcast.20), channel_id=1, replica_groups=mesh['y'=8,'z'=8,'c'=2,'x'=4] {'x','y','z','c'}, dimensions={0} | all-to-all | bytes 1048576 | tf_op jit(solution)/shard_map/all_to_all | solution.py:296
  69.9 0.0 copy-done.3
  69.9 0.0 copy-done.5
  69.9 0.0 copy-done.6
  69.9 0.0 copy-done
  69.9 0.0 copy-done.1
  69.9 0.0 copy-done.2
  69.9 0.0 copy-start.4
  69.9 2.8 %shard_map.125 = (f32[1,128]{1,0:T(1,128)}, bf16[1024,128]{1,0:T(8,128)(2,1)S(1)}) custom-call(bf16[2048,128]{1,0:T(8,128)(2,1)S(1)} %bitcast.22, bf16[512,512]{1,0:T(8,128)(2,1)S(1)} %copy-done.1, bf16[512,512]{1,0:T(8,128)(2,1)S(1)} %copy-done.2, bf16[1536,1024]{1,0:T(8,128)(2,1)S(1)} %copy-done, f32[1,1024]{1,0:T(1,128)S(1)} %bitcast.25, ...), custom_call_target="tpu_custom_call" | custom-call | flops 5000000000 | bytes 5000000 | tf_op jit(solution)/shard_map/pallas_call | solution.py:33
  72.7 26.1 %all_to_all.16 = bf16[512,2,128]{2,1,0:T(2,128)(2,1)S(1)} all-to-all(bf16[512,2,128]{2,1,0:T(2,128)(2,1)S(1)} %bitcast.23), channel_id=1, replica_groups=mesh['y'=8,'z'=8,'c'=2,'x'=4] {'x','y','z','c'}, dimensions={0} | all-to-all | bytes 524288 | tf_op jit(solution)/shard_map/all_to_all | solution.py:308
  98.8 0.0 copy-done.4
  98.8 1.4 %shard_map.126 = f32[1024,128]{1,0:T(8,128)} custom-call(bf16[1024,128]{1,0:T(8,128)(2,1)S(1)} %bitcast.24, s32[8,128]{1,0:T(8,128)S(1)} %bitcast.27), custom_call_target="tpu_custom_call" | custom-call | flops 268435456 | bytes 1000000 | tf_op jit(solution)/shard_map/pallas_call | solution.py:33
Async XLA Ops:
  3.0 33.7 %all-to-all-start = ((bf16[128,8,128]{2,1,0:T(8,128)(2,1)}), bf16[128,8,128]{2,1,0:T(8,128)(2,1)S(1)}, u32[]{:S(2)}, u32[]{:S(2)}) async-start(bf16[128,8,128]{2,1,0:T(8,128)(2,1)} %bitcast.2), calls=%async_computation | async-start | bytes 524288 | tf_op jit(solution)/shard_map/all_to_all | solution.py:277
  29.8 40.1 %copy-start.3 = (f32[1024]{0:T(1024)S(1)}, f32[1024]{0:T(1024)}, u32[]{:S(2)}) copy-start(f32[1024]{0:T(1024)} %param.18) | copy-start | bytes 12292
  29.9 40.0 %copy-start.5 = (s32[128,2]{0,1:T(2,128)S(1)}, s32[128,2]{0,1:T(2,128)}, u32[]{:S(2)}) copy-start(s32[128,2]{0,1:T(2,128)} %param.20) | copy-start | bytes 3076
  29.9 40.0 %copy-start.6 = (s32[128]{0:T(128)S(1)}, s32[128]{0:T(128)}, u32[]{:S(2)}) copy-start(s32[128]{0:T(128)} %param.21) | copy-start | bytes 1540
  36.7 33.2 %copy-start = (bf16[1536,1024]{1,0:T(8,128)(2,1)S(1)}, bf16[1536,1024]{1,0:T(8,128)(2,1)}, u32[]{:S(2)}) copy-start(bf16[1536,1024]{1,0:T(8,128)(2,1)} %pair_ref.1) | copy-start | bytes 9437188
  36.7 33.2 %copy-start.1 = (bf16[512,512]{1,0:T(8,128)(2,1)S(1)}, bf16[512,512]{1,0:T(8,128)(2,1)}, u32[]{:S(2)}) copy-start(bf16[512,512]{1,0:T(8,128)(2,1)} %self_ref.1) | copy-start | bytes 1572868
  36.7 33.2 %copy-start.2 = (bf16[512,512]{1,0:T(8,128)(2,1)S(1)}, bf16[512,512]{1,0:T(8,128)(2,1)}, u32[]{:S(2)}) copy-start(bf16[512,512]{1,0:T(8,128)(2,1)} %near_ref.1) | copy-start | bytes 1572868
  69.9 28.9 %copy-start.4 = (s32[1,128,4,2]{1,3,2,0:T(2,128)S(1)}, s32[1,128,4,2]{1,3,2,0:T(2,128)}, u32[]{:S(2)}) copy-start(s32[1,128,4,2]{1,3,2,0:T(2,128)} %param.19) | copy-start | bytes 12292

commit v12 on v10

--- a/solution.py
+++ b/solution.py
@@ -46,14 +46,14 @@
     ]
 
 
-def halo_kernel(act_ref, rows_ref, out_ref, tmp_ref, pick_ref):
+def halo_kernel(act_ref, rows_ref, out_ref, pick_ref):
     slots, parts = rows_ref.shape
-    for j, rows in enumerate(one_hot_rows(rows_ref[...].T, act_ref.shape[0])):
-        pick_ref[j * parts : (j + 1) * parts, :] = rows
-    picked = jnp.dot(pick_ref[...], act_ref[...], preferred_element_type=F32)
-    for j in range(slots):
-        tmp_ref[pl.ds(j, parts, stride=slots), :] = picked[j * parts : (j + 1) * parts]
-    out_ref[...] = tmp_ref[...].astype(BF)
+    rows = rows_ref[...]
+    number = lax.broadcasted_iota(jnp.int32, (slots, act_ref.shape[0]), 1)
+    for at in range(0, parts, 2):
+        pair = [jnp.where(rows[:, p : p + 1] == number, 1.0, 0.0) for p in (at, at + 1)]
+        pick_ref[at * slots : (at + 2) * slots, :] = jnp.concatenate(pair, 0).astype(BF)
+    out_ref[...] = jnp.dot(pick_ref[...], act_ref[...], preferred_element_type=F32).astype(BF)
 
 
 def count_kernel(
@@ -259,8 +259,7 @@
 
     fetch = ("hbm", "vmem")
     outgoing = call(
-        halo_kernel, shape((halos, narrow), BF),
-        [vmem((halos, narrow), F32), vmem((halos, firms), BF)],
+        halo_kernel, shape((halos, narrow), BF), [vmem((halos, firms), BF)],
         2 * halos * firms * narrow, 600_000, firm_act, halo_t, in_specs=[fetch, fetch],
     )
     incoming = lax.all_to_all(

time: 101 us -> 101 us (level)
  no operation moved by 1% of the time
where the time goes in v12:
time: 101 us; the launch traced here: 100 us
  blocking collectives  59.4 us (59%)
  starting transfers between devices  18.4 us (18%)
  Pallas kernels  15.8 us (16%)
  waiting for transfers between devices  5.84 us (6%)
    all_to_all x1, blocking collectives, per_device(): lax.all_to_all(message.reshape(doms * subs, 2 * cap, narrow), both, 0, 0,...  33.3 us
    all_to_all x1, blocking collectives, per_device(): lax.all_to_all(back.reshape(doms * subs, cap, narrow), both, 0, 0, tiled=...  26.1 us
    all_to_all x1, starting transfers between devices, per_device(): lax.all_to_all(outgoing.reshape(doms, slots, narrow), 'dom', 0, 0, tiled=...  18.4 us
    pallas_call x5, Pallas kernels, call(): pl.pallas_call(kernel, out_shape=out_shape, scratch_shapes=scratch, **spe...  15.8 us
    all_to_all x1, waiting for transfers between devices, per_device(): lax.all_to_all(outgoing.reshape(doms, slots, narrow), 'dom', 0, 0, tiled=...  5.84 us
  transfers between devices with their start and end apart: 1, of which 1 were waited for; matrix products, arithmetic and copies ran while one was open for 0% of the time, Pallas kernels for 8%

profile of v12, /device:TPU:1, one launch (start us, length us, event | category | flops | bytes accessed | tf_op | source)
XLA Modules:
  0.0 100.4 jit_solution(5022927734908267969)
XLA Ops:
  0.6 2.4 %shard_map.122 = bf16[1024,128]{1,0:T(8,128)(2,1)} custom-call(bf16[1024,128]{1,0:T(8,128)(2,1)} %act_ref.3, s32[8,128]{1,0:T(8,128)} %bitcast.31), custom_call_target="tpu_custom_call" | custom-call | flops 268435456 | bytes 600000 | tf_op jit(solution)/shard_map/pallas_call | solution.py:31
  3.0 18.4 %all-to-all-start = ((bf16[128,8,128]{2,1,0:T(8,128)(2,1)}), bf16[128,8,128]{2,1,0:T(8,128)(2,1)S(1)}, u32[]{:S(2)}, u32[]{:S(2)}) async-start(bf16[128,8,128]{2,1,0:T(8,128)(2,1)} %bitcast.2), calls=%async_computation | async-start | bytes 524288 | tf_op jit(solution)/shard_map/all_to_all | solution.py:265
  21.5 8.3 %shard_map.123 = (bf16[1024,1024]{1,0:T(8,128)(2,1)S(1)}, f32[1024,128]{1,0:T(8,128)S(1)}, bf16[1024,128]{1,0:T(8,128)(2,1)S(1)}, f32[8,128]{1,0:T(8,128)S(1)}) custom-call(bf16[1024,128]{1,0:T(8,128)(2,1)} %act_ref.3, s32[8,128]{1,0:T(8,128)} %bitcast.26, s32[16,1024]{1,0:T(8,128)} %bitcast.30, s32[1,1024]{1,0:T(1,128)} %bitcast.32), custom_call_target="tpu_custom_call" | custom-call | flops 10000000000 | bytes 4000000 | tf_op jit(solution)/shard_map/pallas_call | solution.py:31
  29.8 0.0 copy-start.3
  29.8 0.0 copy-start.5
  29.8 0.0 copy-start.6
  29.9 5.8 %all-to-all-done = bf16[128,8,128]{2,1,0:T(8,128)(2,1)S(1)} async-done(((bf16[128,8,128]{2,1,0:T(8,128)(2,1)}), bf16[128,8,128]{2,1,0:T(8,128)(2,1)S(1)}, u32[]{:S(2)}, u32[]{:S(2)}) %all-to-all-start) | async-done | bytes 262176 | tf_op jit(solution)/shard_map/all_to_all | solution.py:265
  35.7 0.0 copy-start
  35.7 0.0 copy-start.1
  35.7 0.0 copy-start.2
  35.7 0.8 shard_map.124
  36.5 33.3 %all_to_all.15 = bf16[512,4,128]{2,1,0:T(4,128)(2,1)S(1)} all-to-all(bf16[512,4,128]{2,1,0:T(4,128)(2,1)S(1)} %bitcast.20), channel_id=1, replica_groups=mesh['dom'=128,'sub'=4] {'sub','dom'}, dimensions={0} | all-to-all | bytes 1048576 | tf_op jit(solution)/shard_map/all_to_all | solution.py:284
  69.9 0.0 copy-done.3
  69.9 0.0 copy-done.5
  69.9 0.0 copy-done.6
  69.9 0.0 copy-done
  69.9 0.0 copy-done.1
  69.9 0.0 copy-done.2
  69.9 0.0 copy-start.4
  69.9 2.8 %shard_map.125 = (f32[1,128]{1,0:T(1,128)}, bf16[1024,128]{1,0:T(8,128)(2,1)S(1)}) custom-call(bf16[2048,128]{1,0:T(8,128)(2,1)S(1)} %bitcast.22, bf16[512,512]{1,0:T(8,128)(2,1)S(1)} %copy-done.1, bf16[512,512]{1,0:T(8,128)(2,1)S(1)} %copy-done.2, bf16[1536,1024]{1,0:T(8,128)(2,1)S(1)} %copy-done, f32[1,1024]{1,0:T(1,128)S(1)} %bitcast.25, ...), custom_call_target="tpu_custom_call" | custom-call | flops 5000000000 | bytes 5000000 | tf_op jit(solution)/shard_map/pallas_call | solution.py:31
  72.7 26.1 %all_to_all.16 = bf16[512,2,128]{2,1,0:T(2,128)(2,1)S(1)} all-to-all(bf16[512,2,128]{2,1,0:T(2,128)(2,1)S(1)} %bitcast.23), channel_id=1, replica_groups=mesh['dom'=128,'sub'=4] {'sub','dom'}, dimensions={0} | all-to-all | bytes 524288 | tf_op jit(solution)/shard_map/all_to_all | solution.py:296
  98.8 0.0 copy-done.4
  98.8 1.4 %shard_map.126 = f32[1024,128]{1,0:T(8,128)} custom-call(bf16[1024,128]{1,0:T(8,128)(2,1)S(1)} %bitcast.24, s32[8,128]{1,0:T(8,128)S(1)} %bitcast.27), custom_call_target="tpu_custom_call" | custom-call | flops 268435456 | bytes 1000000 | tf_op jit(solution)/shard_map/pallas_call | solution.py:31
Async XLA Ops:
  3.0 32.7 %all-to-all-start = ((bf16[128,8,128]{2,1,0:T(8,128)(2,1)}), bf16[128,8,128]{2,1,0:T(8,128)(2,1)S(1)}, u32[]{:S(2)}, u32[]{:S(2)}) async-start(bf16[128,8,128]{2,1,0:T(8,128)(2,1)} %bitcast.2), calls=%async_computation | async-start | bytes 524288 | tf_op jit(solution)/shard_map/all_to_all | solution.py:265
  29.8 40.1 %copy-start.3 = (f32[1024]{0:T(1024)S(1)}, f32[1024]{0:T(1024)}, u32[]{:S(2)}) copy-start(f32[1024]{0:T(1024)} %param.18) | copy-start | bytes 12292
  29.8 40.0 %copy-start.5 = (s32[128,2]{0,1:T(2,128)S(1)}, s32[128,2]{0,1:T(2,128)}, u32[]{:S(2)}) copy-start(s32[128,2]{0,1:T(2,128)} %param.20) | copy-start | bytes 3076
  29.8 40.0 %copy-start.6 = (s32[128]{0:T(128)S(1)}, s32[128]{0:T(128)}, u32[]{:S(2)}) copy-start(s32[128]{0:T(128)} %param.21) | copy-start | bytes 1540
  35.7 34.2 %copy-start = (bf16[1536,1024]{1,0:T(8,128)(2,1)S(1)}, bf16[1536,1024]{1,0:T(8,128)(2,1)}, u32[]{:S(2)}) copy-start(bf16[1536,1024]{1,0:T(8,128)(2,1)} %pair_ref.1) | copy-start | bytes 9437188
  35.7 34.2 %copy-start.1 = (bf16[512,512]{1,0:T(8,128)(2,1)S(1)}, bf16[512,512]{1,0:T(8,128)(2,1)}, u32[]{:S(2)}) copy-start(bf16[512,512]{1,0:T(8,128)(2,1)} %self_ref.1) | copy-start | bytes 1572868
  35.7 34.2 %copy-start.2 = (bf16[512,512]{1,0:T(8,128)(2,1)S(1)}, bf16[512,512]{1,0:T(8,128)(2,1)}, u32[]{:S(2)}) copy-start(bf16[512,512]{1,0:T(8,128)(2,1)} %near_ref.1) | copy-start | bytes 1572868
  69.9 28.9 %copy-start.4 = (s32[1,128,4,2]{1,3,2,0:T(2,128)S(1)}, s32[1,128,4,2]{1,3,2,0:T(2,128)}, u32[]{:S(2)}) copy-start(s32[1,128,4,2]{1,3,2,0:T(2,128)} %param.19) | copy-start | bytes 12292
